TPU v7x, 32 devices: a whole 2x2x4 slice. The times are simulated.
32 devices in a mesh: dp: 8 (over z, y), mp: 4 (over x, core).
Axes of the slice: x: 2, y: 2, z: 4, core: 2. Of those that a mesh axis runs over, the one named last changes fastest.
Arguments:
- passages_in: bfloat16 [18432, 768], P(('dp', 'mp')), may hold values from -6 to 6
- queries: bfloat16 [16, 32, 128], P('dp', 'mp'), may hold values from -0.5390625 to 0.5390625
- w_qkv: bfloat16 [2, 768, 3, 768], P(None, None, None, 'mp'), may hold values from -0.21875 to 0.21875
- b_qv: float32 [2, 2, 768], P(None, None, 'mp'), may hold values from -3 to 3
- w_out: bfloat16 [2, 768, 768], P(None, 'mp'), may hold values from -2.5 to 2.5
- b_out: float32 [2, 768], replicated, may hold values from -3 to 3
- ln_gain: float32 [2, 2, 768], replicated, may hold values from 0.5 to 1.5
- ln_shift: float32 [2, 2, 768], replicated, may hold values from -2 to 2
- w_up: bfloat16 [2, 768, 3072], P(None, None, 'mp'), may hold values from -0.21875 to 0.21875
- b_up: bfloat16 [2, 3072], P(None, 'mp'), may hold values from -3 to 3
- w_down: bfloat16 [2, 3072, 768], P(None, 'mp'), may hold values from -0.15625 to 0.15625
- b_down: float32 [2, 768], replicated, may hold values from -3 to 3
- w_proj: bfloat16 [768, 128], replicated, may hold values from -0.21875 to 0.21875
- lengths: int32 [16, 8], P('dp'), may hold values from 1 to 1024, 1152 in all within a row
- passage_group: int32 [16, 8], P('dp'), may hold values from 0 to 7, as said below
- positive: int32 [16], replicated, may hold values from 0 to 127, as said below
Outputs:
- query_loss: float32 [16], P('dp')
- input_grad: float32 [18432, 768], P(('dp', 'mp'))
- query_grad: float32 [16, 32, 128], P('dp', 'mp')
- g_wqkv: float32 [2, 768, 3, 768], P(None, None, None, 'mp')
- g_bqv: float32 [2, 2, 768], P(None, None, 'mp')
- g_wout: float32 [2, 768, 768], P(None, 'mp')
- g_bout: float32 [2, 768], replicated
- g_lngain: float32 [2, 2, 768], replicated
- g_lnshift: float32 [2, 2, 768], replicated
- g_wup: float32 [2, 768, 3072], P(None, None, 'mp')
- g_bup: float32 [2, 3072], P(None, 'mp')
- g_wdown: float32 [2, 3072, 768], P(None, 'mp')
- g_bdown: float32 [2, 768], replicated
- g_wproj: float32 [768, 128], replicated
Inputs may be any that keep to these rules, and one draw needn't show every extreme that they name: `lengths`: each row sums to 1152; every row has one passage of exactly 1024 tokens. `passage_group`: every group is named by exactly 16 passages. positive[q] is the global passage index (row-major over passage_group) of a passage of group q // 2.
All inputs are finite; a program needn't handle non-finite values.
Results may differ from a plain program's by a relative error of at most 0.025.
Values may be sent and summed in bfloat16 or wider, within the bound.
No kernel may reach another device: no remote copies, remote signals or barrier semaphores. Data moves between devices by JAX's collectives and lax.ppermute only.
A program may use at most 320 MiB of HBM per device.

v0:
```python
import jax
import jax.numpy as jnp
from jax import lax
from jax.sharding import PartitionSpec as P

HEAD = 64


SHARP = 4.0
TEMPER = 0.2
LN_EPS = 1e-12
UNIT_EPS = 1e-06
MASKED = -1000000000.0
FLOOR = -1e30


def joined(value, axis, join):
    pieces = jax.tree.map(lambda part: lax.all_gather(part, axis), value)
    head = jax.tree.map(lambda part: part[0], pieces)
    tail = jax.tree.map(lambda part: part[1:], pieces)
    subtotal, _ = lax.scan(lambda subtotal, share: (join(subtotal, share), None), head, tail)
    return subtotal


def rows_dot(left_side, right_side):
    return lax.dot_general(
        left_side, right_side, (((0,), (0,)), ((), ())), preferred_element_type=jnp.float32
    )


def right_t(left_side, right_side):
    return lax.dot_general(
        left_side, right_side, (((1,), (1,)), ((), ())), preferred_element_type=jnp.float32
    )


def gelu_exact(values):
    return jax.nn.gelu(values, approximate=False)


def layer_norm(norm_in, gain_vec, shift_vec):
    mean_val = jnp.mean(norm_in, -1, keepdims=True)
    centered = norm_in - mean_val
    inv_std = lax.rsqrt(jnp.mean(centered * centered, -1, keepdims=True) + LN_EPS)
    normed = centered * inv_std
    return (normed * gain_vec + shift_vec, normed, inv_std)


def norm_back(grad_in, normed, inv_std, gain_vec):
    g_gain = jnp.sum(grad_in * normed, 0)
    g_shift = jnp.sum(grad_in, 0)
    inner_val = grad_in * gain_vec
    g_norm_in = inv_std * (
        inner_val
        - jnp.mean(inner_val, -1, keepdims=True)
        - normed * jnp.mean(inner_val * normed, -1, keepdims=True)
    )
    return (g_norm_in, g_gain, g_shift)


def split_heads(values, head_size):
    return values.reshape(values.shape[0], values.shape[1] // head_size, head_size)


def block_scores(q_heads, k_heads, same_seg, score_scale):
    raw_scores = (
        jnp.einsum("qhe,khe->hqk", q_heads, k_heads, preferred_element_type=jnp.float32)
        * score_scale
    )
    return jnp.where(same_seg[None], raw_scores, MASKED)


def attend_block(q_heads, k_heads, v_heads, same_seg, score_scale):
    scores_blk = block_scores(q_heads, k_heads, same_seg, score_scale)
    top_val = jnp.max(scores_blk, -1, keepdims=True)
    lse_blk = top_val + jnp.log(jnp.sum(jnp.exp(scores_blk - top_val), -1, keepdims=True))
    probs = jnp.exp(scores_blk - lse_blk).astype(jnp.bfloat16)
    out_blk = jnp.einsum("hqk,khe->qhe", probs, v_heads, preferred_element_type=jnp.float32)
    return (out_blk.reshape(out_blk.shape[0], -1).astype(jnp.bfloat16), lse_blk)


def attend_back(q_heads, k_heads, v_heads, same_seg, score_scale, lse_blk, g_out):
    scores_blk = block_scores(q_heads, k_heads, same_seg, score_scale)
    probs = jnp.exp(scores_blk - lse_blk)
    g_probs = jnp.einsum("qhe,khe->hqk", g_out, v_heads, preferred_element_type=jnp.float32)
    g_v = jnp.einsum(
        "hqk,qhe->khe", probs.astype(jnp.bfloat16), g_out, preferred_element_type=jnp.float32
    )
    g_scores = probs * (g_probs - jnp.sum(probs * g_probs, -1, keepdims=True))
    g_scores = g_scores.astype(jnp.bfloat16)
    g_q = (
        jnp.einsum("hqk,khe->qhe", g_scores, k_heads, preferred_element_type=jnp.float32)
        * score_scale
    )
    g_k = (
        jnp.einsum("hqk,qhe->khe", g_scores, q_heads, preferred_element_type=jnp.float32)
        * score_scale
    )
    tokens_here = g_q.shape[0]
    return (
        g_q.reshape(tokens_here, -1),
        g_k.reshape(tokens_here, -1),
        g_v.reshape(tokens_here, -1),
    )


def spread_rows(values):
    return lax.all_gather(values, "mp", axis=0, tiled=True)


def spread_grad(values):
    return lax.all_gather(values, "mp", axis=0, tiled=True)


def collect_rows(left_side, weight_mat, shard_rows):

    def term_fn(start_at, count_rows):
        return jnp.dot(left_side, weight_mat, preferred_element_type=jnp.float32)

    return lax.psum_scatter(
        term_fn(jnp.int32(0), shard_rows * lax.axis_size("mp")),
        "mp",
        scatter_dimension=0,
        tiled=True,
    )


def collect_grad(left_side, weight_mat, shard_rows):

    def term_fn(start_at, count_rows):
        return right_t(left_side, weight_mat)

    return lax.psum_scatter(
        term_fn(jnp.int32(0), lax.axis_size("mp") * shard_rows).astype(jnp.bfloat16),
        "mp",
        scatter_dimension=0,
        tiled=True,
    ).astype(jnp.float32)


def combine_top(first, second):
    top_both = jnp.maximum(first[0], second[0])
    mass_both = first[1] * jnp.exp(first[0] - top_both) + second[1] * jnp.exp(second[0] - top_both)
    return (top_both, mass_both, first[2] + second[2])


def on_device(
    passages_in,
    queries,
    w_qkv,
    b_qv,
    w_out,
    b_out,
    ln_gain,
    ln_shift,
    w_up,
    b_up,
    w_down,
    b_down,
    w_proj,
    lengths,
    passage_group,
    positive,
):
    n_mp = lax.axis_size("mp")
    n_dp = lax.axis_size("dp")
    shard_rows = passages_in.shape[0]
    model_width = passages_in.shape[1]
    micro_count, per_micro = lengths.shape
    tok_dev = shard_rows * n_mp
    tok_mb = tok_dev // micro_count
    layer_count = w_qkv.shape[0]
    local_width = w_qkv.shape[3]
    head_size = HEAD
    score_scale = head_size ** (-0.5)
    passage_ends = jnp.cumsum(lengths, 1)
    positions = jnp.arange(tok_mb, dtype=jnp.int32)
    segments = jnp.sum((passage_ends[:, None, :] <= positions[None, :, None]).astype(jnp.int32), 2)
    same_lists = [
        segments[micro_at][:, None] == segments[micro_at][None, :]
        for micro_at in range(micro_count)
    ]
    residual = passages_in.astype(jnp.float32)
    stored = []
    for layer_at in range(layer_count):
        x_low = residual.astype(jnp.bfloat16)
        x_all = spread_rows(x_low)
        projected = jnp.dot(
            x_all,
            w_qkv[layer_at].reshape(model_width, 3 * local_width),
            preferred_element_type=jnp.float32,
        )
        q_val = (projected[:, :local_width] + b_qv[layer_at, 0]).astype(jnp.bfloat16)
        k_val = projected[:, local_width : 2 * local_width].astype(jnp.bfloat16)
        v_val = (projected[:, 2 * local_width :] + b_qv[layer_at, 1]).astype(jnp.bfloat16)
        out_list = []
        lse_list = []
        for micro_at in range(micro_count):
            lower = micro_at * tok_mb
            out_blk, lse_blk = attend_block(
                split_heads(q_val[lower : lower + tok_mb], head_size),
                split_heads(k_val[lower : lower + tok_mb], head_size),
                split_heads(v_val[lower : lower + tok_mb], head_size),
                same_lists[micro_at],
                score_scale,
            )
            out_list.append(out_blk)
            lse_list.append(lse_blk)
        attended = jnp.concatenate(out_list, 0)
        branch_one = collect_rows(attended, w_out[layer_at], shard_rows) + b_out[layer_at]
        y_one, n_one, r_one = layer_norm(
            residual + branch_one, ln_gain[layer_at, 0], ln_shift[layer_at, 0]
        )
        y_low = y_one.astype(jnp.bfloat16)
        up_all = w_up[layer_at]
        down_all = w_down[layer_at]
        ffn_in = spread_rows(y_low)
        pre_act = jnp.dot(ffn_in, up_all, preferred_element_type=jnp.float32) + b_up[
            layer_at
        ].astype(jnp.float32)
        hidden = gelu_exact(pre_act).astype(jnp.bfloat16)
        branch_two = collect_rows(hidden, down_all, shard_rows) + b_down[layer_at]
        y_two, n_two, r_two = layer_norm(
            y_one + branch_two, ln_gain[layer_at, 1], ln_shift[layer_at, 1]
        )
        stored.append(
            (
                x_all,
                q_val,
                k_val,
                v_val,
                lse_list,
                attended,
                n_one,
                r_one,
                ffn_in,
                pre_act,
                hidden,
                up_all,
                down_all,
                n_two,
                r_two,
            )
        )
        residual = y_two
    final_low = residual.astype(jnp.bfloat16)
    embedded = jnp.dot(final_low, w_proj, preferred_element_type=jnp.float32)
    unit_scale = lax.rsqrt(jnp.sum(embedded * embedded, -1, keepdims=True) + UNIT_EPS)
    unit_vec = embedded * unit_scale
    unit_low = unit_vec.astype(jnp.bfloat16)
    proj_width = w_proj.shape[1]
    q_group = queries.shape[0]
    q_piece = queries.shape[1]
    gathered = lax.all_gather(queries, ("dp", "mp"), axis=0, tiled=True)
    q_tok = q_group * n_mp * q_piece
    gathered = gathered.reshape(n_dp, n_mp, q_group, q_piece, proj_width).transpose(0, 2, 1, 3, 4)
    gathered = gathered.reshape(n_dp, q_tok, proj_width)
    n_pass = micro_count * per_micro
    groups = passage_group.reshape(n_pass)
    picked = gathered[groups]
    flat_q = picked.reshape(n_pass * q_tok, proj_width)
    mp_here = lax.axis_index("mp")
    places = mp_here * shard_rows + jnp.arange(shard_rows, dtype=jnp.int32)
    which_micro = places // tok_mb
    within = places % tok_mb
    seg_here = jnp.sum((passage_ends[which_micro] <= within[:, None]).astype(jnp.int32), 1)
    passage_here = which_micro * per_micro + seg_here
    owners = (passage_here[:, None] == jnp.arange(n_pass, dtype=jnp.int32)[None, :]).astype(
        jnp.float32
    )
    similar = right_t(unit_low, flat_q)
    weights_tok = (
        jnp.exp(SHARP * (similar - 1.0)).reshape(shard_rows, n_pass, q_tok) * owners[:, :, None]
    )
    partial_sums = jnp.sum(weights_tok, 0)
    totals = lax.psum(partial_sums, "mp")
    span_len = lengths.reshape(n_pass).astype(jnp.float32)
    term_all = (jnp.log(totals) - jnp.log(span_len)[:, None]) / SHARP + 1.0
    q_len = q_tok // q_group
    logits = jnp.sum(term_all.reshape(n_pass, q_group, q_len), -1) / TEMPER
    dp_here = lax.axis_index("dp")
    member = groups[:, None] == jnp.arange(n_dp, dtype=jnp.int32)[None, :]
    identity = dp_here * n_pass + jnp.arange(n_pass, dtype=jnp.int32)
    targets = positive.reshape(n_dp, q_group)
    hit_mask = member[:, :, None] & (targets[None, :, :] == identity[:, None, None])
    spread_logit = jnp.where(member[:, :, None], logits[:, None, :], FLOOR)
    top_here = jnp.max(spread_logit, 0)
    mass_here = jnp.sum(
        jnp.where(member[:, :, None], jnp.exp(spread_logit - top_here[None]), 0.0), 0
    )
    aim_here = jnp.sum(jnp.where(hit_mask, logits[:, None, :], 0.0), 0)
    top_all, mass_all, aim_all = joined((top_here, mass_here, aim_here), "dp", combine_top)
    lse_q = top_all + jnp.log(mass_all)
    query_loss = lax.dynamic_index_in_dim(lse_q - aim_all, dp_here, 0, keepdims=False)
    lse_pass = jnp.sum(jnp.where(member[:, :, None], lse_q[None], 0.0), 1)
    aimed_at = jnp.sum(hit_mask.astype(jnp.float32), 1)
    g_logit = jnp.exp(logits - lse_pass) - aimed_at
    g_term = jnp.broadcast_to((g_logit / TEMPER)[:, :, None], (n_pass, q_group, q_len)).reshape(
        n_pass, q_tok
    )
    g_total = g_term / (SHARP * totals)
    g_sim = (
        (SHARP * weights_tok * g_total[None])
        .reshape(shard_rows, n_pass * q_tok)
        .astype(jnp.bfloat16)
    )
    g_unit = jnp.dot(g_sim, flat_q, preferred_element_type=jnp.float32)
    g_picked = rows_dot(g_sim, unit_low).reshape(n_pass, q_tok, proj_width)
    g_groups = jnp.einsum(
        "pg,pqd->gqd", member.astype(jnp.float32), g_picked, precision=lax.Precision.HIGHEST
    )
    g_groups = g_groups.reshape(n_dp, q_group, n_mp, q_piece, proj_width).transpose(0, 2, 1, 3, 4)
    g_groups = g_groups.reshape(n_dp * n_mp * q_group, q_piece, proj_width)
    query_grad = lax.psum_scatter(g_groups, ("dp", "mp"), scatter_dimension=0, tiled=True)
    g_emb = unit_scale * (g_unit - unit_vec * jnp.sum(g_unit * unit_vec, -1, keepdims=True))
    g_emb_low = g_emb.astype(jnp.bfloat16)
    g_proj = rows_dot(final_low, g_emb_low)
    g_resid = right_t(g_emb_low, w_proj)
    list_wqkv = [None] * layer_count
    list_bqv = [None] * layer_count
    list_wout = [None] * layer_count
    list_bout = [None] * layer_count
    list_gain = [None] * layer_count
    list_shift = [None] * layer_count
    list_wup = [None] * layer_count
    list_bup = [None] * layer_count
    list_wdown = [None] * layer_count
    list_bdown = [None] * layer_count
    for layer_at in reversed(range(layer_count)):
        (
            x_all,
            q_val,
            k_val,
            v_val,
            lse_list,
            attended,
            n_one,
            r_one,
            ffn_in,
            pre_act,
            hidden,
            up_all,
            down_all,
            n_two,
            r_two,
        ) = stored[layer_at]
        g_z_two, g_gain_two, g_shift_two = norm_back(g_resid, n_two, r_two, ln_gain[layer_at, 1])
        g_branch_two = g_z_two.astype(jnp.bfloat16)
        list_bdown[layer_at] = jnp.sum(g_branch_two.astype(jnp.float32), 0)
        _, gelu_pull = jax.vjp(gelu_exact, pre_act)
        g_all_two = spread_grad(g_branch_two)
        g_w_down = rows_dot(hidden, g_all_two)
        g_hidden = right_t(g_all_two, down_all)
        g_pre = gelu_pull(g_hidden)[0].astype(jnp.bfloat16)
        g_w_up = rows_dot(ffn_in, g_pre)
        g_b_up = jnp.sum(g_pre.astype(jnp.float32), 0)
        g_from_ffn = collect_grad(g_pre, up_all, shard_rows)
        list_wdown[layer_at] = g_w_down
        list_wup[layer_at] = g_w_up
        list_bup[layer_at] = g_b_up
        g_z_one, g_gain_one, g_shift_one = norm_back(
            g_z_two + g_from_ffn, n_one, r_one, ln_gain[layer_at, 0]
        )
        list_gain[layer_at] = jnp.stack([g_gain_one, g_gain_two])
        list_shift[layer_at] = jnp.stack([g_shift_one, g_shift_two])
        g_branch_one = g_z_one.astype(jnp.bfloat16)
        list_bout[layer_at] = jnp.sum(g_branch_one.astype(jnp.float32), 0)
        g_all_one = spread_grad(g_branch_one)
        list_wout[layer_at] = rows_dot(attended, g_all_one)
        g_attended = right_t(g_all_one, w_out[layer_at]).astype(jnp.bfloat16)
        q_parts, k_parts, v_parts = ([], [], [])
        for micro_at in range(micro_count):
            lower = micro_at * tok_mb
            g_q, g_k, g_v = attend_back(
                split_heads(q_val[lower : lower + tok_mb], head_size),
                split_heads(k_val[lower : lower + tok_mb], head_size),
                split_heads(v_val[lower : lower + tok_mb], head_size),
                same_lists[micro_at],
                score_scale,
                lse_list[micro_at],
                split_heads(g_attended[lower : lower + tok_mb], head_size),
            )
            q_parts.append(g_q)
            k_parts.append(g_k)
            v_parts.append(g_v)
        g_qkv = jnp.concatenate(
            [jnp.concatenate(q_parts, 0), jnp.concatenate(k_parts, 0), jnp.concatenate(v_parts, 0)],
            1,
        ).astype(jnp.bfloat16)
        list_wqkv[layer_at] = rows_dot(x_all, g_qkv).reshape(model_width, 3, local_width)
        g_qkv_sum = jnp.sum(g_qkv.astype(jnp.float32), 0)
        list_bqv[layer_at] = jnp.stack([g_qkv_sum[:local_width], g_qkv_sum[2 * local_width :]])
        g_resid = g_z_one + collect_grad(
            g_qkv, w_qkv[layer_at].reshape(model_width, 3 * local_width), shard_rows
        )
    g_wqkv, g_bqv, g_wout, g_wup, g_bup, g_wdown = lax.psum(
        (
            jnp.stack(list_wqkv),
            jnp.stack(list_bqv),
            jnp.stack(list_wout),
            jnp.stack(list_wup),
            jnp.stack(list_bup),
            jnp.stack(list_wdown),
        ),
        "dp",
    )
    g_bout, g_lngain, g_lnshift, g_bdown, g_wproj = lax.psum(
        (
            jnp.stack(list_bout),
            jnp.stack(list_gain),
            jnp.stack(list_shift),
            jnp.stack(list_bdown),
            g_proj,
        ),
        ("dp", "mp"),
    )
    return (
        query_loss,
        g_resid,
        query_grad,
        g_wqkv,
        g_bqv,
        g_wout,
        g_bout,
        g_lngain,
        g_lnshift,
        g_wup,
        g_bup,
        g_wdown,
        g_bdown,
        g_wproj,
    )


def solution(mesh):
    placed = (
        P(("dp", "mp"), None),
        P("dp", "mp", None),
        P(None, None, None, "mp"),
        P(None, None, "mp"),
        P(None, "mp", None),
        P(),
        P(),
        P(),
        P(None, None, "mp"),
        P(None, "mp"),
        P(None, "mp", None),
        P(),
        P(),
        P("dp", None),
        P("dp", None),
        P(),
    )
    return jax.shard_map(
        on_device,
        mesh=mesh,
        in_specs=placed,
        out_specs=(
            P("dp"),
            P(("dp", "mp"), None),
            P("dp", "mp", None),
            P(None, None, None, "mp"),
            P(None, None, "mp"),
            P(None, "mp", None),
            P(),
            P(),
            P(),
            P(None, None, "mp"),
            P(None, "mp"),
            P(None, "mp", None),
            P(),
            P(),
        ),
        check_vma=False,
    )
```

profile of v0, /device:TPU:0, one launch (start us, length us, event | category | flops | bytes accessed | tf_op | source)
XLA Modules:
  0.0 1869.4 jit_solution(7532022962706610187)
XLA Ops:
  14.1 29.0 %all-gather.15.cloned.1.call-done = bf16[2304,768]{1,0:T(8,128)(2,1)} async-done(((bf16[576,768]{1,0:T(8,128)(2,1)}), bf16[2304,768]{1,0:T(8,128)(2,1)}) %all-gather.15.cloned.1.call-update) | async-done | bytes 3538960 | tf_op jit(solution)/shard_map/all_gather | solution.py:108
  99.3 62.5 %reduce-scatter.10.cloned.1.call-done = f32[576,768]{1,0:T(8,128)} async-done(((f32[2304,768]{1,0:T(8,128)}), f32[576,768]{1,0:T(8,128)}) %reduce-scatter.10.cloned.1.call-update) | async-done | bytes 1769488 | tf_op jit(solution)/shard_map/reduce_scatter | solution.py:120
  165.4 30.8 %all-gather.17.cloned.1.call-done = bf16[2304,768]{1,0:T(8,128)(2,1)} async-done(((bf16[576,768]{1,0:T(8,128)(2,1)}), bf16[2304,768]{1,0:T(8,128)(2,1)}) %all-gather.17.cloned.1.call-update) | async-done | bytes 3538960 | tf_op jit(solution)/shard_map/all_gather | solution.py:108
  196.2 20.8 %multiply_convert_fusion.5 = (bf16[2304,768]{1,0:T(8,128)(2,1)S(1)}, f32[2304,768]{1,0:T(8,128)}, f32[2304,768]{1,0:T(8,128)}) fusion(f32[768]{0:T(1024)S(1)} %get-tuple-element.87, bf16[2304,768]{1,0:T(8,128)(2,1)} %all-gather.17.cloned.1.call-done, bf16[2,768,768]{2,1,0:T(8,128)(2,1)} %param.26), kind=kOutput, calls=%fused_computation.58 | convolution fusion | flops 2834694144 | bytes 22416384 | tf_op jit(solution)/shard_map/dot_general | solution.py:218
  224.4 63.2 %reduce-scatter.12.cloned.1.call-done = f32[576,768]{1,0:T(8,128)} async-done(((f32[2304,768]{1,0:T(8,128)}), f32[576,768]{1,0:T(8,128)}) %reduce-scatter.12.cloned.1.call-update) | async-done | bytes 1769488 | tf_op jit(solution)/shard_map/reduce_scatter | solution.py:120
  292.5 30.7 %all-gather.19.cloned.1.call-done = bf16[2304,768]{1,0:T(8,128)(2,1)} async-done(((bf16[576,768]{1,0:T(8,128)(2,1)}), bf16[2304,768]{1,0:T(8,128)(2,1)}) %all-gather.19.cloned.1.call-update) | async-done | bytes 3538960 | tf_op jit(solution)/shard_map/all_gather | solution.py:108
  378.7 63.8 %reduce-scatter.14.cloned.1.call-done = f32[576,768]{1,0:T(8,128)} async-done(((f32[2304,768]{1,0:T(8,128)}), f32[576,768]{1,0:T(8,128)}) %reduce-scatter.14.cloned.1.call-update) | async-done | bytes 1769488 | tf_op jit(solution)/shard_map/reduce_scatter | solution.py:120
  447.6 30.5 %all-gather.21.cloned.1.call-done = bf16[2304,768]{1,0:T(8,128)(2,1)} async-done(((bf16[576,768]{1,0:T(8,128)(2,1)}), bf16[2304,768]{1,0:T(8,128)(2,1)}) %all-gather.21.cloned.1.call-update) | async-done | bytes 3538960 | tf_op jit(solution)/shard_map/all_gather | solution.py:108
  478.0 20.4 %multiply_convert_fusion.4 = (bf16[2304,768]{1,0:T(8,128)(2,1)S(1)}, f32[2304,768]{1,0:T(8,128)}, f32[2304,768]{1,0:T(8,128)}) fusion(f32[768]{0:T(1024)S(1)} %get-tuple-element.86, bf16[2304,768]{1,0:T(8,128)(2,1)} %all-gather.21.cloned.1.call-done, bf16[2,768,768]{2,1,0:T(8,128)(2,1)S(1)} %copy-done.144), kind=kOutput, calls=%fused_computation.45 | convolution fusion | flops 2834694144 | bytes 22417408 | tf_op jit(solution)/shard_map/dot_general | solution.py:218
  506.2 41.3 %all_gather.49 = bf16[64,8,128]{2,1,0:T(8,128)(2,1)S(1)} all-gather(bf16[2,8,128]{2,1,0:T(8,128)(2,1)S(1)} %copy-done.124), channel_id=1, replica_groups=mesh['dp'=8,'mp'=4] {'dp','mp'}, dimensions={0}, use_global_device_ids=true | all-gather | bytes 135168 | tf_op jit(solution)/shard_map/all_gather | solution.py:254
  555.0 14.3 reduce-scatter.16.cloned.1.call-done
  581.5 20.7 %all-gather.5 = f32[8,8,2]{1,2,0:T(2,128)S(1)} all-gather(f32[1,8,2]{1,2,0:T(2,128)S(1)} %bitcast.375), channel_id=4, replica_groups=mesh['dp'=8,'mp'=4] {'dp'}, dimensions={0}, use_global_device_ids=true | all-gather | bytes 576 | tf_op jit(solution)/shard_map/all_gather | solution.py:18
  602.2 16.3 all-gather.4
  618.5 18.4 all-gather.3
  646.6 28.0 %all-gather.23.cloned.1.call-done = bf16[2304,768]{1,0:T(8,128)(2,1)} async-done(((bf16[576,768]{1,0:T(8,128)(2,1)}), bf16[2304,768]{1,0:T(8,128)(2,1)}) %all-gather.23.cloned.1.call-update) | async-done | bytes 3538960 | tf_op jit(solution)/shard_map/all_gather | solution.py:112
  674.6 12.3 convert_reduce_fusion
  693.2 40.5 %reduce-scatter.18.cloned.1.call-done = bf16[576,768]{1,0:T(8,128)(2,1)} async-done(((bf16[2304,768]{1,0:T(8,128)(2,1)}), bf16[576,768]{1,0:T(8,128)(2,1)}) %reduce-scatter.18.cloned.1.call-update) | async-done | bytes 884752 | tf_op jit(solution)/shard_map/reduce_scatter | solution.py:133
  741.3 30.9 %all-gather.25.cloned.1.call-done = bf16[2304,768]{1,0:T(8,128)(2,1)} async-done(((bf16[576,768]{1,0:T(8,128)(2,1)}), bf16[2304,768]{1,0:T(8,128)(2,1)}) %all-gather.25.cloned.1.call-update) | async-done | bytes 3538960 | tf_op jit(solution)/shard_map/all_gather | solution.py:112
  783.8 13.4 multiply_reduce_fusion.3
  834.9 13.6 convolution_convert_fusion.3
  848.6 40.6 %reduce-scatter.20.cloned.1.call-done = bf16[576,768]{1,0:T(8,128)(2,1)} async-done(((bf16[2304,768]{1,0:T(8,128)(2,1)}), bf16[576,768]{1,0:T(8,128)(2,1)}) %reduce-scatter.20.cloned.1.call-update) | async-done | bytes 884752 | tf_op jit(solution)/shard_map/reduce_scatter | solution.py:133
  897.0 30.7 %all-gather.27.cloned.1.call-done = bf16[2304,768]{1,0:T(8,128)(2,1)} async-done(((bf16[576,768]{1,0:T(8,128)(2,1)}), bf16[2304,768]{1,0:T(8,128)(2,1)}) %all-gather.27.cloned.1.call-update) | async-done | bytes 3538960 | tf_op jit(solution)/shard_map/all_gather | solution.py:112
  927.7 11.8 convert_reduce_fusion.1
  945.8 40.5 %reduce-scatter.22.cloned.1.call-done = bf16[576,768]{1,0:T(8,128)(2,1)} async-done(((bf16[2304,768]{1,0:T(8,128)(2,1)}), bf16[576,768]{1,0:T(8,128)(2,1)}) %reduce-scatter.22.cloned.1.call-update) | async-done | bytes 884752 | tf_op jit(solution)/shard_map/reduce_scatter | solution.py:133
  992.8 30.9 %all-gather.29.cloned.1.call-done = bf16[2304,768]{1,0:T(8,128)(2,1)} async-done(((bf16[576,768]{1,0:T(8,128)(2,1)}), bf16[2304,768]{1,0:T(8,128)(2,1)}) %all-gather.29.cloned.1.call-update) | async-done | bytes 3538960 | tf_op jit(solution)/shard_map/all_gather | solution.py:112
  1035.3 13.5 multiply_reduce_fusion.1
  1086.3 13.6 convolution_convert_fusion.2
  1149.2 41.2 %all-reduce = (f32[2,768]{1,0:T(2,128)}, f32[2,2,768]{2,1,0:T(2,128)}, f32[2,2,768]{2,1,0:T(2,128)}, f32[2,768]{1,0:T(2,128)}) all-reduce(f32[2,768]{1,0:T(2,128)S(1)} %pad_maximum_fusion.12, f32[2,2,768]{2,1,0:T(2,128)S(1)} %pad_maximum_fusion.10, ...), channel_id=1, replica_groups=mesh['dp'=8,'mp'=4] {'dp','mp'}, use_global_device_ids=true, to_apply=%region_59.60 | all-reduce | flops 9216 | bytes 73728 | tf_op jit(solution)/shard_map/psum | solution.py:407
  1192.4 36.8 %all-reduce.1 = (f32[2,2,192]{2,1,0:T(2,128)}, f32[2,768]{1,0:T(2,128)}) all-reduce(f32[2,2,192]{2,1,0:T(2,128)S(1)} %pad_maximum_fusion.15, f32[2,768]{1,0:T(2,128)S(1)} %pad_maximum_fusion.13), channel_id=1, replica_groups=mesh['dp'=8,'mp'=4] {'dp'}, use_global_device_ids=true, to_apply=%region_55.56 | all-reduce | flops 2304 | bytes 18432 | tf_op jit(solution)/shard_map/psum | solution.py:396
  1231.8 42.0 %all-reduce.6.cloned.1.call-done = f32[768,128]{1,0:T(8,128)} async-done(((f32[768,128]{1,0:T(8,128)}), f32[768,128]{1,0:T(8,128)}) %all-reduce.6.cloned.1.call-update) | async-done | bytes 393232 | tf_op jit(solution)/shard_map/psum | solution.py:407
  1273.7 135.2 %reduce-scatter.26.cloned.1.call-done = f32[2,8,128]{2,1,0:T(8,128)} async-done(((f32[64,8,128]{2,1,0:T(8,128)}), f32[2,8,128]{2,1,0:T(8,128)}) %reduce-scatter.26.cloned.1.call-update) | async-done | bytes 8208 | tf_op jit(solution)/shard_map/reduce_scatter | solution.py:314
  1408.9 441.9 %all-reduce.8.cloned.1.call-done = (f32[2,768,3,192]{1,3,2,0:T(8,128)}, f32[2,192,768]{2,1,0:T(8,128)}, f32[2,768,768]{2,1,0:T(8,128)}, f32[2,768,768]{2,1,0:T(8,128)}) async-done(((f32[2,768,3,192]{1,3,2,0:T(8,128)}, f32[2,192,768]{2,1,0:T(8,128)}, f32[2,768,768]{2,1,0:T(8,128)}, f32[2,768,768]{2,1,0:T(8,128)}), (f32[2,768,3,192]{1,3,2,0:T(8,128)}, f32[2,192,768]{2,1,0:T(8,128)}, f32[2,768,768]{2,1,0:T(8,128)}, ...) | async-done | bytes 14155792 | tf_op jit(solution)/shard_map/psum | solution.py:396
  (606 shorter events, 373.0 us)
Async XLA Ops:
  7.2 565.1 %copy-start = (bf16[768,128]{1,0:T(8,128)(2,1)S(1)}, bf16[768,128]{1,0:T(8,128)(2,1)}, u32[]{:S(2)}) copy-start(bf16[768,128]{1,0:T(8,128)(2,1)} %param.30) | copy-start | bytes 589828
  7.2 35.9 %all-gather.15.cloned.1.call-start = ((), (), s32[]{:S(2)}) async-start(), calls=%async_computation.9 | async-start | bytes 4423680 | tf_op jit(solution)/shard_map/all_gather | solution.py:108
  7.9 153.9 %reduce-scatter.10.cloned.1.call-start = ((), (), s32[]{:S(2)}) async-start(), calls=%async_computation.10 | async-start | bytes 8847360 | tf_op jit(solution)/shard_map/reduce_scatter | solution.py:120
  97.9 63.9 %copy-start.40 = (bf16[576,768]{1,0:T(8,128)(2,1)S(1)}, bf16[576,768]{1,0:T(8,128)(2,1)}, u32[]{:S(2)}) copy-start(bf16[576,768]{1,0:T(8,128)(2,1)} %param.18) | copy-start | bytes 2654212
  97.9 98.3 %all-gather.17.cloned.1.call-start = ((), (), s32[]{:S(2)}) async-start(), calls=%async_computation.11 | async-start | bytes 4423680 | tf_op jit(solution)/shard_map/all_gather | solution.py:108
  99.3 188.3 %copy-start.100 = (f32[768]{0:T(1024)}, f32[768]{0:T(1024)S(1)}, u32[]{:S(2)}) copy-start(f32[768]{0:T(1024)S(1)} %get-tuple-element.212) | copy-start | bytes 9220
  99.3 343.2 %copy-start.102 = (f32[768]{0:T(1024)}, f32[768]{0:T(1024)S(1)}, u32[]{:S(2)}) copy-start(f32[768]{0:T(1024)S(1)} %get-tuple-element.213) | copy-start | bytes 9220
  163.6 124.0 %copy-start.4 = (f32[576,768]{1,0:T(8,128)}, f32[576,768]{1,0:T(8,128)S(1)}, u32[]{:S(2)}) copy-start(f32[576,768]{1,0:T(8,128)S(1)} %get-tuple-element.142) | copy-start | bytes 5308420
  163.6 123.9 %copy-start.94 = (f32[576]{0:T(1024)}, f32[576]{0:T(1024)S(1)}, u32[]{:S(2)}) copy-start(f32[576]{0:T(1024)S(1)} %broadcast_multiply_fusion.11) | copy-start | bytes 6916
  164.0 123.6 %copy-start.104 = (f32[576]{0:T(1024)}, f32[576]{0:T(1024)S(1)}, u32[]{:S(2)}) copy-start(f32[576]{0:T(1024)S(1)} %add_rsqrt_fusion.4) | copy-start | bytes 6916
  165.3 122.3 %reduce-scatter.12.cloned.1.call-start = ((), (), s32[]{:S(2)}) async-start(), calls=%async_computation.12 | async-start | bytes 8847360 | tf_op jit(solution)/shard_map/reduce_scatter | solution.py:120
  223.7 99.5 %all-gather.19.cloned.1.call-start = ((), (), s32[]{:S(2)}) async-start(), calls=%async_computation.13 | async-start | bytes 4423680 | tf_op jit(solution)/shard_map/all_gather | solution.py:108
  289.8 152.7 %copy-start.96 = (f32[576]{0:T(1024)}, f32[576]{0:T(1024)S(1)}, u32[]{:S(2)}) copy-start(f32[576]{0:T(1024)S(1)} %broadcast_multiply_fusion.10) | copy-start | bytes 6916
  290.1 152.4 %copy-start.106 = (f32[576]{0:T(1024)}, f32[576]{0:T(1024)S(1)}, u32[]{:S(2)}) copy-start(f32[576]{0:T(1024)S(1)} %add_rsqrt_fusion.3) | copy-start | bytes 6916
  292.2 150.2 %reduce-scatter.14.cloned.1.call-start = ((), (), s32[]{:S(2)}) async-start(), calls=%async_computation.14 | async-start | bytes 8847360 | tf_op jit(solution)/shard_map/reduce_scatter | solution.py:120
  378.6 63.9 %copy-start.7 = (f32[576,768]{1,0:T(8,128)S(1)}, f32[576,768]{1,0:T(8,128)}, u32[]{:S(2)}) copy-start(f32[576,768]{1,0:T(8,128)} %copy-done.6) | copy-start | bytes 5308420
  378.6 99.4 %all-gather.21.cloned.1.call-start = ((), (), s32[]{:S(2)}) async-start(), calls=%async_computation.15 | async-start | bytes 4423680 | tf_op jit(solution)/shard_map/all_gather | solution.py:108
  447.1 122.2 %reduce-scatter.16.cloned.1.call-start = ((), (), s32[]{:S(2)}) async-start(), calls=%async_computation.16 | async-start | bytes 8847360 | tf_op jit(solution)/shard_map/reduce_scatter | solution.py:120
  505.1 169.4 %all-gather.23.cloned.1.call-start = ((), (), s32[]{:S(2)}) async-start(), calls=%async_computation.17 | async-start | bytes 4423680 | tf_op jit(solution)/shard_map/all_gather | solution.py:112
  572.8 68.0 %copy-start.17 = (f32[576,128]{1,0:T(8,128)}, f32[576,128]{1,0:T(8,128)S(1)}, u32[]{:S(2)}) copy-start(f32[576,128]{1,0:T(8,128)S(1)} %get-tuple-element.189) | copy-start | bytes 884740
  572.8 68.0 %copy-start.98 = (f32[576]{0:T(1024)}, f32[576]{0:T(1024)S(1)}, u32[]{:S(2)}) copy-start(f32[576]{0:T(1024)S(1)} %add_rsqrt_fusion) | copy-start | bytes 6916
  646.6 87.1 %reduce-scatter.18.cloned.1.call-start = ((), (), s32[]{:S(2)}) async-start(), calls=%async_computation.18 | async-start | bytes 4423680 | tf_op jit(solution)/shard_map/reduce_scatter | solution.py:133
  693.1 79.0 %all-gather.25.cloned.1.call-start = ((), (), s32[]{:S(2)}) async-start(), calls=%async_computation.19 | async-start | bytes 4423680 | tf_op jit(solution)/shard_map/all_gather | solution.py:112
  741.2 148.0 %reduce-scatter.20.cloned.1.call-start = ((), (), s32[]{:S(2)}) async-start(), calls=%async_computation.20 | async-start | bytes 4423680 | tf_op jit(solution)/shard_map/reduce_scatter | solution.py:133
  848.6 79.1 %all-gather.27.cloned.1.call-start = ((), (), s32[]{:S(2)}) async-start(), calls=%async_computation.21 | async-start | bytes 4423680 | tf_op jit(solution)/shard_map/all_gather | solution.py:112
  896.8 89.5 %reduce-scatter.22.cloned.1.call-start = ((), (), s32[]{:S(2)}) async-start(), calls=%async_computation.22 | async-start | bytes 4423680 | tf_op jit(solution)/shard_map/reduce_scatter | solution.py:133
  945.7 78.0 %all-gather.29.cloned.1.call-start = ((), (), s32[]{:S(2)}) async-start(), calls=%async_computation.23 | async-start | bytes 4423680 | tf_op jit(solution)/shard_map/all_gather | solution.py:112
  992.7 236.5 %reduce-scatter.24.cloned.1.call-start = ((), (), s32[]{:S(2)}) async-start(), calls=%async_computation.24 | async-start | bytes 4423680 | tf_op jit(solution)/shard_map/reduce_scatter | solution.py:133
  1100.0 173.8 %all-reduce.6.cloned.1.call-start = ((), (), s32[]{:S(2)}) async-start(), calls=%async_computation.26 | async-start | bytes 786432 | tf_op jit(solution)/shard_map/psum | solution.py:407
  1107.4 301.5 %reduce-scatter.26.cloned.1.call-start = ((), (), s32[]{:S(2)}) async-start(), calls=%async_computation.25 | async-start | bytes 270336 | tf_op jit(solution)/shard_map/reduce_scatter | solution.py:314
  1108.9 742.0 %all-reduce.8.cloned.1.call-start = ((), (), s32[]{:S(2)}) async-start(), calls=%async_computation.27 | async-start | bytes 28311552 | tf_op jit(solution)/shard_map/psum | solution.py:396
  1145.6 83.6 %copy-start.18 = (f32[576,768]{1,0:T(8,128)S(1)}, f32[576,768]{1,0:T(8,128)}, u32[]{:S(2)}) copy-start(f32[576,768]{1,0:T(8,128)} %get-tuple-element.125) | copy-start | bytes 5308420
  (162 other events, 1860.7 us)
Sparse Core Ops, SparseCore 0:
  9.6 33.4 all-gather.14
  98.0 63.6 reduce-scatter.9
  165.4 30.7 all-gather.16
  223.8 63.7 reduce-scatter.11
  292.4 30.7 all-gather.18
  378.7 63.6 reduce-scatter.13
  447.2 30.7 all-gather.20
  505.3 63.9 reduce-scatter.15
  646.7 27.8 all-gather.22
  693.3 40.3 reduce-scatter.17
  741.3 30.7 all-gather.24
  848.7 40.4 reduce-scatter.19
  896.9 30.7 all-gather.26
  945.8 40.3 reduce-scatter.21
  992.9 30.7 all-gather.28
  1100.1 40.4 reduce-scatter.23
  1146.2 127.4 all-reduce.5
  1276.5 132.3 reduce-scatter.25
  1414.8 436.0 all-reduce.7
where the time goes:
time: 1880 us; the launch traced here: 1870 us
  waiting for transfers between devices  1190 us (63%)
  matrix products  303 us (16%)
  blocking collectives  181 us (10%)
  other arithmetic  129 us (7%)
  local copies, waits for them, and re-layouts  52.2 us (3%)
    psum x1, waiting for transfers between devices, on_device(): lax.psum((jnp.stack(list_wqkv), jnp.stack(list_bqv), jnp.stack(list_wout)...  442 us
    reduce_scatter x4, waiting for transfers between devices, collect_rows(): lax.psum_scatter(term_fn(jnp.int32(0), shard_rows * lax.axis_size('mp')),...  204 us
    reduce_scatter x1, waiting for transfers between devices, on_device(): lax.psum_scatter(g_groups, ('dp', 'mp'), scatter_dimension=0, tiled=True)  135 us
    reduce_scatter x4, waiting for transfers between devices, collect_grad(): lax.psum_scatter(term_fn(jnp.int32(0), lax.axis_size('mp') * shard_rows)....  122 us
    all_gather x4, waiting for transfers between devices, spread_rows(): return lax.all_gather(values, 'mp', axis=0, tiled=True)  121 us
    all_gather x4, waiting for transfers between devices, spread_grad(): return lax.all_gather(values, 'mp', axis=0, tiled=True)  120 us
    dot_general x10, matrix products, right_t(): lax.dot_general(left_side, right_side, (((1,), (1,)), ((), ())), preferre...  71.9 us
    all_gather x3, blocking collectives, joined(): pieces = jax.tree.map(lambda part: lax.all_gather(part, axis), value)  55.4 us
  transfers between devices with their start and end apart: 19, of which 18 were waited for; matrix products, arithmetic and copies ran while one was open for 3% of the time, Pallas kernels for 0%

commit v1 on v0

v1 whole, which is shorter than its diff:
```python
from types import SimpleNamespace

import jax
import jax.numpy as jnp
from jax import lax
from jax.experimental import pallas as pl
from jax.experimental.pallas import tpu as pltpu
from jax.sharding import PartitionSpec as P

HEAD = 64
LONGEST = 1024
SHARP = 4.0
TEMPER = 0.2
LN_EPS = 1e-12
UNIT_EPS = 1e-06
MASKED = -1000000000.0
FLOOR = -1e30
Q_ROWS = 512
AHEAD = 3
COST = 5000000
TURNS = (1, 2, 3, 1, 3, 4, 2, 1, 3, 4, 0, 2, 1, 3, 4, 2, 3, 0, 1, 4, 2, 3, 2, 3)
VMEM_LIMIT = 40 * 2**20

bf16 = jnp.bfloat16
f32 = jnp.float32
i32 = jnp.int32
HIGH = lax.Precision.HIGHEST
VMEM = pl.BlockSpec(memory_space=pltpu.VMEM)
SMEM = pl.BlockSpec(memory_space=pltpu.SMEM)
HBM = pl.BlockSpec(memory_space=pltpu.HBM)
NEAR, FAR, SCALAR = range(3)


def nn(left_side, right_side):
    return lax.dot_general(
        left_side, right_side, (((1,), (0,)), ((), ())), preferred_element_type=f32
    )


def nt(left_side, right_side):
    return lax.dot_general(
        left_side, right_side, (((1,), (1,)), ((), ())), preferred_element_type=f32
    )


def tn(left_side, right_side):
    return lax.dot_general(
        left_side, right_side, (((0,), (0,)), ((), ())), preferred_element_type=f32
    )


def exact(left_side, right_side, dims=((1,), (0,))):
    return lax.dot_general(
        left_side, right_side, (dims, ((), ())), precision=HIGH, preferred_element_type=f32
    )


def gelu_pair(values):
    size = jnp.abs(values)
    t = 1.0 / (1.0 + (0.3275911 * 0.7071067811865476) * size)
    bell = jnp.exp(-0.5 * values * values)
    poly = t * (
        0.254829592
        + t * (-0.284496736 + t * (1.421413741 + t * (-1.453152027 + t * 1.061405429)))
    )
    tail = 0.5 * poly * bell
    phi = jnp.where(values < 0, tail, 1.0 - tail)
    return values * phi, phi + values * (0.3989422804014327 * bell)


class Fetched:
    def __init__(self, ref, held, sem, line):
        self.copy, self.held, self.line, self.due = pltpu.make_async_copy(ref, held, sem), held, line, True
        line.append(self)

    def begin(self):
        self.line.remove(self)
        self.copy.start()

    def __getitem__(self, at):
        if self.due:
            if self in self.line:
                self.begin()
            if self.line:
                self.line[0].begin()
            self.copy.wait()
            self.due = False
        value = self.held[at]
        return value.reshape(-1, value.shape[-1]) if value.ndim == 3 else value


class Flushed:
    def __init__(self, ref, held, sems, pieces):
        self.ref, self.held, self.sems, self.pieces = ref, held, sems, pieces
        self.copies = []

    def __getitem__(self, at):
        return self.held[at]

    def __setitem__(self, at, value):
        self.held[at] = value

    def flush(self, which=0):
        first, last = self.pieces[which]
        rows = pl.ds(first, last - first)
        copy = pltpu.make_async_copy(self.held.at[rows], self.ref.at[rows], self.sems.at[which])
        copy.start()
        self.copies.append(copy)


def part_shape(shape, part=()):
    if isinstance(part, int):
        return shape[1:]
    return tuple(len(range(*at.indices(size))) for at, size in zip(part, shape)) + shape[len(part) :]


def run(name, body, operands, results, scratch=()):
    spaces = (pltpu.VMEM, pltpu.HBM)
    kinds = [given[0] for given in operands.values()]
    arrays = [
        given[1] if given[0] == SCALAR else pltpu.with_memory_space_constraint(given[1], spaces[given[0]])
        for given in operands.values()
    ]
    parts = [given[2:] for given in operands.values()]
    fetch = [at for at, kind in enumerate(kinds) if kind == FAR]
    made = list(results.values())
    pieces = {}
    for at, (kind, shape, _) in enumerate(made):
        if kind != NEAR:
            pieces[at] = [(0, shape[0])] if kind == FAR else kind
    added = [pltpu.VMEM(part_shape(arrays[at].shape, *parts[at]), arrays[at].dtype) for at in fetch]
    added += [pltpu.VMEM(made[at][1], made[at][2]) for at in pieces]
    added += [pltpu.SemaphoreType.DMA((max(len(fetch), 1),))]
    added += [pltpu.SemaphoreType.DMA((len(rows),)) for rows in pieces.values()]

    def outer(*refs):
        refs = list(refs)
        first = len(refs) - len(added)
        extra, refs = refs[first:], refs[:first]
        sems = extra[len(fetch) + len(pieces) :]
        line = []
        for count, at in enumerate(fetch):
            ref = refs[at].at[parts[at][0]] if parts[at] else refs[at]
            refs[at] = Fetched(ref, extra[count], sems[0].at[count], line)
        for _ in range(min(AHEAD, len(line))):
            line[0].begin()
        outs = []
        for count, (at, rows) in enumerate(pieces.items()):
            out = Flushed(refs[len(operands) + at], extra[len(fetch) + count], sems[1 + count], rows)
            refs[len(operands) + at] = out
            outs.append(out)
        named = SimpleNamespace(scratch=refs[len(operands) + len(results) :])
        for key, ref in zip(list(operands) + list(results), refs):
            setattr(named, key, ref)
        body(named)
        for at in fetch:
            refs[at][0:1]
        for out in outs:
            for copy in out.copies:
                copy.wait()

    given = pl.pallas_call(
        outer,
        out_shape=tuple(spaces[kind != NEAR](shape, dtype) for kind, shape, dtype in made),
        in_specs=[(VMEM, HBM, SMEM)[kind] for kind in kinds],
        out_specs=tuple(VMEM if kind == NEAR else HBM for kind, _, _ in made),
        scratch_shapes=list(scratch) + added,
        compiler_params=pltpu.CompilerParams(vmem_limit_bytes=VMEM_LIMIT),
        cost_estimate=pl.CostEstimate(flops=COST, transcendentals=0, bytes_accessed=0),
        name=name,
    )(*arrays)
    return SimpleNamespace(**dict(zip(results, given)))


def facts(meta, per):
    core, micro = meta[1] % 2, meta[1] // 2
    ends, begin, last = [], 0, 0
    for at in range(per):
        length = meta[2 + micro * per + at]
        begin = begin + jnp.where(length == LONGEST, last, 0)
        last = last + length
        ends.append(last)
    groups = [meta[2 + 2 * per + micro * per + at] for at in range(per)]
    return core, micro, begin, ends, groups


def long_rows(values, half, small):
    return jnp.concatenate([values[0:half], values[half + small : 2 * half + small]], 0)


def small_rows(values, half, small):
    return jnp.concatenate([values[half : half + small], values[2 * half + small :]], 0)


def q_starts(half, small, step):
    return [at for base in (0, half + small) for at in range(base, base + half, step)]


def segment_of(place, ends):
    return sum((place >= end).astype(i32) for end in ends)


def small_same(meta, per, small):
    core, _, begin, ends, _ = facts(meta, per)

    def segments(shape, axis):
        at = lax.broadcasted_iota(i32, shape, axis)
        which = jnp.where(at < small, core, 1 - core)
        place = begin + LONGEST + which * small + jnp.where(at < small, at, at - small)
        total = LONGEST + 2 * small
        return segment_of(jnp.where(place >= total, place - total, place), ends)

    count = 2 * small
    return segments((count, count), 0) == segments((count, count), 1)


def row_places(meta, per, half, small, axis):
    core, _, begin, _, _ = facts(meta, per)
    own = half + small
    at = lax.broadcasted_iota(i32, (2 * own, 1) if axis == 0 else (1, 2 * own), axis)
    which = jnp.where(at < own, core, 1 - core)
    at = jnp.where(at < own, at, at - own)
    place = begin + jnp.where(at < half, which * half + at, LONGEST + which * small + at - half)
    total = LONGEST + 2 * small
    return jnp.where(place >= total, place - total, place)


def row_segments(meta, per, half, small):
    return segment_of(row_places(meta, per, half, small, 0), facts(meta, per)[3])


def chunks(rows):
    step = rows // PIECES
    return [slice(at, at + step) for at in range(0, rows, step)]


PIECES = 4


def both(refs, rows):
    at = rows.start // (rows.stop - rows.start)
    there = (at + PIECES // 2) % PIECES
    return getattr(refs, f"mine{at}")[...].astype(f32) + getattr(refs, f"came{there}")[...].astype(f32)


def parts_in(norm):
    made = {f"mine{at}": (NEAR, value) for at, value in enumerate(norm.mine)}
    return made | {f"came{at}": (NEAR, value) for at, value in enumerate(norm.came)}


def parts_out(rows, model):
    return {f"mine{at}": (NEAR, (rows // PIECES, model), bf16) for at in range(PIECES)}


def parts_of(got):
    return [getattr(got, f"mine{at}") for at in range(PIECES)]


def norm_into(refs, line):
    vecs = refs.vecs[8 * line : 8 * line + 8]
    for rows in chunks(refs.low.held.shape[0]):
        value = refs.base[rows].astype(f32) + (both(refs, rows) + vecs[0:1])
        centered = value - jnp.mean(value, -1, keepdims=True)
        inv_std = lax.rsqrt(jnp.mean(centered * centered, -1, keepdims=True) + LN_EPS)
        normed = centered * inv_std
        made = normed * vecs[1:2] + vecs[2:3]
        if hasattr(refs, "y"):
            refs.y[rows] = made
        refs.low[rows] = made.astype(bf16)
        refs.n[rows] = normed.astype(bf16)
        refs.r[rows] = inv_std
    for ref in (refs.low, refs.n, refs.r):
        ref.flush()
    if hasattr(refs, "y"):
        refs.y.flush()


def norm_results(rows, width, keep=True):
    made = dict(
        low=(FAR, (rows, width), bf16),
        n=(FAR, (rows, width), bf16),
        r=(FAR, (rows, 1), f32),
    )
    return made | (dict(y=(FAR, (rows, width), f32)) if keep else {})


def norm_back_into(refs, line):
    gain = refs.vecs[8 * line : 8 * line + 8][1:2]
    sums = None
    rows_all = refs.n.held.shape[0]
    for rows in chunks(rows_all):
        if hasattr(refs, "grad"):
            grad = refs.grad[rows]
        else:
            grad = refs.base[rows] + both(refs, rows)
        normed = refs.n[rows].astype(f32)
        inner = grad * gain
        made = refs.r[rows] * (
            inner
            - jnp.mean(inner, -1, keepdims=True)
            - normed * jnp.mean(inner * normed, -1, keepdims=True)
        )
        low = made.astype(bf16)
        refs.g[rows] = made
        refs.low[rows] = low
        lines = [
            jnp.sum(value, 0, keepdims=True) for value in (grad * normed, grad, low.astype(f32))
        ]
        sums = lines if sums is None else [a + b for a, b in zip(sums, lines)]
    refs.g.flush()
    refs.low.flush()
    for at, value in enumerate(sums):
        refs.sums[at : at + 1] = value
    refs.sums[3:] = jnp.zeros((5, sums[0].shape[1]), f32)
    refs.sums.flush()


def heads_into(refs, meta, per, line, heads, half, small):
    width = heads * HEAD
    x_ref = refs.low
    bias = refs.units[line : line + 1]
    made = nt(x_ref[...], refs.w_qkv[...])
    refs.q[...] = (made[:, :width] + bias[:, :width]).astype(bf16)
    refs.k[...] = made[:, width : 2 * width].astype(bf16)
    refs.v[...] = (made[:, 2 * width :] + bias[:, width : 2 * width]).astype(bf16)
    for ref in (refs.q, refs.k, refs.v):
        ref.flush()
    scale = HEAD**-0.5
    same = small_same(meta, per, small)
    a_out, lse_out = refs.a, refs.lse
    for head in range(heads):
        cols = slice(head * HEAD, (head + 1) * HEAD)
        line = slice(head, head + 1)
        k_head = refs.k[:, cols]
        v_head = refs.v[:, cols]
        q_head = refs.q[:, cols] * scale
        k_long = long_rows(k_head, half, small)
        v_long_t = long_rows(v_head, half, small).T
        for at in q_starts(half, small, Q_ROWS):
            scores = nt(k_long, q_head[at : at + Q_ROWS])
            top = jnp.max(scores, 0, keepdims=True)
            probs = jnp.exp(scores - top)
            mass = jnp.sum(probs, 0, keepdims=True)
            out = nn(v_long_t, probs.astype(bf16)) / mass
            a_out[at : at + Q_ROWS, cols] = out.T.astype(bf16)
            lse_out[line, at : at + Q_ROWS] = top + jnp.log(mass)
        scores = nt(small_rows(k_head, half, small), small_rows(q_head, half, small))
        scores = jnp.where(same, scores, MASKED)
        top = jnp.max(scores, 0, keepdims=True)
        probs = jnp.exp(scores - top)
        mass = jnp.sum(probs, 0, keepdims=True)
        out = nn(small_rows(v_head, half, small).T, probs.astype(bf16)) / mass
        out = out.T.astype(bf16)
        a_out[half : half + small, cols] = out[:small]
        a_out[2 * half + small :, cols] = out[small:]
        lse = top + jnp.log(mass)
        lse_out[line, half : half + small] = lse[:, :small]
        lse_out[line, 2 * half + small :] = lse[:, small:]
    a_out.flush()
    lse_out.flush()


def heads_results(rows, width):
    made = (FAR, (rows, width), bf16)
    return dict(q=made, k=made, v=made, a=made, lse=(FAR, (8, rows), f32))


def attend_first(meta, per, small, line, x_all, norm, w_qkv, layer, units):
    width = w_qkv.shape[1] // 3
    heads = width // HEAD
    rows, model = (x_all if norm is None else norm.base).shape
    half = rows // 2 - small
    operands = dict(meta=(SCALAR, meta))
    results = {}
    if norm is None:
        operands |= dict(low=(NEAR, x_all))
    else:
        operands |= parts_in(norm) | dict(base=(FAR, norm.base), vecs=(FAR, norm.vecs))
        results = norm_results(rows, model)
    operands |= dict(w_qkv=(FAR, w_qkv, layer), units=(FAR, units))

    def body(refs):
        if norm is not None:
            norm_into(refs, norm.line)
        heads_into(refs, refs.meta, per, line, heads, half, small)

    return run("attend", body, operands, results | heads_results(rows, width))


def attend_second(meta, per, small, line, x_all, w_qkv, units, a_own, w_out_own, layer, w_out_par):
    width = w_qkv.shape[0] // 3
    heads = width // HEAD
    rows, model = x_all.shape
    half = rows // 2 - small

    def body(refs):
        heads_into(refs, refs.meta, per, line, heads, half, small)
        for at, part in enumerate(chunks(rows)):
            made = nn(refs.a_own[part], refs.wo_own[...]) + nn(refs.a[part], refs.wo_par[...])
            getattr(refs, f"mine{at}")[...] = made.astype(bf16)

    operands = dict(
        meta=(SCALAR, meta),
        low=(FAR, x_all),
        w_qkv=(FAR, w_qkv),
        units=(FAR, units),
        a_own=(FAR, a_own),
        wo_own=(FAR, w_out_own, layer),
        wo_par=(FAR, w_out_par),
    )
    return run("attend", body, operands, heads_results(rows, width) | parts_out(rows, model))


def ffn_into(refs, line):
    bias = refs.units[line : line + 1]
    rows_all = refs.hidden.held.shape[0]
    for rows in chunks(rows_all):
        hidden, slope = gelu_pair(nn(refs.low[rows], refs.w_up[...]) + bias)
        refs.hidden[rows] = hidden.astype(bf16)
        refs.slope[rows] = slope.astype(bf16)
        if rows.stop * 2 % rows_all == 0:
            refs.hidden.flush(rows.stop * 2 // rows_all - 1)
            refs.slope.flush(rows.stop * 2 // rows_all - 1)


def hidden_results(rows, units):
    made = ([(0, rows // 2), (rows // 2, rows)], (rows, units), bf16)
    return dict(hidden=made, slope=made)


def ffn_first(meta, line, norm, w_up, layer, units):
    rows, model = norm.base.shape

    def body(refs):
        norm_into(refs, norm.line)
        ffn_into(refs, line)

    operands = dict(meta=(SCALAR, meta)) | parts_in(norm)
    operands |= dict(
        base=(FAR, norm.base), vecs=(FAR, norm.vecs), w_up=(FAR, w_up, layer), units=(FAR, units)
    )
    return run("ffn", body, operands, norm_results(rows, model) | hidden_results(rows, w_up.shape[2]))


def ffn_second(meta, line, y_low, w_up, units, hidden_own, w_down_own, layer, w_down_par):
    rows, model = y_low.shape

    def body(refs):
        ffn_into(refs, line)
        for at, part in enumerate(chunks(rows)):
            made = nn(refs.hidden_own[part], refs.wd_own[...]) + nn(refs.hidden[part], refs.wd_par[...])
            getattr(refs, f"mine{at}")[...] = made.astype(bf16)

    operands = dict(
        meta=(SCALAR, meta),
        low=(FAR, y_low),
        w_up=w_up,
        units=(FAR, units),
        hidden_own=(FAR, hidden_own),
        wd_own=(FAR, w_down_own, layer),
        wd_par=w_down_par,
    )
    results = hidden_results(rows, w_up[1].shape[-1]) | parts_out(rows, model)
    return run("ffn", body, operands, results)


def norm_back_results(rows, width):
    return dict(
        g=(FAR, (rows, width), f32), low=(FAR, (rows, width), bf16), sums=(FAR, (8, width), f32)
    )


def ffn_back(meta, norm, kept, y_low, w_up, w_down, extra, other):
    rows, model = y_low.shape
    units = w_up[1].shape[-1]
    count = units + model + (0 if extra is None else extra.shape[0])
    first = norm is not None
    operands = dict(meta=(SCALAR, meta))
    operands |= norm.operands if first else dict(low=(FAR, other.low))
    operands |= dict(w_down=w_down, slope=(FAR, kept.slope), hidden=(FAR, kept.hidden), y=(FAR, y_low))
    if extra is not None:
        operands |= dict(extra=(FAR, extra))
    results = dict(
        grads=([(0, units), (units, count)], (count, model), bf16), line=(FAR, (8, units), f32)
    )
    if first:
        results |= norm_back_results(rows, model) | dict(pre=(FAR, (rows, units), bf16))
    else:
        operands |= dict(w_up=w_up, pre_other=(FAR, other.pre), w_up_other=other.w_up)
        results |= parts_out(rows, model)

    def body(refs):
        if first:
            norm_back_into(refs, norm.line)
            pre_ref = refs.pre
        else:
            pre_ref = refs.scratch[0]
        total = None
        for at in chunks(rows):
            pre = (refs.slope[at].astype(f32) * nt(refs.low[at], refs.w_down[...])).astype(bf16)
            pre_ref[at] = pre
            line = jnp.sum(pre.astype(f32), 0, keepdims=True)
            total = line if total is None else total + line
        if first:
            pre_ref.flush()
        refs.line[0:1] = total
        refs.line[1:] = jnp.zeros((7, units), f32)
        refs.line.flush()
        refs.grads[:units] = tn(refs.hidden[...], refs.low[...]).astype(bf16)
        refs.grads.flush(0)
        refs.grads[units : units + model] = tn(refs.y[...], pre_ref[...]).astype(bf16)
        if extra is not None:
            refs.grads[units + model :] = refs.extra[...]
        refs.grads.flush(1)
        if not first:
            for at, part in enumerate(chunks(rows)):
                made = nt(pre_ref[part], refs.w_up[...]) + nt(refs.pre_other[part], refs.w_up_other[...])
                getattr(refs, f"mine{at}")[...] = made.astype(bf16)

    scratch = () if first else (pltpu.VMEM((rows, units), bf16),)
    return run("ffn_back", body, operands, results, scratch=scratch)


def attend_back(meta, per, small, norm, kept, x_all, w_qkv, w_out, other, last):
    rows, model = x_all.shape
    width = w_out[1].shape[-2]
    half = rows // 2 - small
    first = norm is not None
    scale = HEAD**-0.5
    operands = dict(meta=(SCALAR, meta))
    operands |= norm.operands if first else dict(low=(FAR, other.low))
    operands |= dict(
        w_out=w_out,
        a=(FAR, kept.a),
        k=(FAR, kept.k),
        q=(FAR, kept.q),
        lse=(FAR, kept.lse),
        v=(FAR, kept.v),
        x=(FAR, x_all),
    )
    results = dict(
        grads=([(0, 3 * width), (3 * width, 4 * width)], (4 * width, model), bf16),
        line=(FAR, (8, 3 * width), f32),
    )
    if first:
        results |= norm_back_results(rows, model) | dict(g_qkv=(FAR, (rows, 3 * width), bf16))
    else:
        operands |= dict(w_qkv=w_qkv, g_other=(FAR, other.g_qkv), w_other=(FAR, other.w_qkv))
        if last:
            operands |= dict(g_norm=(FAR, other.g))
            results |= dict(own=(NEAR, (rows // 2, model), f32), away=(NEAR, (rows // 2, model), bf16))
        else:
            results |= parts_out(rows, model)
    scratch = [
        pltpu.VMEM((rows, width), bf16),
        pltpu.VMEM((2 * half, HEAD), f32),
        pltpu.VMEM((2 * half, HEAD), f32),
    ]
    if not first:
        scratch.append(pltpu.VMEM((rows, 3 * width), bf16))

    def body(refs):
        if first:
            norm_back_into(refs, norm.line)
            g_ref = refs.g_qkv
        else:
            g_ref = refs.scratch[3]
        da_ref, dv_sum, dk_sum = refs.scratch[:3]
        low = refs.low[...]
        da_ref[...] = nt(low, refs.w_out[...]).astype(bf16)
        refs.grads[3 * width :] = tn(refs.a[...], low).astype(bf16)
        refs.grads.flush(1)
        same = small_same(refs.meta, per, small)
        ones = jnp.ones((8, HEAD), f32)
        for head in range(width // HEAD):
            cols = slice(head * HEAD, (head + 1) * HEAD)
            line = slice(head, head + 1)
            k_head = refs.k[:, cols]
            v_head = refs.v[:, cols]
            q_head = refs.q[:, cols] * scale
            da_head = da_ref[:, cols]
            inner = da_head.astype(f32) * refs.a[:, cols].astype(f32)
            delta = exact(ones, inner, ((1,), (1,)))[0:1]
            k_long = long_rows(k_head, half, small)
            v_long = long_rows(v_head, half, small)
            k_long_t = (k_long * scale).T
            for count, at in enumerate(q_starts(half, small, Q_ROWS)):
                here = slice(at, at + Q_ROWS)
                q_blk = q_head[here]
                da_blk = da_head[here]
                probs = jnp.exp(nt(k_long, q_blk) - refs.lse[line, here])
                g_probs = nt(v_long, da_blk)
                g_scores = (probs * (g_probs - delta[:, here])).astype(bf16)
                g_v = nn(probs.astype(bf16), da_blk)
                g_k = nn(g_scores, q_blk)
                if count == 0:
                    dv_sum[...] = g_v
                    dk_sum[...] = g_k
                else:
                    dv_sum[...] += g_v
                    dk_sum[...] += g_k
                g_ref[here, cols] = nn(k_long_t, g_scores).T.astype(bf16)
            k_cols = slice(width + head * HEAD, width + (head + 1) * HEAD)
            v_cols = slice(2 * width + head * HEAD, 2 * width + (head + 1) * HEAD)
            for part, base in enumerate((0, half + small)):
                g_ref[base : base + half, k_cols] = dk_sum[part * half : (part + 1) * half].astype(bf16)
                g_ref[base : base + half, v_cols] = dv_sum[part * half : (part + 1) * half].astype(bf16)
            k_small = small_rows(k_head, half, small)
            q_small = small_rows(q_head, half, small)
            da_small = small_rows(da_head, half, small)
            lse = jnp.concatenate(
                [refs.lse[line, half : half + small], refs.lse[line, 2 * half + small :]], 1
            )
            delta = jnp.concatenate([delta[:, half : half + small], delta[:, 2 * half + small :]], 1)
            probs = jnp.exp(jnp.where(same, nt(k_small, q_small), MASKED) - lse)
            g_probs = nt(small_rows(v_head, half, small), da_small)
            g_scores = (probs * (g_probs - delta)).astype(bf16)
            for where, made in (
                (cols, nn((k_small * scale).T, g_scores).T),
                (k_cols, nn(g_scores, q_small)),
                (v_cols, nn(probs.astype(bf16), da_small)),
            ):
                g_ref[half : half + small, where] = made[:small].astype(bf16)
                g_ref[2 * half + small :, where] = made[small:].astype(bf16)
        if first:
            g_ref.flush()
        g_all = g_ref[...]
        refs.grads[: 3 * width] = tn(g_all, refs.x[...]).astype(bf16)
        refs.grads.flush(0)
        refs.line[0:1] = jnp.sum(g_all.astype(f32), 0, keepdims=True)
        refs.line[1:] = jnp.zeros((7, 3 * width), f32)
        refs.line.flush()
        if not first:
            made = nn(g_all, refs.w_qkv[...]) + nn(refs.g_other[...], refs.w_other[...])
            if last:
                own = rows // 2
                made = made + jnp.concatenate([refs.g_norm[:own], jnp.zeros((own, model), f32)], 0)
                high = made.astype(bf16)
                rest = (made - high.astype(f32)).astype(bf16)
                core = facts(refs.meta, per)[0]
                place = row_places(refs.meta, per, half, small, 1)
                at = lax.broadcasted_iota(i32, (own, rows), 0)
                pick = (place == core * own + at).astype(bf16)
                refs.own[...] = nn(pick, high) + nn(pick, rest)
                refs.away[...] = nn((place == (1 - core) * own + at).astype(bf16), high).astype(bf16)
            else:
                for at, part in enumerate(chunks(rows)):
                    getattr(refs, f"mine{at}")[...] = made[part].astype(bf16)

    return run("attend_back", body, operands, results, scratch=scratch)


def halve(place, value, other):
    rows, width = value.shape[0] // 2, value.shape[1]
    kind = value.dtype
    if rows % 16:

        def take(which):
            return sum(
                lax.dynamic_slice_in_dim(part, which * rows, rows, 0).astype(f32) for part in (value, other)
            ).astype(kind)

        return take(place[0]), take(1 - place[0])

    def body(refs):
        place = refs.place[0]
        for out, which in ((refs.sent, 1 - place), (refs.kept, place)):
            part = pl.ds(pl.multiple_of(which * rows, 16), rows)
            out[...] = (refs.value[part].astype(f32) + refs.other[part].astype(f32)).astype(kind)

    made = (NEAR, (rows, width), kind)
    got = run(
        "halve",
        body,
        dict(place=(SCALAR, place), value=(NEAR, value), other=(NEAR, other)),
        dict(kept=made, sent=made),
    )
    return got.kept, got.sent


def join(place, mine, other):
    rows, width = mine.shape
    if rows % 16:
        return jnp.where(place[0] == 1, jnp.concatenate([other, mine], 0), jnp.concatenate([mine, other], 0))

    def body(refs):
        place = refs.place[0]
        refs.out[pl.ds(pl.multiple_of(place * rows, 16), rows)] = refs.mine[...]
        refs.out[pl.ds(pl.multiple_of((1 - place) * rows, 16), rows)] = refs.other[...]

    return run(
        "join",
        body,
        dict(place=(SCALAR, place), mine=(NEAR, mine), other=(NEAR, other)),
        dict(out=(NEAR, (2 * rows, width), mine.dtype)),
    ).out


def slices(meta, weights, strips, strip_rows):
    given = [*weights, *strips]
    model = given[-1][0].shape[2]

    def body(meta_ref, *refs):
        sems, outs = refs[-1], refs[len(given) : -1]
        copies = []
        for at, (_, layer) in enumerate(given):
            if at < len(weights):
                copies.append((refs[at].at[layer], outs[at]))
            else:
                rows = pl.ds(pl.multiple_of(meta_ref[0] * strip_rows, 16), strip_rows)
                part = pl.ds((at - len(weights)) * strip_rows, strip_rows)
                copies.append((refs[at].at[layer, rows], outs[-1].at[part]))
        copies = [pltpu.make_async_copy(*pair, sems.at[at]) for at, pair in enumerate(copies)]
        for copy in copies:
            copy.start()
        for copy in copies:
            copy.wait()

    made = [pltpu.VMEM(array.shape[1:], array.dtype) for array, _ in weights]
    made += [pltpu.VMEM((len(strips) * strip_rows, model), bf16)] if strips else []
    return pl.pallas_call(
        body,
        out_shape=tuple(made),
        in_specs=[SMEM] + [HBM] * len(given),
        out_specs=(VMEM,) * len(made),
        scratch_shapes=[pltpu.SemaphoreType.DMA((len(given),))],
        cost_estimate=pl.CostEstimate(flops=COST, transcendentals=0, bytes_accessed=0),
        name="slices",
    )(meta, *[pltpu.with_memory_space_constraint(array, pltpu.HBM) for array, _ in given])


def gather_small(meta, per, b_out, b_down, ln_gain, ln_shift, b_up, b_qv, queries):
    layers, units = b_up.shape
    model = b_out.shape[1]
    width = b_qv.shape[2]
    q_group, q_piece, dim = queries.shape
    q_rows = q_group * q_piece

    def body(meta, bo_ref, bd_ref, gain_ref, shift_ref, bu_ref, bqv_ref, q_ref, vec_out, line_out, carried_out):
        vec_out[...] = jnp.zeros(vec_out.shape, f32)
        line_out[...] = jnp.zeros(line_out.shape, f32)
        for layer in range(layers):
            for at, ref in ((0, bo_ref), (1, bd_ref)):
                first = 8 * (2 * layer + at)
                vec_out[first : first + 1] = ref[layer : layer + 1]
                vec_out[first + 1 : first + 2] = gain_ref[layer, at : at + 1]
                vec_out[first + 2 : first + 3] = shift_ref[layer, at : at + 1]
                line_out[2 * layer + 1 : 2 * layer + 2, at * width : (at + 1) * width] = bqv_ref[
                    layer, at : at + 1
                ]
            line_out[2 * layer : 2 * layer + 1] = bu_ref[layer : layer + 1].astype(f32)
        for at in range(q_group):
            carried_out[at * q_piece : (at + 1) * q_piece] = q_ref[at]
        lane = lax.broadcasted_iota(i32, (CARRIED - q_rows, dim), 1)
        row = lax.broadcasted_iota(i32, (CARRIED - q_rows, dim), 0)
        made = jnp.zeros((CARRIED - q_rows, dim), f32)
        for at in range(2 * per):
            made = jnp.where((lane == at) & (row == 0), meta[2 + 2 * per + at].astype(f32), made)
        carried_out[q_rows:] = made.astype(bf16)

    return pl.pallas_call(
        body,
        out_shape=(
            jax.ShapeDtypeStruct((16 * layers, model), f32),
            jax.ShapeDtypeStruct((-(-2 * layers // 8) * 8, units), f32),
            jax.ShapeDtypeStruct((CARRIED, dim), bf16),
        ),
        in_specs=[SMEM] + [VMEM] * 7,
        out_specs=(VMEM,) * 3,
        cost_estimate=pl.CostEstimate(flops=COST, transcendentals=0, bytes_accessed=0),
        name="gather_small",
    )(meta, b_out, b_down, ln_gain, ln_shift, b_up, b_qv, queries)


def turn(meta, per, small, x_own, x_other):
    own, model = x_own.shape
    rows = 2 * own

    def body(refs):
        core = facts(refs.meta, per)[0]
        place = row_places(refs.meta, per, own - small, small, 0)
        at = lax.broadcasted_iota(i32, (rows, own), 1)
        made = nn((place == core * own + at).astype(bf16), refs.mine[...])
        made = made + nn((place == (1 - core) * own + at).astype(bf16), refs.came[...])
        made = made.astype(bf16)
        refs.near[...] = made
        refs.low[...] = made
        refs.low.flush()

    operands = dict(meta=(SCALAR, meta), mine=(NEAR, x_own), came=(NEAR, x_other))
    results = dict(near=(NEAR, (rows, model), bf16), low=(FAR, (rows, model), bf16))
    return run("turn", body, operands, results)


CARRIED = 32


def query_of(at, q_group, q_piece):
    return at // q_piece % q_group


def score(meta, per, small, norm, w_proj, carried, q_group, q_piece, n_mp):
    rows, model = norm.base.shape
    half = rows // 2 - small
    dim = w_proj.shape[1]
    q_rows = q_group * q_piece
    q_tok = q_rows * n_mp
    count = per * q_tok
    n_dp = carried.shape[0] // (n_mp * CARRIED)

    def body(refs):
        norm_into(refs, norm.line)
        groups = facts(refs.meta, per)[4]
        for at in range(per):
            for piece in range(n_mp):
                side = piece % 2 * 2 + piece // 2
                source = pl.multiple_of((side * n_dp + groups[at]) * CARRIED, CARRIED)
                first = at * q_tok + piece * q_rows
                refs.flat_q[first : first + q_rows] = refs.carried[pl.ds(source, q_rows)]
        emb = nn(refs.low[...], refs.w_proj[...])
        unit = emb * lax.rsqrt(jnp.sum(emb * emb, -1, keepdims=True) + UNIT_EPS)
        segment = row_segments(refs.meta, per, half, small)
        owner = lax.broadcasted_iota(i32, (rows, count), 1) // q_tok == segment
        similar = nt(unit.astype(bf16), refs.flat_q[...])
        terms = jnp.where(owner, jnp.exp(SHARP * (similar - 1.0)), 0.0)
        totals = jnp.sum(terms, 0, keepdims=True)
        refs.totals[...] = jnp.broadcast_to(totals, (8, count))
        _, micro, _, _, _ = facts(refs.meta, per)
        slot = (refs.meta[0] * 2 + micro) * per
        lane = lax.broadcasted_iota(i32, (8, count), 1)
        length = jnp.zeros((8, count), f32)
        for at in range(per):
            size = jnp.full((8, count), refs.meta[2 + micro * per + at].astype(f32))
            length = jnp.where(lane // q_tok == at, size, length)
        term = (jnp.log(jnp.broadcast_to(totals, (8, count))) - jnp.log(length)) / SHARP + 1.0
        row = lax.broadcasted_iota(i32, (8, count), 0)
        term = jnp.where(query_of(lane, q_group, q_piece) == row, term, 0.0)
        n_pass = refs.logits.shape[1]
        target = lax.broadcasted_iota(i32, (count, n_pass), 1)
        source = lax.broadcasted_iota(i32, (count, n_pass), 0)
        pick = (source // q_tok + slot == target).astype(f32)
        refs.logits[...] = exact(term, pick) / TEMPER

    n_pass = carried.shape[0] // (n_mp * CARRIED) * 2 * per
    operands = dict(meta=(SCALAR, meta)) | parts_in(norm)
    operands |= dict(
        base=(FAR, norm.base),
        vecs=(FAR, norm.vecs),
        carried=(NEAR, carried),
        w_proj=(FAR, w_proj),
    )
    results = norm_results(rows, model, keep=False) | dict(
        flat_q=(NEAR, (count, dim), bf16),
        totals=(NEAR, (8, count), f32),
        logits=(NEAR, (8, n_pass), f32),
    )
    return run("score", body, operands, results)


def loss_back(meta, per, small, logits, groups, targets, totals, flat_q, final, w_proj, q_group, q_piece, n_mp):
    n_dp, n_pass = targets.shape[1], logits.shape[1]
    rows, model = final.shape
    half = rows // 2 - small
    dim = w_proj.shape[1]
    q_rows = q_group * q_piece
    q_tok = q_rows * n_mp
    count = per * q_tok
    held = n_dp * q_rows * (n_mp // 2)

    def body(refs):
        meta = refs.meta
        core, micro, _, _, own_groups = facts(meta, per)
        member = refs.groups[...] == lax.broadcasted_iota(i32, (n_dp, n_pass), 0)
        lane = lax.broadcasted_iota(i32, (n_dp, n_pass), 1)
        g_rows = []
        for query in range(q_group):
            logit = refs.logits[query : query + 1]
            spread = jnp.where(member, logit, FLOOR)
            top = jnp.max(spread, 1, keepdims=True)
            mass = jnp.sum(jnp.where(member, jnp.exp(spread - top), 0.0), 1, keepdims=True)
            lse = top + jnp.log(mass)
            hit = lane == refs.targets[query]
            refs.loss[query] = lse - jnp.sum(jnp.where(hit, logit, 0.0), 1, keepdims=True)
            lse_pass = jnp.sum(jnp.where(member, lse, 0.0), 0, keepdims=True)
            hits = jnp.sum(jnp.where(hit & member, 1.0, 0.0), 0, keepdims=True)
            g_rows.append(jnp.exp(logit - lse_pass) - hits)
        g_logit = jnp.concatenate(g_rows + [jnp.zeros((8 - q_group, n_pass), f32)], 0)
        slot = (meta[0] * 2 + micro) * per
        lane = lax.broadcasted_iota(i32, (n_pass, count), 0)
        at = lax.broadcasted_iota(i32, (n_pass, count), 1)
        wide = exact(g_logit, (at // q_tok + slot == lane).astype(f32))
        at = lax.broadcasted_iota(i32, (8, count), 1)
        row = lax.broadcasted_iota(i32, (8, count), 0)
        wide = jnp.where(query_of(at, q_group, q_piece) == row, wide, 0.0)
        wide = jnp.sum(wide, 0, keepdims=True)
        g_total = (wide / TEMPER) / (SHARP * refs.totals[0:1])
        low = refs.final[...]
        emb = nn(low, refs.w_proj[...])
        scale = lax.rsqrt(jnp.sum(emb * emb, -1, keepdims=True) + UNIT_EPS)
        unit = emb * scale
        unit_low = unit.astype(bf16)
        segment = row_segments(meta, per, half, small)
        owner = lax.broadcasted_iota(i32, (rows, count), 1) // q_tok == segment
        similar = nt(unit_low, refs.flat_q[...])
        terms = jnp.where(owner, jnp.exp(SHARP * (similar - 1.0)), 0.0)
        g_sim = (SHARP * terms * g_total).astype(bf16)
        g_unit = nn(g_sim, refs.flat_q[...])
        g_emb = scale * (g_unit - unit * jnp.sum(g_unit * unit, -1, keepdims=True))
        g_emb = g_emb.astype(bf16)
        refs.grad[...] = nt(g_emb, refs.w_proj[...])
        refs.proj[...] = tn(g_emb, low).astype(bf16)
        g_picked = tn(g_sim, unit_low)
        row = lax.broadcasted_iota(i32, (held, count), 0)
        source = lax.broadcasted_iota(i32, (held, count), 1)
        group = row // q_rows % n_dp
        piece = row // (q_rows * n_dp) * 2 + core
        want = piece * q_rows + row % q_rows
        line = lax.broadcasted_iota(i32, (1, count), 1) // q_tok
        source_group = jnp.zeros((1, count), i32)
        for passage in range(per):
            source_group = jnp.where(line == passage, own_groups[passage], source_group)
        pick = ((source % q_tok == want) & (source_group == group)).astype(f32)
        refs.queries[...] = exact(pick, g_picked)

    operands = dict(
        meta=(SCALAR, meta),
        logits=(NEAR, logits),
        groups=(NEAR, groups),
        targets=(NEAR, targets),
        totals=(NEAR, totals),
        flat_q=(NEAR, flat_q),
        final=(FAR, final),
        w_proj=(FAR, w_proj),
    )
    results = dict(
        loss=(NEAR, (q_group, n_dp, 1), f32),
        queries=(NEAR, (held, dim), f32),
        proj=(NEAR, (dim, model), bf16),
        grad=(NEAR, (rows, model), f32),
    )
    return run("loss_back", body, operands, results)


def pack(meta, sums, own, par):
    model = sums[0].shape[1]
    first = 8 * len(sums)
    rows = first + -(-2 * len(own) // 8) * 8
    operands = dict(meta=(SCALAR, meta)) | {f"sum{at}": (FAR, value) for at, value in enumerate(sums)}
    for layer, pairs in enumerate(zip(own, par)):
        for side, pair in enumerate(pairs):
            for at, value in enumerate(pair):
                operands[f"line{layer}{side}{at}"] = (FAR, value)

    def body(refs):
        for side, out in enumerate((refs.own, refs.par)):
            out[first:] = jnp.zeros((rows - first, model), f32)
            for at in range(len(sums)):
                out[8 * at : 8 * at + 8] = getattr(refs, f"sum{at}")[...]
            for layer in range(len(own)):
                for at in range(2):
                    value = getattr(refs, f"line{layer}{side}{at}")
                    row = first + 2 * layer + at
                    out[row : row + 1, : value.held.shape[1]] = value[0:1]

    made = (NEAR, (rows, model), f32)
    got = run("pack", body, operands, dict(own=made, par=made))
    return got.own, got.par


def quarters(place, value, other):
    rows, width = value.shape[0] // 4, value.shape[1]

    def body(refs):
        for at in (1, 2, 3, 0):
            part = pl.ds(pl.multiple_of((refs.place[0] ^ at) * rows, 16), rows)
            made = refs.value[part].astype(f32) + refs.other[part].astype(f32)
            getattr(refs, f"part{at}")[...] = made.astype(value.dtype)

    operands = dict(place=(SCALAR, place), value=(NEAR, value), other=(NEAR, other))
    results = {f"part{at}": (NEAR, (rows, width), value.dtype) for at in range(4)}
    got = run("quarters", body, operands, results)
    return [getattr(got, f"part{at}") for at in range(4)]


def join_quarters(place, *parts):
    rows, width = parts[0].shape

    def body(refs):
        for at in range(4):
            part = pl.ds(pl.multiple_of((refs.place[0] ^ at) * rows, 16), rows)
            refs.out[part] = getattr(refs, f"part{at}")[...]

    operands = dict(place=(SCALAR, place)) | {f"part{at}": (NEAR, part) for at, part in enumerate(parts)}
    return run("join", body, operands, dict(out=(NEAR, (4 * rows, width), parts[0].dtype))).out


def add(*parts):
    def body(refs):
        total = sum(getattr(refs, f"part{at}")[...].astype(f32) for at in range(len(parts)))
        refs.out[...] = total.astype(parts[0].dtype)

    operands = {f"part{at}": (NEAR, part) for at, part in enumerate(parts)}
    return run("add", body, operands, dict(out=(NEAR, parts[0].shape, parts[0].dtype))).out


def on_device(
    passages_in,
    queries,
    w_qkv,
    b_qv,
    w_out,
    b_out,
    ln_gain,
    ln_shift,
    w_up,
    b_up,
    w_down,
    b_down,
    w_proj,
    lengths,
    passage_group,
    positive,
):
    n_mp = lax.axis_size("mp")
    n_dp = lax.axis_size("dp")
    own, model = passages_in.shape
    micro_count, per = lengths.shape
    tok_mb = own * n_mp // micro_count
    assert n_mp == 4 and micro_count == 2 and n_dp & (n_dp - 1) == 0
    layers = w_qkv.shape[0]
    width = w_qkv.shape[3]
    ff = w_up.shape[2]
    small = (tok_mb - LONGEST) // 2
    q_group, q_piece, dim = queries.shape
    q_rows = q_group * q_piece

    mp_here = lax.axis_index("mp")
    dp_here = lax.axis_index("dp")
    core, micro = mp_here % 2, mp_here // 2
    dp_bits = [1 << at for at in range(n_dp.bit_length() - 1)]

    def to_pair(value):
        return jax.tree.map(lambda part: lax.ppermute(part, "mp", [(at, at ^ 1) for at in range(n_mp)]), value)

    def to_x(value):
        return lax.ppermute(value, "mp", [(at, at ^ 2) for at in range(n_mp)])

    def to_dp(value, bit):
        return lax.ppermute(value, "dp", [(at, at ^ bit) for at in range(n_dp)])

    noted = []

    def here(value):
        return lax.optimization_barrier((value, noted[-1]))[0] if noted else value

    def note(value):
        noted.append(value)
        return value

    meta = jnp.concatenate(
        [jnp.stack([dp_here, mp_here]).astype(i32), lengths.reshape(-1), passage_group.reshape(-1)]
    )
    core_place, micro_place = core[None].astype(i32), micro[None].astype(i32)
    places = {bit: ((dp_here // bit) % 2)[None].astype(i32) for bit in dp_bits}

    w_qkv = w_qkv.transpose(0, 2, 3, 1).reshape(layers, 3 * width, model)
    x_other = to_pair(passages_in)
    strip_rows = model // n_dp

    def strips_of(meta, pairs):
        if strip_rows % 16 == 0:
            return slices(meta, [], pairs, strip_rows)[0]
        parts = [
            lax.dynamic_slice_in_dim(array[layer], dp_here * strip_rows, strip_rows, 0) for array, layer in pairs
        ]
        return jnp.concatenate(parts, 0)

    def gathered(strip):
        count = strip.shape[0] // strip_rows
        stack = lax.all_gather(strip, "dp", axis=0)
        if strip_rows % 16:
            parts = [stack[:, at * strip_rows : (at + 1) * strip_rows] for at in range(count)]
            return [(FAR, part.reshape(-1, model)) for part in parts]
        return [
            (FAR, stack, (slice(None), slice(at * strip_rows, (at + 1) * strip_rows))) for at in range(count)
        ]

    def after(value, first):
        return lax.optimization_barrier((value, first))[0]

    strip = strips_of(meta, [(w_up, 0)])
    strip_par = to_x(strip)
    vecs, lines, first_carried = gather_small(
        after(meta, strip), per, b_out, b_down, ln_gain, ln_shift, b_up, b_qv, queries
    )
    sent = slices(after(meta, lines), [(w_qkv, 0), (w_out, 0), (w_down, 0)], [], strip_rows)
    strip_par = after(strip_par, sent[0])
    w_par = [SimpleNamespace() for _ in range(layers)]
    (w_par[0].up,) = gathered(strip_par)
    w_par[0].qkv, w_par[0].out = (to_x(after(value, strip_par)) for value in sent[:2])
    lines_par = to_x(after(lines, strip_par))
    turned = turn(after(meta, sent[0]), per, small, passages_in, x_other)
    strips_par = [
        to_x(strips_of(after(meta, turned.low), [(w_up, layer), (w_down, layer)])) for layer in range(1, layers)
    ]

    def spread():
        value = first_carried
        steps = [((lambda v, bit=bit: to_dp(v, bit)), places[bit]) for bit in dp_bits]
        steps += [(to_x, micro_place), (to_pair, core_place)]
        for send, place in steps:
            other = send(value)
            yield
            value = note(join(here(place), value, other))
        yield value

    spreading, spread_out = spread(), []

    def spread_on():
        spread_out.append(next(spreading, None))

    spread_on()

    x_all, base, norm = turned.low, turned.low, None
    stored = []
    for layer in range(layers):
        par = w_par[layer]
        att_own = attend_first(
            here(meta), per, small, 2 * layer + 1, turned.near if norm is None else None, norm, w_qkv, layer, lines
        )
        note(att_own.lse)
        if layer == 0:
            spread_on()
        if norm is not None:
            x_all, base = att_own.low, att_own.y
        att_par = attend_second(
            here(meta), per, small, 2 * layer + 1, x_all, par.qkv, lines_par, att_own.a, w_out, layer, par.out
        )
        note(att_par.lse)
        if layer == 0:
            strips_par = [here(strip) for strip in strips_par]
            w_par[0].down = (FAR, to_x(after(sent[2], strips_par[0])))
            for at in range(1, layers):
                w_par[at].up, w_par[at].down = gathered(strips_par[at - 1])
        norm = SimpleNamespace(
            mine=parts_of(att_par), came=to_pair(parts_of(att_par)), base=base, vecs=vecs, line=2 * layer
        )
        spread_on()
        ffn_own = ffn_first(here(meta), 2 * layer, norm, w_up, layer, lines)
        note(ffn_own.r)
        if layer != 0:
            spread_on()
        if layer + 1 < layers:
            at = layer + 1
            pieces = slices(here(meta), [(w_qkv, at), (w_out, at)], [], strip_rows)
            w_par[at].qkv, w_par[at].out = (to_x(value) for value in pieces)
        ffn_par = ffn_second(
            here(meta), 2 * layer, ffn_own.low, par.up, lines_par, ffn_own.hidden, w_down, layer, par.down
        )
        note(ffn_par.mine0)
        norm = SimpleNamespace(
            mine=parts_of(ffn_par),
            came=to_pair(parts_of(ffn_par)),
            base=ffn_own.y,
            vecs=vecs,
            line=2 * layer + 1,
        )
        if layer == 0:
            spread_on()
        stored.append([x_all, att_own, att_par, ffn_own, ffn_par])
    spread_out += list(spreading)
    carried = next(value for value in spread_out if value is not None)
    groups = carried.reshape(n_mp, n_dp, CARRIED, dim)[0, :, q_rows, : passage_group.size]
    groups = groups.reshape(1, -1).astype(i32)

    found = score(here(meta), per, small, norm, w_proj, carried, q_group, q_piece, n_mp)
    norms_after = [stored[layer][1] for layer in range(1, layers)] + [found]
    logits = found.logits
    logits = logits + to_x(logits)
    for bit in dp_bits:
        logits = logits + to_dp(logits, bit)
    back = loss_back(
        meta,
        per,
        small,
        logits,
        groups,
        positive.reshape(n_dp, q_group).T[:, :, None],
        found.totals,
        found.flat_q,
        found.low,
        w_proj,
        q_group,
        q_piece,
        n_mp,
    )
    note(back.grad)
    query_loss = lax.dynamic_index_in_dim(back.loss[:, :, 0], dp_here, 1, keepdims=False)

    def total(theirs):
        other = to_x(here(theirs))
        value = yield
        yield
        for bit in dp_bits:
            value, sent = halve(here(places[bit]), value, other)
            note(value)
            other = to_dp(sent, bit)
            yield
        value = note(add(here(value), other))
        for bit in reversed(dp_bits):
            other = to_dp(value, bit)
            yield
            value = note(join(here(places[bit]), value, other))
        yield value

    def total_early(theirs):
        other = to_x(here(theirs))
        value = yield
        yield
        value, sent = halve(here(places[1]), value, other)
        note(value)
        other = to_dp(sent, 1)
        yield
        value = note(add(here(value), other))
        value = lax.psum(value, "dp", axis_index_groups=[list(range(side, n_dp, 2)) for side in range(2)])
        yield
        value = here(value)
        other = to_dp(value, 1)
        yield
        yield note(join(here(places[1]), value, other))

    def query_sums():
        value = back.queries
        rows = value.shape[0] // 2
        other = to_x(lax.dynamic_slice_in_dim(value, (1 - micro) * rows, rows, 0))
        value = lax.dynamic_slice_in_dim(value, micro * rows, rows, 0)
        for bit in reversed(dp_bits):
            yield
            value, sent = halve(here(places[bit]), value, other)
            note(value)
            other = to_dp(sent, bit)
        yield
        yield value + other

    queried = query_sums()
    next(queried)
    running = []

    def advance(which, count=1):
        for _ in range(count):
            got = next(running[which])
        return got

    finals = [None] * (2 * layers)
    rep_sums, own_sums, par_sums = [None] * (2 * layers), [None] * layers, [None] * layers
    grads = dict(grad=(NEAR, back.grad))
    for layer in reversed(range(layers)):
        x_all, att_own, att_par, ffn_own, ffn_par = stored[layer]
        par = w_par[layer]
        last = layer == layers - 1
        extra = back.proj if last else None

        def way(line, kept):
            rest = dict(n=(FAR, kept.n), r=(FAR, kept.r), vecs=(FAR, vecs))
            return SimpleNamespace(operands=grads | rest, line=line)

        got_par = ffn_back(
            here(meta),
            way(2 * layer + 1, norms_after[layer]),
            ffn_par,
            ffn_own.low,
            par.up,
            par.down,
            extra,
            None,
        )
        note(got_par.line)
        if last:
            next(queried)
        else:
            advance(1)
        running.append((total_early if last else total)(got_par.grads))
        advance(-1)
        other = SimpleNamespace(low=got_par.low, pre=got_par.pre, w_up=par.up)
        got_own = ffn_back(
            here(meta), None, ffn_own, ffn_own.low, (FAR, w_up, layer), (FAR, w_down, layer), extra, other
        )
        note(got_own.line)
        running[-1].send(got_own.grads)
        rep_sums[2 * layer + 1] = got_par.sums
        bup = (got_own.line, got_par.line)
        exchanged = SimpleNamespace(mine=parts_of(got_own), came=to_pair(parts_of(got_own)))
        grads = parts_in(exchanged) | dict(base=(FAR, got_par.g))
        if last:
            next(queried)
        else:
            advance(0)
        got_par = attend_back(
            here(meta),
            per,
            small,
            way(2 * layer, ffn_own),
            att_par,
            x_all,
            (FAR, par.qkv),
            (FAR, par.out),
            None,
            False,
        )
        note(got_par.line)
        if not last:
            advance(2)
            advance(1)
        running.append(total(got_par.grads))
        advance(-1)
        if last:
            next(queried)
        other = SimpleNamespace(low=got_par.low, g_qkv=got_par.g_qkv, w_qkv=par.qkv, g=got_par.g)
        got_own = attend_back(
            here(meta), per, small, None, att_own, x_all, (FAR, w_qkv, layer), (FAR, w_out, layer), other, layer == 0
        )
        note(got_own.line)
        running[-1].send(got_own.grads)
        rep_sums[2 * layer] = got_par.sums
        own_sums[layer] = (bup[0], got_own.line)
        par_sums[layer] = (bup[1], got_par.line)
        if layer:
            exchanged = SimpleNamespace(mine=parts_of(got_own), came=to_pair(parts_of(got_own)))
            grads = parts_in(exchanged) | dict(base=(FAR, got_par.g))
        if last:
            advance(0)
            query_grad = [value for value in queried if value is not None][0].reshape(q_group, q_piece, dim)
    input_grad = got_own.own + to_pair(got_own.away).astype(f32)

    count = 2 * layers * 8
    flat, flat_par = pack(here(meta), rep_sums, own_sums, par_sums)
    flat_other = to_x(flat_par)

    def flat_sums():
        value, other = flat, flat_other
        for bit in dp_bits:
            yield
            value = note(add(here(value), other))
            other = to_dp(value, bit)
        yield
        yield note(add(here(value), other))

    running.append(flat_sums())
    advance(-1)
    finals = [None] * len(running)
    turns = TURNS if n_dp == 8 and layers == 2 else []
    for which in turns:
        finals[which] = advance(which)
    for which in range(len(running)):
        for got in running[which]:
            finals[which] = got
    flat = finals.pop()
    lists = [[], [], [], []]
    for layer in range(layers):
        summed = finals[2 * (layers - 1 - layer)]
        lists[3].append(summed[:ff])
        lists[2].append(summed[ff : ff + model])
        if layer == layers - 1:
            g_wproj = summed[ff + model :].astype(f32).T
        summed = finals[2 * (layers - 1 - layer) + 1]
        lists[0].append(summed[: 3 * width])
        lists[1].append(summed[3 * width :])
    norms = flat[:count].reshape(layers, 2, 8, model)
    units = flat[count : count + 2 * layers].reshape(layers, 2, model)
    g_bqv = jnp.stack([units[:, 1, :width], units[:, 1, 2 * width : 3 * width]], 1)
    g_wqkv, g_wout, g_wup, g_wdown = (
        jnp.stack([value.astype(f32) for value in values]) for values in lists
    )
    g_wqkv = g_wqkv.reshape(layers, 3, width, model).transpose(0, 3, 1, 2)
    return (
        query_loss,
        input_grad,
        query_grad,
        g_wqkv,
        g_bqv,
        g_wout,
        norms[:, 0, 2],
        norms[:, :, 0],
        norms[:, :, 1],
        g_wup,
        units[:, 0],
        g_wdown,
        norms[:, 1, 2],
        g_wproj,
    )


def solution(mesh):
    placed = (
        P(("dp", "mp"), None),
        P("dp", "mp", None),
        P(None, None, None, "mp"),
        P(None, None, "mp"),
        P(None, "mp", None),
        P(),
        P(),
        P(),
        P(None, None, "mp"),
        P(None, "mp"),
        P(None, "mp", None),
        P(),
        P(),
        P("dp", None),
        P("dp", None),
        P(),
    )
    return jax.shard_map(
        on_device,
        mesh=mesh,
        in_specs=placed,
        out_specs=(
            P("dp"),
            P(("dp", "mp"), None),
            P("dp", "mp", None),
            P(None, None, None, "mp"),
            P(None, None, "mp"),
            P(None, "mp", None),
            P(),
            P(),
            P(),
            P(None, None, "mp"),
            P(None, "mp"),
            P(None, "mp", None),
            P(),
            P(),
        ),
        check_vma=False,
    )
```

time: 1880 us -> 582 us (0.31)
  waiting for transfers between devices: 1190 us -> 172 us
  matrix products: 303 us -> 0 us
  Pallas kernels: 0 us -> 283 us
  blocking collectives: 181 us -> 0 us
  other arithmetic: 129 us -> 11.9 us
  starting transfers between devices: 1.71 us -> 66.6 us
  local copies, waits for them, and re-layouts: 52.2 us -> 23.2 us
    psum x2 -> x1, waiting for transfers between devices: 484 us -> 0.02 us  [total_early(): lax.psum(value, 'dp', axis_index_groups=[list(range(side, n_dp, 2)) for s...]
    reduce_scatter x9 -> x0, waiting for transfers between devices: 461 us -> none  [the longest x4 204 us: collect_rows(): lax.psum_scatter(term_fn(jnp.int32(0), shard_rows * lax.axis_size('mp')),...]
    dot_general x55 -> x0, matrix products: 303 us -> none  [the longest x10 71.9 us: right_t(): lax.dot_general(left_side, right_side, (((1,), (1,)), ((), ())), preferre...]
    pallas_call x0 -> x61, Pallas kernels: none -> 283 us  [the longest x56 271 us: run(): pl.pallas_call(outer, out_shape=tuple((spaces[kind != NEAR](shape, dtype)...]
    all_gather x8 -> x2, waiting for transfers between devices: 241 us -> 0.02 us  [gathered(): stack = lax.all_gather(strip, 'dp', axis=0)]
    ppermute x0 -> x79, waiting for transfers between devices: none -> 172 us  [the longest x32 134 us: to_dp(): return lax.ppermute(value, 'dp', [(at, at ^ bit) for at in range(n_dp)])]
    all_gather x4 -> x0, blocking collectives: 96.7 us -> none  [the longest x3 55.4 us: joined(): pieces = jax.tree.map(lambda part: lax.all_gather(part, axis), value)]
    psum x3 -> x0, blocking collectives: 83.9 us -> none  [the longest x1 41.2 us: on_device(): lax.psum((jnp.stack(list_bout), jnp.stack(list_gain), jnp.stack(list_shif...]
  transfers between devices with their start and end apart: 19 -> 82, of which waited for: 18 -> 39; matrix products, arithmetic and copies ran while one was open for 3% -> 2% of each run, Pallas kernels for 0% -> 45%
where the time goes in v1:
time: 582 us; the launch traced here: 572 us
  Pallas kernels  283 us (49%)
  waiting for transfers between devices  172 us (30%)
  starting transfers between devices  66.6 us (11%)
  local copies, waits for them, and re-layouts  23.2 us (4%)
  between operations  15.5 us (3%)
  other arithmetic  11.9 us (2%)
    pallas_call x56, Pallas kernels, run(): pl.pallas_call(outer, out_shape=tuple((spaces[kind != NEAR](shape, dtype)...  271 us
    ppermute x32, waiting for transfers between devices, to_dp(): return lax.ppermute(value, 'dp', [(at, at ^ bit) for at in range(n_dp)])  134 us
    ppermute x32, starting transfers between devices, to_dp(): return lax.ppermute(value, 'dp', [(at, at ^ bit) for at in range(n_dp)])  41.6 us
    ppermute x16, waiting for transfers between devices, to_x(): return lax.ppermute(value, 'mp', [(at, at ^ 2) for at in range(n_mp)])  27.7 us
    ppermute x16, starting transfers between devices, to_x(): return lax.ppermute(value, 'mp', [(at, at ^ 2) for at in range(n_mp)])  18.9 us
    unnamed x86, local copies, waits for them, and re-layouts  16.3 us
  transfers between devices with their start and end apart: 82, of which 39 were waited for; matrix products, arithmetic and copies ran while one was open for 2% of the time, Pallas kernels for 45%

profile of v1, /device:TPU:0, one launch (start us, length us, event | category | flops | bytes accessed | tf_op | source)
XLA Modules:
  0.0 571.6 jit_solution(16893732336269405374)
XLA Ops:
  23.1 4.7 turn.1
  33.4 9.6 %attend.4 = (bf16[1152,192]{1,0:T(8,128)(2,1)}, bf16[1152,192]{1,0:T(8,128)(2,1)}, bf16[1152,192]{1,0:T(8,128)(2,1)}, bf16[1152,192]{1,0:T(8,128)(2,1)}, f32[8,1152]{1,0:T(8,128)}) custom-call(s32[34]{0:T(128)S(1)} %copy-done.13, bf16[1152,768]{1,0:T(8,128)(2,1)S(1)} %get-tuple-element.237.refs_1_, bf16[2,576,768]{2,1,0:T(8,128)(2,1)} %bitcast.55, ...), custom_call_target="tpu_custom_call" | custom-call | flops 5000000 | tf_op jit(solution)/shard_map/attend/pallas_call | solution.py:162
  43.0 13.2 %collective-permute-done.4.refs_3_ = f32[8,768]{1,0:T(8,128)S(1)} collective-permute-done((f32[8,768]{1,0:T(8,128)S(1)}, f32[8,768]{1,0:T(8,128)S(1)}, u32[]{:S(2)}, u32[]{:S(2)}) %collective-permute-start.4) | collective-permute-done | bytes 24608 | tf_op jit(solution)/shard_map/ppermute | solution.py:1046
  56.9 10.8 %attend.5 = (bf16[1152,192]{1,0:T(8,128)(2,1)}, bf16[1152,192]{1,0:T(8,128)(2,1)}, bf16[1152,192]{1,0:T(8,128)(2,1)}, bf16[1152,192]{1,0:T(8,128)(2,1)}, f32[8,1...) custom-call(s32[34]{0:T(128)S(1)} %copy-done.13, ...), custom_call_target="tpu_custom_call" | custom-call | flops 5000000 | tf_op jit(solution)/shard_map/attend/pallas_call | solution.py:162
  75.0 9.4 %ffn.4 = (bf16[1152,768]{1,0:T(8,128)(2,1)}, bf16[1152,768]{1,0:T(8,128)(2,1)}, f32[1152,1]{1,0:T(8,128)}, f32[1152,768]{1,0:T(8,128)}, bf16[1152,768]{1,0:T(8,128)(2,1)}, /*index=5*/bf16[1152,768]{1,0:T(8,128)(2,1)}) custom-call(s32[34]{0:T(128)S(1)} %copy-done.13, bf16[288,768]{1,0:T(8,128)(2,1)S(1)} %get-tuple-element.252.refs_1_, ...), custom_call_target="tpu_custom_call" | custom-call | flops 5000000 | tf_op jit(solution)/shard_map/ffn/pallas_call | solution.py:162
  89.3 8.5 %collective-permute-done.12.refs_6_.refs_13_ = bf16[768,768]{1,0:T(8,128)(2,1)} collective-permute-done((bf16[768,768]{1,0:T(8,128)(2,1)}, bf16[768,768]{1,0:T(8,128)(2,1)}, u32[]{:S(2)}, u32[]{:S(2)}) %collective-permute-start.12) | collective-permute-done | bytes 1179680 | tf_op jit(solution)/shard_map/ppermute | solution.py:1046
  97.8 9.8 %ffn.5 = (bf16[1152,768]{1,0:T(8,128)(2,1)}, bf16[1152,768]{1,0:T(8,128)(2,1)}, bf16[288,768]{1,0:T(8,128)(2,1)S(1)}, bf16[288,768]{1,0:T(8,128)(2,1)S(1)}, bf16...) custom-call(s32[34]{0:T(128)S(1)} %copy-done.14, bf16[1152,768]{1,0:T(8,128)(2,1)} %get-tuple-element.259.refs_1_.refs_16_.refs_5_, ...), custom_call_target="tpu_custom_call" | custom-call | flops 5000000 | tf_op jit(solution)/shard_map/ffn/pallas_call | solution.py:162
  116.9 12.3 %attend.6 = (bf16[1152,768]{1,0:T(8,128)(2,1)}, bf16[1152,768]{1,0:T(8,128)(2,1)}, f32[1152,1]{1,0:T(8,128)}, f32[1152,768]{1,0:T(8,128)}, bf16[1152,192]{1,0:T(...) custom-call(s32[34]{0:T(128)S(1)} %copy-done.14, ...), custom_call_target="tpu_custom_call" | custom-call | flops 5000000 | tf_op jit(solution)/shard_map/attend/pallas_call | solution.py:162
  129.3 10.7 %attend.7 = (bf16[1152,192]{1,0:T(8,128)(2,1)}, bf16[1152,192]{1,0:T(8,128)(2,1)}, bf16[1152,192]{1,0:T(8,128)(2,1)}, bf16[1152,192]{1,0:T(8,128)(2,1)}, f32[8,1...) custom-call(s32[34]{0:T(128)S(1)} %copy-done.14, ...), custom_call_target="tpu_custom_call" | custom-call | flops 5000000 | tf_op jit(solution)/shard_map/attend/pallas_call | solution.py:162
  146.8 10.2 %ffn.6 = (bf16[1152,768]{1,0:T(8,128)(2,1)}, bf16[1152,768]{1,0:T(8,128)(2,1)}, f32[1152,1]{1,0:T(8,128)}, f32[1152,768]{1,0:T(8,128)}, bf16[1152,768]{1,0:T(8,128)(2,1)}, /*index=5*/bf16[1152,768]{1,0:T(8,128)(2,1)}) custom-call(s32[34]{0:T(128)S(1)} %copy-done.14, bf16[288,768]{1,0:T(8,128)(2,1)S(1)} %get-tuple-element.281.refs_1_, ...), custom_call_target="tpu_custom_call" | custom-call | flops 5000000 | tf_op jit(solution)/shard_map/ffn/pallas_call | solution.py:162
  158.6 10.0 %ffn.7 = (bf16[1152,768]{1,0:T(8,128)(2,1)}, bf16[1152,768]{1,0:T(8,128)(2,1)}, bf16[288,768]{1,0:T(8,128)(2,1)S(1)}, bf16[288,768]{1,0:T(8,128)(2,1)S(1)}, bf16...) custom-call(s32[34]{0:T(128)S(1)} %copy-done.14, bf16[1152,768]{1,0:T(8,128)(2,1)} %get-tuple-element.289.refs_1_.refs_8_.refs_5_, ...), custom_call_target="tpu_custom_call" | custom-call | flops 5000000 | tf_op jit(solution)/shard_map/ffn/pallas_call | solution.py:162
  172.4 6.8 %score.1 = (bf16[1152,768]{1,0:T(8,128)(2,1)}, bf16[1152,768]{1,0:T(8,128)(2,1)}, f32[1152,1]{1,0:T(8,128)}, bf16[512,128]{1,0:T(8,128)(2,1)S(1)}, f32[8,512]{1,0:T(8,128)S(1)}, /*index=5*/f32[8,128]{1,0:T(8,128)S(1)}) custom-call(s32[34]{0:T(128)S(1)} %copy-done.14, bf16[288,768]{1,0:T(8,128)(2,1)S(1)} %get-tuple-element.291.refs_1_, ...), custom_call_target="tpu_custom_call" | custom-call | flops 5000000 | tf_op jit(solution)/shard_map/score/pallas_call | solution.py:162
  195.2 6.9 %loss_back.1 = (f32[2,8,1]{2,1,0:T(8,128)S(1)}, f32[256,128]{1,0:T(8,128)S(1)}, bf16[128,768]{1,0:T(8,128)(2,1)S(1)}, f32[1152,768]{1,0:T(8,128)S(1)}) custom-call(s32[34]{0:T(128)S(1)} %copy-done.14, f32[8,128]{1,0:T(8,128)S(1)} %add.62.refs_1_, s32[1,128]{1,0:T(1,128)S(1)} %reshape.83.refs_2_, s32[2,8,1]{2,1,0:T(8,128)S(1)} %copy.41.refs_3_, ...), custom_call_target="tpu_custom_call" | custom-call | flops 5000000 | tf_op jit(solution)/shard_map/loss_back/pallas_call | solution.py:162
  204.6 11.8 %ffn_back.4 = (bf16[1664,768]{1,0:T(8,128)(2,1)}, f32[8,768]{1,0:T(8,128)}, f32[1152,768]{1,0:T(8,128)}, bf16[1152,768]{1,0:T(8,128)(2,1)}, f32[8,768]{1,0:T(8,128)}, /*index=5*/bf16[1152,768]{1,0:T(8,128)(2,1)}) custom-call(s32[34]{0:T(128)S(1)} %copy-done.14, f32[1152,768]{1,0:T(8,128)S(1)} %get-tuple-element.302.refs_1_, ...), custom_call_target="tpu_custom_call" | custom-call | flops 5000000 | tf_op jit(solution)/shard_map/ffn_back/pallas_call | solution.py:162
  219.7 12.4 %ffn_back.5 = (bf16[1664,768]{1,0:T(8,128)(2,1)}, f32[8,768]{1,0:T(8,128)}, bf16[288,768]{1,0:T(8,128)(2,1)S(1)}, bf16[288,768]{1,0:T(8,128)(2,1)S(1)}, bf16[288...) custom-call(s32[34]{0:T(128)S(1)} %copy-done.14, bf16[1152,768]{1,0:T(8,128)(2,1)} %get-tuple-element.314.refs_1_, ...), custom_call_target="tpu_custom_call" | custom-call | flops 5000000 | tf_op jit(solution)/shard_map/ffn_back/pallas_call | solution.py:162
  235.9 22.2 %attend_back.4 = (bf16[768,768]{1,0:T(8,128)(2,1)}, f32[8,576]{1,0:T(8,128)}, f32[1152,768]{1,0:T(8,128)}, bf16[1152,768]{1,0:T(8,128)(2,1)}, f32[8,768]{1,0:T(8,128)}, /*index=5*/bf16[1152,576]{1,0:T(8,128)(2,1)}) custom-call(s32[34]{0:T(128)S(1)} %copy-done.14, bf16[288,768]{1,0:T(8,128)(2,1)S(1)} %get-tuple-element.322.refs_1_, ...), custom_call_target="tpu_custom_call" | custom-call | flops 5000000 | tf_op jit(solution)/shard_map/attend_back/pallas_call | solution.py:162
  264.4 21.3 %attend_back.5 = (bf16[768,768]{1,0:T(8,128)(2,1)}, f32[8,576]{1,0:T(8,128)}, bf16[288,768]{1,0:T(8,128)(2,1)S(1)}, bf16[288,768]{1,0:T(8,128)(2,1)S(1)}, bf16[2...) custom-call(s32[34]{0:T(128)S(1)} %copy-done.14, bf16[1152,768]{1,0:T(8,128)(2,1)} %get-tuple-element.337.refs_1_, ...), custom_call_target="tpu_custom_call" | custom-call | flops 5000000 | tf_op jit(solution)/shard_map/attend_back/pallas_call | solution.py:162
  289.4 13.5 %ffn_back.6 = (bf16[1536,768]{1,0:T(8,128)(2,1)}, f32[8,768]{1,0:T(8,128)}, f32[1152,768]{1,0:T(8,128)}, bf16[1152,768]{1,0:T(8,128)(2,1)}, f32[8,768]{1,0:T(8,128)}, /*index=5*/bf16[1152,768]{1,0:T(8,128)(2,1)}) custom-call(s32[34]{0:T(128)S(1)} %copy-done.14, bf16[288,768]{1,0:T(8,128)(2,1)S(1)} %get-tuple-element.349.refs_1_, ...), custom_call_target="tpu_custom_call" | custom-call | flops 5000000 | tf_op jit(solution)/shard_map/ffn_back/pallas_call | solution.py:162
  306.1 13.5 %ffn_back.7 = (bf16[1536,768]{1,0:T(8,128)(2,1)}, f32[8,768]{1,0:T(8,128)}, bf16[288,768]{1,0:T(8,128)(2,1)S(1)}, bf16[288,768]{1,0:T(8,128)(2,1)S(1)}, bf16[288...) custom-call(s32[34]{0:T(128)S(1)} %copy-done.14, bf16[1152,768]{1,0:T(8,128)(2,1)} %get-tuple-element.365.refs_1_, ...), custom_call_target="tpu_custom_call" | custom-call | flops 5000000 | tf_op jit(solution)/shard_map/ffn_back/pallas_call | solution.py:162
  322.4 12.9 %collective-permute-done.47.refs_1_ = bf16[832,768]{1,0:T(8,128)(2,1)S(1)} collective-permute-done((bf16[832,768]{1,0:T(8,128)(2,1)S(1)}, bf16[832,768]{1,0:T(8,128)(2,1)S(1)}, u32[]{:S(2)}, u32[]{:S(2)}) %collective-permute-start.47) | collective-permute-done | bytes 1277984 | tf_op jit(solution)/shard_map/ppermute | solution.py:1049
  338.4 23.1 %attend_back.6 = (bf16[768,768]{1,0:T(8,128)(2,1)}, f32[8,576]{1,0:T(8,128)}, f32[1152,768]{1,0:T(8,128)}, bf16[1152,768]{1,0:T(8,128)(2,1)}, f32[8,768]{1,0:T(8,128)}, /*index=5*/bf16[1152,576]{1,0:T(8,128)(2,1)}) custom-call(s32[34]{0:T(128)S(1)} %copy-done.14, bf16[288,768]{1,0:T(8,128)(2,1)S(1)} %get-tuple-element.372.refs_1_, ...), custom_call_target="tpu_custom_call" | custom-call | flops 5000000 | tf_op jit(solution)/shard_map/attend_back/pallas_call | solution.py:162
  369.7 26.1 %attend_back.7 = (bf16[768,768]{1,0:T(8,128)(2,1)}, f32[8,576]{1,0:T(8,128)}, f32[576,768]{1,0:T(8,128)S(1)}, bf16[576,768]{1,0:T(8,128)(2,1)S(1)}) custom-call(s32[34]{0:T(128)S(1)} %copy-done.14, bf16[1152,768]{1,0:T(8,128)(2,1)} %get-tuple-element.392.refs_1_, bf16[2,192,768]{2,1,0:T(8,128)(2,1)} %refs_2_.9, ...), custom_call_target="tpu_custom_call" | custom-call | flops 5000000 | tf_op jit(solution)/shard_map/attend_back/pallas_call | solution.py:162
  400.7 32.0 %collective-permute-done.59.refs_1_ = bf16[96,768]{1,0:T(8,128)(2,1)S(1)} collective-permute-done((bf16[96,768]{1,0:T(8,128)(2,1)S(1)}, bf16[96,768]{1,0:T(8,128)(2,1)S(1)}, u32[]{:S(2)}, u32[]{:S(2)}) %collective-permute-start.59) | collective-permute-done | bytes 147488 | tf_op jit(solution)/shard_map/ppermute | solution.py:1049
  433.0 3.6 pack.1
  454.6 12.8 %collective-permute-done.66.refs_1_ = bf16[192,768]{1,0:T(8,128)(2,1)S(1)} collective-permute-done((bf16[192,768]{1,0:T(8,128)(2,1)}, bf16[192,768]{1,0:T(8,128)(2,1)S(1)}, u32[]{:S(2)}, u32[]{:S(2)}) %collective-permute-start.66) | collective-permute-done | bytes 294944 | tf_op jit(solution)/shard_map/ppermute | solution.py:1049
  468.5 9.8 %collective-permute-done.55 = f32[16,128]{1,0:T(8,128)S(1)} collective-permute-done((f32[16,128]{1,0:T(8,128)S(1)}, f32[16,128]{1,0:T(8,128)S(1)}, u32[]{:S(2)}, u32[]{:S(2)}) %collective-permute-start.55) | collective-permute-done | bytes 8224 | tf_op jit(solution)/shard_map/ppermute | solution.py:1049
  483.3 5.3 collective-permute-done.69.refs_1_
  495.3 8.3 %collective-permute-done.71.refs_2_ = bf16[96,768]{1,0:T(8,128)(2,1)S(1)} collective-permute-done((bf16[96,768]{1,0:T(8,128)(2,1)S(1)}, bf16[96,768]{1,0:T(8,128)(2,1)S(1)}, u32[]{:S(2)}, u32[]{:S(2)}) %collective-permute-start.71) | collective-permute-done | bytes 147488 | tf_op jit(solution)/shard_map/ppermute | solution.py:1049
  507.5 7.4 %collective-permute-done.75.refs_2_ = bf16[384,768]{1,0:T(8,128)(2,1)} collective-permute-done((bf16[384,768]{1,0:T(8,128)(2,1)}, bf16[384,768]{1,0:T(8,128)(2,1)}, u32[]{:S(2)}, u32[]{:S(2)}) %collective-permute-start.75) | collective-permute-done | bytes 589856 | tf_op jit(solution)/shard_map/ppermute | solution.py:1049
  526.8 19.8 %collective-permute-done.77.refs_2_ = bf16[768,768]{1,0:T(8,128)(2,1)} collective-permute-done((bf16[768,768]{1,0:T(8,128)(2,1)}, bf16[768,768]{1,0:T(8,128)(2,1)}, u32[]{:S(2)}, u32[]{:S(2)}) %collective-permute-start.77) | collective-permute-done | bytes 1179680 | tf_op jit(solution)/shard_map/ppermute | solution.py:1049
  548.3 7.0 %collective-permute-done.78.refs_2_ = bf16[384,768]{1,0:T(8,128)(2,1)} collective-permute-done((bf16[384,768]{1,0:T(8,128)(2,1)S(1)}, bf16[384,768]{1,0:T(8,128)(2,1)}, u32[]{:S(2)}, u32[]{:S(2)}) %collective-permute-start.78) | collective-permute-done | bytes 589856 | tf_op jit(solution)/shard_map/ppermute | solution.py:1049
  560.3 4.3 maximum_convert_fusion
  (320 shorter events, 166.2 us)
Async XLA Ops:
  7.2 82.1 %all-gather.5.cloned.1.call-start = ((), (), s32[]{:S(2)}) async-start(), calls=%async_computation.1 | async-start | bytes 1327104 | tf_op jit(solution)/shard_map/all_gather | solution.py:1080
  20.6 138.0 %all-gather.7.cloned.1.call-start = ((), (), s32[]{:S(2)}) async-start(), calls=%async_computation.2 | async-start | bytes 2654208 | tf_op jit(solution)/shard_map/all_gather | solution.py:1080
  20.7 35.5 %collective-permute-start.3 = (bf16[576,768]{1,0:T(8,128)(2,1)}, bf16[576,768]{1,0:T(8,128)(2,1)}, u32[]{:S(2)}, u32[]{:S(2)}) collective-permute-start(bf16[576,768]{1,0:T(8,128)(2,1)} %get-tuple-element.244), channel_id=1, source_target_pairs={{0,2},{1,3},{2,0},{3,1},{4,6},{5,7},{6,4},{7,5},{8,10},{9,11},{10,... | collective-permute-start | bytes 2654216 | tf_op jit(solution)/shard_map/ppermute | solution.py:1046
  20.8 35.4 %collective-permute-start.5 = (bf16[192,768]{1,0:T(8,128)(2,1)}, bf16[192,768]{1,0:T(8,128)(2,1)S(1)}, u32[]{:S(2)}, u32[]{:S(2)}) collective-permute-start(bf16[192,768]{1,0:T(8,128)(2,1)} %get-tuple-element.248), channel_id=1, source_target_pairs={{0,2},{1,3},{2,0},{3,1},{4,6},{5,7},{6,4},{7,5},{8,10},{9,11},{10,... | collective-permute-start | bytes 884744 | tf_op jit(solution)/shard_map/ppermute | solution.py:1046
  29.7 38.0 %collective-permute-start.11 = (bf16[192,768]{1,0:T(8,128)(2,1)S(1)}, bf16[192,768]{1,0:T(8,128)(2,1)S(1)}, u32[]{:S(2)}, u32[]{:S(2)}) collective-permute-start(bf16[192,768]{1,0:T(8,128)(2,1)S(1)} %slices.6), channel_id=1, source_target_pairs={{0,2},{1,3},{2,0},{3,1},{4,6},{5,7},{6,4},{7,5},{8,10},{9,11},{10,... | collective-permute-start | bytes 884744 | tf_op jit(solution)/shard_map/ppermute | solution.py:1046
  29.8 26.4 %collective-permute-start.4 = (f32[8,768]{1,0:T(8,128)S(1)}, f32[8,768]{1,0:T(8,128)S(1)}, u32[]{:S(2)}, u32[]{:S(2)}) collective-permute-start(f32[8,768]{1,0:T(8,128)S(1)} %copy-done.37), channel_id=1, source_target_pairs={{0,2},{1,3},{2,0},{3,1},{4,6},{5,7},{6,4},{7,5},{8,10},{9,11},{10,... | collective-permute-start | bytes 73736 | tf_op jit(solution)/shard_map/ppermute | solution.py:1046
  68.5 380.4 %all-reduce.2.cloned.1.call-start = ((), (), s32[]{:S(2)}) async-start(), calls=%async_computation | async-start | bytes 2555904 | tf_op jit(solution)/shard_map/psum | solution.py:1225
  68.5 29.3 %collective-permute-start.12 = (bf16[768,768]{1,0:T(8,128)(2,1)}, bf16[768,768]{1,0:T(8,128)(2,1)}, u32[]{:S(2)}, u32[]{:S(2)}) collective-permute-start(bf16[768,768]{1,0:T(8,128)(2,1)} %copy-done.30), channel_id=1, source_target_pairs={{0,2},{1,3},{2,0},{3,1},{4,6},{5,7},{6,4},{7,5},{8,10},{9,11},{10,... | collective-permute-start | bytes 3538952 | tf_op jit(solution)/shard_map/ppermute | solution.py:1046
  87.5 41.8 %collective-permute-start.18 = (bf16[576,768]{1,0:T(8,128)(2,1)}, bf16[576,768]{1,0:T(8,128)(2,1)}, u32[]{:S(2)}, u32[]{:S(2)}) collective-permute-start(bf16[576,768]{1,0:T(8,128)(2,1)} %get-tuple-element.275), channel_id=1, source_target_pairs={{0,2},{1,3},{2,0},{3,1},{4,6},{5,7},{6,4},{7,5},{8,10},{9,11},{10,... | collective-permute-start | bytes 2654216 | tf_op jit(solution)/shard_map/ppermute | solution.py:1046
  216.5 69.8 %collective-permute-start.41 = (bf16[1664,768]{1,0:T(8,128)(2,1)}, bf16[1664,768]{1,0:T(8,128)(2,1)S(1)}, u32[]{:S(2)}, u32[]{:S(2)}) collective-permute-start(bf16[1664,768]{1,0:T(8,128)(2,1)} %get-tuple-element.346), channel_id=1, source_target_pairs={{0,2},{1,3},{2,0},{3,1},{4,6},{5,7},{6,4},{7,5},{8,10},{9,11},{10,... | collective-permute-start | bytes 7667720 | tf_op jit(solution)/shard_map/ppermute | solution.py:1046
  258.1 44.8 %collective-permute-start.46 = (bf16[768,768]{1,0:T(8,128)(2,1)}, bf16[768,768]{1,0:T(8,128)(2,1)S(1)}, u32[]{:S(2)}, u32[]{:S(2)}) collective-permute-start(bf16[768,768]{1,0:T(8,128)(2,1)} %get-tuple-element.362), channel_id=1, source_target_pairs={{0,2},{1,3},{2,0},{3,1},{4,6},{5,7},{6,4},{7,5},{8,10},{9,11},{10,... | collective-permute-start | bytes 3538952 | tf_op jit(solution)/shard_map/ppermute | solution.py:1046
  304.0 57.6 %collective-permute-start.52 = (bf16[1536,768]{1,0:T(8,128)(2,1)}, bf16[1536,768]{1,0:T(8,128)(2,1)S(1)}, u32[]{:S(2)}, u32[]{:S(2)}) collective-permute-start(bf16[1536,768]{1,0:T(8,128)(2,1)} %get-tuple-element.386), channel_id=1, source_target_pairs={{0,2},{1,3},{2,0},{3,1},{4,6},{5,7},{6,4},{7,5},{8,10},{9,11},{10,... | collective-permute-start | bytes 7077896 | tf_op jit(solution)/shard_map/ppermute | solution.py:1046
  304.3 30.9 %collective-permute-start.47 = (bf16[832,768]{1,0:T(8,128)(2,1)S(1)}, bf16[832,768]{1,0:T(8,128)(2,1)S(1)}, u32[]{:S(2)}, u32[]{:S(2)}) collective-permute-start(bf16[832,768]{1,0:T(8,128)(2,1)S(1)} %get-tuple-element.370), channel_id=1, source_target_pairs={{0,4},{4,0},{8,12},{12,8},{16,20},{20,16},{24,28},{28,24},{1,5},{5... | collective-permute-start | bytes 3833864 | tf_op jit(solution)/shard_map/ppermute | solution.py:1049
  319.7 45.2 %collective-permute-start.53 = (bf16[384,768]{1,0:T(8,128)(2,1)}, bf16[384,768]{1,0:T(8,128)(2,1)}, u32[]{:S(2)}, u32[]{:S(2)}) collective-permute-start(bf16[384,768]{1,0:T(8,128)(2,1)} %get-tuple-element.389), channel_id=1, source_target_pairs={{0,4},{4,0},{8,12},{12,8},{16,20},{20,16},{24,28},{28,24},{1,5},{5... | collective-permute-start | bytes 1769480 | tf_op jit(solution)/shard_map/ppermute | solution.py:1049
  320.1 16.6 %collective-permute-start.49 = (bf16[288,768]{1,0:T(8,128)(2,1)S(1)}, bf16[288,768]{1,0:T(8,128)(2,1)}, u32[]{:S(2)}, u32[]{:S(2)}) collective-permute-start(bf16[288,768]{1,0:T(8,128)(2,1)S(1)} %get-tuple-element.373.refs_2_), channel_id=1, source_target_pairs={{0,1},{1,0},{2,3},{3,2},{4,5},{5,4},{6,7},{7,6},{8,9},{9,8},{10,11... | collective-permute-start | bytes 1327112 | tf_op jit(solution)/shard_map/ppermute | solution.py:1043
  363.1 33.6 %collective-permute-start.57 = (bf16[768,768]{1,0:T(8,128)(2,1)}, bf16[768,768]{1,0:T(8,128)(2,1)}, u32[]{:S(2)}, u32[]{:S(2)}) collective-permute-start(bf16[768,768]{1,0:T(8,128)(2,1)} %get-tuple-element.412), channel_id=1, source_target_pairs={{0,4},{4,0},{8,12},{12,8},{16,20},{20,16},{24,28},{28,24},{1,5},{5... | collective-permute-start | bytes 3538952 | tf_op jit(solution)/shard_map/ppermute | solution.py:1049
  366.2 32.2 %collective-permute-start.58 = (bf16[768,768]{1,0:T(8,128)(2,1)}, bf16[768,768]{1,0:T(8,128)(2,1)}, u32[]{:S(2)}, u32[]{:S(2)}) collective-permute-start(bf16[768,768]{1,0:T(8,128)(2,1)} %get-tuple-element.417), channel_id=1, source_target_pairs={{0,2},{1,3},{2,0},{3,1},{4,6},{5,7},{6,4},{7,5},{8,10},{9,11},{10,... | collective-permute-start | bytes 3538952 | tf_op jit(solution)/shard_map/ppermute | solution.py:1046
  367.6 29.1 %collective-permute-start.56 = (bf16[192,768]{1,0:T(8,128)(2,1)S(1)}, bf16[192,768]{1,0:T(8,128)(2,1)S(1)}, u32[]{:S(2)}, u32[]{:S(2)}) collective-permute-start(bf16[192,768]{1,0:T(8,128)(2,1)S(1)} %get-tuple-element.409), channel_id=1, source_target_pairs={{0,8},{4,12},{8,0},{12,4},{16,24},{20,28},{24,16},{28,20},{1,9},{5... | collective-permute-start | bytes 884744 | tf_op jit(solution)/shard_map/ppermute | solution.py:1049
  400.0 32.8 %collective-permute-start.60 = (bf16[384,768]{1,0:T(8,128)(2,1)S(1)}, bf16[384,768]{1,0:T(8,128)(2,1)S(1)}, u32[]{:S(2)}, u32[]{:S(2)}) collective-permute-start(bf16[384,768]{1,0:T(8,128)(2,1)S(1)} %get-tuple-element.422), channel_id=1, source_target_pairs={{0,4},{4,0},{8,12},{12,8},{16,20},{20,16},{24,28},{28,24},{1,5},{5... | collective-permute-start | bytes 1769480 | tf_op jit(solution)/shard_map/ppermute | solution.py:1049
  400.6 42.3 %collective-permute-start.62 = (bf16[384,768]{1,0:T(8,128)(2,1)S(1)}, bf16[384,768]{1,0:T(8,128)(2,1)S(1)}, u32[]{:S(2)}, u32[]{:S(2)}) collective-permute-start(bf16[384,768]{1,0:T(8,128)(2,1)S(1)} %get-tuple-element.427), channel_id=1, source_target_pairs={{0,8},{4,12},{8,0},{12,4},{16,24},{20,28},{24,16},{28,20},{1,9},{5... | collective-permute-start | bytes 1769480 | tf_op jit(solution)/shard_map/ppermute | solution.py:1049
  400.7 32.0 %collective-permute-start.59 = (bf16[96,768]{1,0:T(8,128)(2,1)S(1)}, bf16[96,768]{1,0:T(8,128)(2,1)S(1)}, u32[]{:S(2)}, u32[]{:S(2)}) collective-permute-start(bf16[96,768]{1,0:T(8,128)(2,1)S(1)} %get-tuple-element.420), channel_id=1, source_target_pairs={{0,16},{4,20},{8,24},{12,28},{16,0},{20,4},{24,8},{28,12},{1,17},{... | collective-permute-start | bytes 442376 | tf_op jit(solution)/shard_map/ppermute | solution.py:1049
  448.8 54.9 %collective-permute-start.72 = (bf16[832,768]{1,0:T(8,128)(2,1)}, bf16[832,768]{1,0:T(8,128)(2,1)}, u32[]{:S(2)}, u32[]{:S(2)}) collective-permute-start(bf16[832,768]{1,0:T(8,128)(2,1)} %all-reduce.2.cloned.1.call-done.refs_1_), channel_id=1, source_target_pairs={{0,4},{4,0},{8,12},{12,8},{16,20},{20,16},{24,28},{28,24},{1,5},{5... | collective-permute-start | bytes 3833864 | tf_op jit(solution)/shard_map/ppermute | solution.py:1049
  450.2 42.3 %collective-permute-start.54 = (bf16[576,768]{1,0:T(8,128)(2,1)}, bf16[576,768]{1,0:T(8,128)(2,1)}, u32[]{:S(2)}, u32[]{:S(2)}) collective-permute-start(bf16[576,768]{1,0:T(8,128)(2,1)} %copy-done.31), channel_id=1, source_target_pairs={{0,1},{1,0},{2,3},{3,2},{4,5},{5,4},{6,7},{7,6},{8,9},{9,8},{10,11... | collective-permute-start | bytes 2654216 | tf_op jit(solution)/shard_map/ppermute | solution.py:1043
  450.2 17.2 %collective-permute-start.66 = (bf16[192,768]{1,0:T(8,128)(2,1)}, bf16[192,768]{1,0:T(8,128)(2,1)S(1)}, u32[]{:S(2)}, u32[]{:S(2)}) collective-permute-start(bf16[192,768]{1,0:T(8,128)(2,1)} %copy-done.32), channel_id=1, source_target_pairs={{0,16},{4,20},{8,24},{12,28},{16,0},{20,4},{24,8},{28,12},{1,17},{... | collective-permute-start | bytes 884744 | tf_op jit(solution)/shard_map/ppermute | solution.py:1049
  454.6 26.3 %collective-permute-start.68 = (bf16[96,768]{1,0:T(8,128)(2,1)}, bf16[96,768]{1,0:T(8,128)(2,1)}, u32[]{:S(2)}, u32[]{:S(2)}) collective-permute-start(bf16[96,768]{1,0:T(8,128)(2,1)} %get-tuple-element.438), channel_id=1, source_target_pairs={{0,16},{4,20},{8,24},{12,28},{16,0},{20,4},{24,8},{28,12},{1,17},{... | collective-permute-start | bytes 442376 | tf_op jit(solution)/shard_map/ppermute | solution.py:1049
  467.5 21.5 %collective-permute-start.70 = (bf16[192,768]{1,0:T(8,128)(2,1)S(1)}, bf16[192,768]{1,0:T(8,128)(2,1)S(1)}, u32[]{:S(2)}, u32[]{:S(2)}) collective-permute-start(bf16[192,768]{1,0:T(8,128)(2,1)S(1)} %add.82.refs_1_), channel_id=1, source_target_pairs={{0,16},{4,20},{8,24},{12,28},{16,0},{20,4},{24,8},{28,12},{1,17},{... | collective-permute-start | bytes 884744 | tf_op jit(solution)/shard_map/ppermute | solution.py:1049
  478.3 26.9 %collective-permute-start.73 = (bf16[384,768]{1,0:T(8,128)(2,1)S(1)}, bf16[384,768]{1,0:T(8,128)(2,1)}, u32[]{:S(2)}, u32[]{:S(2)}) collective-permute-start(bf16[384,768]{1,0:T(8,128)(2,1)S(1)} %join.21.refs_1_), channel_id=1, source_target_pairs={{0,4},{4,0},{8,12},{12,8},{16,20},{20,16},{24,28},{28,24},{1,5},{5... | collective-permute-start | bytes 1769480 | tf_op jit(solution)/shard_map/ppermute | solution.py:1049
  488.7 18.7 %collective-permute-start.74 = (f32[40,768]{1,0:T(8,128)S(1)}, f32[40,768]{1,0:T(8,128)S(1)}, u32[]{:S(2)}, u32[]{:S(2)}) collective-permute-start(f32[40,768]{1,0:T(8,128)S(1)} %add.84.refs_0_), channel_id=1, source_target_pairs={{0,16},{4,20},{8,24},{12,28},{16,0},{20,4},{24,8},{28,12},{1,17},{... | collective-permute-start | bytes 368648 | tf_op jit(solution)/shard_map/ppermute | solution.py:1049
  492.5 22.3 %collective-permute-start.75 = (bf16[384,768]{1,0:T(8,128)(2,1)}, bf16[384,768]{1,0:T(8,128)(2,1)}, u32[]{:S(2)}, u32[]{:S(2)}) collective-permute-start(bf16[384,768]{1,0:T(8,128)(2,1)} %join.22.refs_1_), channel_id=1, source_target_pairs={{0,8},{4,12},{8,0},{12,4},{16,24},{20,28},{24,16},{28,20},{1,9},{5... | collective-permute-start | bytes 1769480 | tf_op jit(solution)/shard_map/ppermute | solution.py:1049
  503.6 16.1 %collective-permute-start.76 = (bf16[192,768]{1,0:T(8,128)(2,1)S(1)}, bf16[192,768]{1,0:T(8,128)(2,1)}, u32[]{:S(2)}, u32[]{:S(2)}) collective-permute-start(bf16[192,768]{1,0:T(8,128)(2,1)S(1)} %join.23.refs_1_), channel_id=1, source_target_pairs={{0,8},{4,12},{8,0},{12,4},{16,24},{20,28},{24,16},{28,20},{1,9},{5... | collective-permute-start | bytes 884744 | tf_op jit(solution)/shard_map/ppermute | solution.py:1049
  517.2 29.3 %collective-permute-start.77 = (bf16[768,768]{1,0:T(8,128)(2,1)}, bf16[768,768]{1,0:T(8,128)(2,1)}, u32[]{:S(2)}, u32[]{:S(2)}) collective-permute-start(bf16[768,768]{1,0:T(8,128)(2,1)} %join.26.refs_1_), channel_id=1, source_target_pairs={{0,4},{4,0},{8,12},{12,8},{16,20},{20,16},{24,28},{28,24},{1,5},{5... | collective-permute-start | bytes 3538952 | tf_op jit(solution)/shard_map/ppermute | solution.py:1049
  520.8 34.6 %collective-permute-start.78 = (bf16[384,768]{1,0:T(8,128)(2,1)S(1)}, bf16[384,768]{1,0:T(8,128)(2,1)}, u32[]{:S(2)}, u32[]{:S(2)}) collective-permute-start(bf16[384,768]{1,0:T(8,128)(2,1)S(1)} %join.27.refs_1_), channel_id=1, source_target_pairs={{0,4},{4,0},{8,12},{12,8},{16,20},{20,16},{24,28},{28,24},{1,5},{5... | collective-permute-start | bytes 1769480 | tf_op jit(solution)/shard_map/ppermute | solution.py:1049
  (94 other events, 579.5 us)
Sparse Core Ops, SparseCore 0:
  20.7 41.4 all-gather.4
  68.6 52.3 all-gather.6
  367.7 75.0 all-reduce.1

commit v2 on v1

--- a/solution.py
+++ b/solution.py
@@ -18,7 +18,7 @@
 Q_ROWS = 512
 AHEAD = 3
 COST = 5000000
-TURNS = (1, 2, 3, 1, 3, 4, 2, 1, 3, 4, 0, 2, 1, 3, 4, 2, 3, 0, 1, 4, 2, 3, 2, 3)
+TURNS = (2, 3, 1, 4, 2, 3, 0, 1, 2, 4, 3, 1, 0, 2, 4, 3, 1, 2, 3, 4, 3, 2, 3)
 VMEM_LIMIT = 40 * 2**20
 
 bf16 = jnp.bfloat16
@@ -69,13 +69,18 @@
 
 
 class Fetched:
-    def __init__(self, ref, held, sem, line):
-        self.copy, self.held, self.line, self.due = pltpu.make_async_copy(ref, held, sem), held, line, True
+    def __init__(self, ref, part, held, sems, count, line):
+        self.where = (ref, part, held, sems, count)
+        self.held, self.line, self.due = held, line, True
         line.append(self)
+
+    def copy(self):
+        ref, part, held, sems, count = self.where
+        return pltpu.make_async_copy(ref.at[part[0]] if part else ref, held, sems.at[count])
 
     def begin(self):
         self.line.remove(self)
-        self.copy.start()
+        self.copy().start()
 
     def __getitem__(self, at):
         if self.due:
@@ -83,7 +88,7 @@
                 self.begin()
             if self.line:
                 self.line[0].begin()
-            self.copy.wait()
+            self.copy().wait()
             self.due = False
         value = self.held[at]
         return value.reshape(-1, value.shape[-1]) if value.ndim == 3 else value
@@ -92,7 +97,7 @@
 class Flushed:
     def __init__(self, ref, held, sems, pieces):
         self.ref, self.held, self.sems, self.pieces = ref, held, sems, pieces
-        self.copies = []
+        self.sent = []
 
     def __getitem__(self, at):
         return self.held[at]
@@ -100,12 +105,18 @@
     def __setitem__(self, at, value):
         self.held[at] = value
 
-    def flush(self, which=0):
+    def copy(self, which):
         first, last = self.pieces[which]
         rows = pl.ds(first, last - first)
-        copy = pltpu.make_async_copy(self.held.at[rows], self.ref.at[rows], self.sems.at[which])
-        copy.start()
-        self.copies.append(copy)
+        return pltpu.make_async_copy(self.held.at[rows], self.ref.at[rows], self.sems.at[which])
+
+    def flush(self, which=0):
+        self.copy(which).start()
+        self.sent.append(which)
+
+
+def stage(body):
+    pl.when(lax.axis_index("dp") >= 0)(body)
 
 
 def part_shape(shape, part=()):
@@ -140,8 +151,7 @@
         sems = extra[len(fetch) + len(pieces) :]
         line = []
         for count, at in enumerate(fetch):
-            ref = refs[at].at[parts[at][0]] if parts[at] else refs[at]
-            refs[at] = Fetched(ref, extra[count], sems[0].at[count], line)
+            refs[at] = Fetched(refs[at], parts[at], extra[count], sems[0], count, line)
         for _ in range(min(AHEAD, len(line))):
             line[0].begin()
         outs = []
@@ -156,8 +166,8 @@
         for at in fetch:
             refs[at][0:1]
         for out in outs:
-            for copy in out.copies:
-                copy.wait()
+            for which in out.sent:
+                out.copy(which).wait()
 
     given = pl.pallas_call(
         outer,
@@ -173,11 +183,11 @@
 
 
 def facts(meta, per):
-    core, micro = meta[1] % 2, meta[1] // 2
+    core, micro = meta[1] & 1, meta[1] >> 1
     ends, begin, last = [], 0, 0
     for at in range(per):
         length = meta[2 + micro * per + at]
-        begin = begin + jnp.where(length == LONGEST, last, 0)
+        begin = begin + (length == LONGEST).astype(i32) * last
         last = last + length
         ends.append(last)
     groups = [meta[2 + 2 * per + micro * per + at] for at in range(per)]
@@ -317,9 +327,9 @@
 
 def heads_into(refs, meta, per, line, heads, half, small):
     width = heads * HEAD
-    x_ref = refs.low
+
     bias = refs.units[line : line + 1]
-    made = nt(x_ref[...], refs.w_qkv[...])
+    made = nt(refs.low[...], refs.w_qkv[...])
     refs.q[...] = (made[:, :width] + bias[:, :width]).astype(bf16)
     refs.k[...] = made[:, width : 2 * width].astype(bf16)
     refs.v[...] = (made[:, 2 * width :] + bias[:, width : 2 * width]).astype(bf16)
@@ -395,6 +405,7 @@
 
     def body(refs):
         heads_into(refs, refs.meta, per, line, heads, half, small)
+
         for at, part in enumerate(chunks(rows)):
             made = nn(refs.a_own[part], refs.wo_own[...]) + nn(refs.a[part], refs.wo_par[...])
             getattr(refs, f"mine{at}")[...] = made.astype(bf16)
@@ -495,27 +506,40 @@
             pre_ref = refs.pre
         else:
             pre_ref = refs.scratch[0]
-        total = None
-        for at in chunks(rows):
-            pre = (refs.slope[at].astype(f32) * nt(refs.low[at], refs.w_down[...])).astype(bf16)
-            pre_ref[at] = pre
-            line = jnp.sum(pre.astype(f32), 0, keepdims=True)
-            total = line if total is None else total + line
-        if first:
-            pre_ref.flush()
-        refs.line[0:1] = total
-        refs.line[1:] = jnp.zeros((7, units), f32)
-        refs.line.flush()
-        refs.grads[:units] = tn(refs.hidden[...], refs.low[...]).astype(bf16)
-        refs.grads.flush(0)
-        refs.grads[units : units + model] = tn(refs.y[...], pre_ref[...]).astype(bf16)
-        if extra is not None:
-            refs.grads[units + model :] = refs.extra[...]
-        refs.grads.flush(1)
+
+        @stage
+        def _():
+            total = None
+            for at in chunks(rows):
+                pre = (refs.slope[at].astype(f32) * nt(refs.low[at], refs.w_down[...])).astype(bf16)
+                pre_ref[at] = pre
+                line = jnp.sum(pre.astype(f32), 0, keepdims=True)
+                total = line if total is None else total + line
+            if first:
+                pre_ref.flush()
+            refs.line[0:1] = total
+            refs.line[1:] = jnp.zeros((7, units), f32)
+            refs.line.flush()
+
+        @stage
+        def _():
+            refs.grads[:units] = tn(refs.hidden[...], refs.low[...]).astype(bf16)
+            refs.grads.flush(0)
+
+        @stage
+        def _():
+            refs.grads[units : units + model] = tn(refs.y[...], pre_ref[...]).astype(bf16)
+            if extra is not None:
+                refs.grads[units + model :] = refs.extra[...]
+            refs.grads.flush(1)
+
         if not first:
-            for at, part in enumerate(chunks(rows)):
-                made = nt(pre_ref[part], refs.w_up[...]) + nt(refs.pre_other[part], refs.w_up_other[...])
-                getattr(refs, f"mine{at}")[...] = made.astype(bf16)
+
+            @stage
+            def _():
+                for at, part in enumerate(chunks(rows)):
+                    made = nt(pre_ref[part], refs.w_up[...]) + nt(refs.pre_other[part], refs.w_up_other[...])
+                    getattr(refs, f"mine{at}")[...] = made.astype(bf16)
 
     scratch = () if first else (pltpu.VMEM((rows, units), bf16),)
     return run("ffn_back", body, operands, results, scratch=scratch)
@@ -566,11 +590,14 @@
         else:
             g_ref = refs.scratch[3]
         da_ref, dv_sum, dk_sum = refs.scratch[:3]
+
         low = refs.low[...]
         da_ref[...] = nt(low, refs.w_out[...]).astype(bf16)
         refs.grads[3 * width :] = tn(refs.a[...], low).astype(bf16)
         refs.grads.flush(1)
+
         same = small_same(refs.meta, per, small)
+
         ones = jnp.ones((8, HEAD), f32)
         for head in range(width // HEAD):
             cols = slice(head * HEAD, (head + 1) * HEAD)
@@ -622,6 +649,7 @@
             ):
                 g_ref[half : half + small, where] = made[:small].astype(bf16)
                 g_ref[2 * half + small :, where] = made[small:].astype(bf16)
+
         if first:
             g_ref.flush()
         g_all = g_ref[...]
@@ -630,15 +658,17 @@
         refs.line[0:1] = jnp.sum(g_all.astype(f32), 0, keepdims=True)
         refs.line[1:] = jnp.zeros((7, 3 * width), f32)
         refs.line.flush()
+
         if not first:
-            made = nn(g_all, refs.w_qkv[...]) + nn(refs.g_other[...], refs.w_other[...])
+            core = facts(refs.meta, per)[0]
+            place = row_places(refs.meta, per, half, small, 1)
+
+            made = nn(g_ref[...], refs.w_qkv[...]) + nn(refs.g_other[...], refs.w_other[...])
             if last:
                 own = rows // 2
                 made = made + jnp.concatenate([refs.g_norm[:own], jnp.zeros((own, model), f32)], 0)
                 high = made.astype(bf16)
                 rest = (made - high.astype(f32)).astype(bf16)
-                core = facts(refs.meta, per)[0]
-                place = row_places(refs.meta, per, half, small, 1)
                 at = lax.broadcasted_iota(i32, (own, rows), 0)
                 pick = (place == core * own + at).astype(bf16)
                 refs.own[...] = nn(pick, high) + nn(pick, rest)
@@ -994,6 +1024,41 @@
     return run("join", body, operands, dict(out=(NEAR, (4 * rows, width), parts[0].dtype))).out
 
 
+def store(layer, layers, parts, before):
+    count = len(parts)
+    model = parts[0][0].shape[1]
+    sources = []
+    for array, _, _ in parts:
+        if all(array is not other for other in sources):
+            sources.append(array)
+
+    def body(*refs):
+        outs = refs[len(sources) + (count if before else 0) :][:count]
+        held, sems = refs[-1 - count : -1], refs[-1]
+        for at, (array, first, rows) in enumerate(parts):
+            source = [ref for ref, given in zip(refs, sources) if given is array][0]
+            held[at][...] = source[first : first + rows].astype(f32)
+            pltpu.make_async_copy(held[at], outs[at].at[layer], sems.at[at]).start()
+        for at in range(count):
+            pltpu.make_async_copy(held[at], outs[at].at[layer], sems.at[at]).wait()
+
+    given = [pltpu.with_memory_space_constraint(value, pltpu.VMEM) for value in sources]
+    if before:
+        given += [pltpu.with_memory_space_constraint(value, pltpu.HBM) for value in before]
+    return pl.pallas_call(
+        body,
+        out_shape=tuple(pltpu.HBM((layers, rows, model), f32) for _, _, rows in parts),
+        in_specs=[VMEM] * len(sources) + [HBM] * (count if before else 0),
+        out_specs=(HBM,) * count,
+        scratch_shapes=[pltpu.VMEM((rows, model), f32) for _, _, rows in parts]
+        + [pltpu.SemaphoreType.DMA((count,))],
+        input_output_aliases={len(sources) + at: at for at in range(count)} if before else {},
+        compiler_params=pltpu.CompilerParams(vmem_limit_bytes=VMEM_LIMIT),
+        cost_estimate=pl.CostEstimate(flops=COST, transcendentals=0, bytes_accessed=0),
+        name="store",
+    )(*given)
+
+
 def add(*parts):
     def body(refs):
         total = sum(getattr(refs, f"part{at}")[...].astype(f32) for at in range(len(parts)))
@@ -1088,21 +1153,17 @@
     def after(value, first):
         return lax.optimization_barrier((value, first))[0]
 
-    strip = strips_of(meta, [(w_up, 0)])
+    strip = strips_of(meta, [(w_up, 0), (w_down, 0)])
     strip_par = to_x(strip)
+    turned = turn(after(meta, strip), per, small, passages_in, x_other)
     vecs, lines, first_carried = gather_small(
-        after(meta, strip), per, b_out, b_down, ln_gain, ln_shift, b_up, b_qv, queries
-    )
-    sent = slices(after(meta, lines), [(w_qkv, 0), (w_out, 0), (w_down, 0)], [], strip_rows)
-    strip_par = after(strip_par, sent[0])
+        after(meta, turned.low), per, b_out, b_down, ln_gain, ln_shift, b_up, b_qv, queries
+    )
+    lines_par = to_x(lines)
+    sent = slices(after(meta, lines), [(w_qkv, 0), (w_out, 0)], [], strip_rows)
     w_par = [SimpleNamespace() for _ in range(layers)]
-    (w_par[0].up,) = gathered(strip_par)
-    w_par[0].qkv, w_par[0].out = (to_x(after(value, strip_par)) for value in sent[:2])
-    lines_par = to_x(after(lines, strip_par))
-    turned = turn(after(meta, sent[0]), per, small, passages_in, x_other)
-    strips_par = [
-        to_x(strips_of(after(meta, turned.low), [(w_up, layer), (w_down, layer)])) for layer in range(1, layers)
-    ]
+    w_par[0].up, w_par[0].down = gathered(after(strip_par, sent[0]))
+    w_par[0].qkv, w_par[0].out = (to_x(after(value, lines_par)) for value in sent)
 
     def spread():
         value = first_carried
@@ -1137,11 +1198,8 @@
             here(meta), per, small, 2 * layer + 1, x_all, par.qkv, lines_par, att_own.a, w_out, layer, par.out
         )
         note(att_par.lse)
-        if layer == 0:
-            strips_par = [here(strip) for strip in strips_par]
-            w_par[0].down = (FAR, to_x(after(sent[2], strips_par[0])))
-            for at in range(1, layers):
-                w_par[at].up, w_par[at].down = gathered(strips_par[at - 1])
+        if layer + 1 < layers:
+            strip_par = to_x(strips_of(here(meta), [(w_up, layer + 1), (w_down, layer + 1)]))
         norm = SimpleNamespace(
             mine=parts_of(att_par), came=to_pair(parts_of(att_par)), base=base, vecs=vecs, line=2 * layer
         )
@@ -1152,6 +1210,7 @@
             spread_on()
         if layer + 1 < layers:
             at = layer + 1
+            w_par[at].up, w_par[at].down = gathered(here(strip_par))
             pieces = slices(here(meta), [(w_qkv, at), (w_out, at)], [], strip_rows)
             w_par[at].qkv, w_par[at].out = (to_x(value) for value in pieces)
         ffn_par = ffn_second(
@@ -1224,6 +1283,8 @@
         value = note(add(here(value), other))
         value = lax.psum(value, "dp", axis_index_groups=[list(range(side, n_dp, 2)) for side in range(2)])
         yield
+        value = note(here(value))
+        yield
         value = here(value)
         other = to_dp(value, 1)
         yield
@@ -1240,7 +1301,7 @@
             note(value)
             other = to_dp(sent, bit)
         yield
-        yield value + other
+        yield note(add(here(value), other))
 
     queried = query_sums()
     next(queried)
@@ -1278,6 +1339,7 @@
         if last:
             next(queried)
         else:
+            advance(0)
             advance(1)
         running.append((total_early if last else total)(got_par.grads))
         advance(-1)
@@ -1294,7 +1356,7 @@
         if last:
             next(queried)
         else:
-            advance(0)
+            advance(1)
         got_par = attend_back(
             here(meta),
             per,
@@ -1311,6 +1373,7 @@
         if not last:
             advance(2)
             advance(1)
+            advance(0)
         running.append(total(got_par.grads))
         advance(-1)
         if last:
@@ -1328,8 +1391,8 @@
             exchanged = SimpleNamespace(mine=parts_of(got_own), came=to_pair(parts_of(got_own)))
             grads = parts_in(exchanged) | dict(base=(FAR, got_par.g))
         if last:
+            query_grad = [value for value in queried if value is not None][0].reshape(q_group, q_piece, dim)
             advance(0)
-            query_grad = [value for value in queried if value is not None][0].reshape(q_group, q_piece, dim)
     input_grad = got_own.own + to_pair(got_own.away).astype(f32)
 
     count = 2 * layers * 8
@@ -1355,22 +1418,17 @@
         for got in running[which]:
             finals[which] = got
     flat = finals.pop()
-    lists = [[], [], [], []]
-    for layer in range(layers):
-        summed = finals[2 * (layers - 1 - layer)]
-        lists[3].append(summed[:ff])
-        lists[2].append(summed[ff : ff + model])
+    made = None
+    for layer in reversed(range(layers)):
+        ffn_sums, att_sums = finals[2 * (layers - 1 - layer) : 2 * (layers - layer)]
         if layer == layers - 1:
-            g_wproj = summed[ff + model :].astype(f32).T
-        summed = finals[2 * (layers - 1 - layer) + 1]
-        lists[0].append(summed[: 3 * width])
-        lists[1].append(summed[3 * width :])
+            g_wproj = ffn_sums[ff + model :].astype(f32).T
+        parts = [(att_sums, 0, 3 * width), (att_sums, 3 * width, width), (ffn_sums, ff, model), (ffn_sums, 0, ff)]
+        made = store(layer, layers, parts, made)
+    g_wqkv, g_wout, g_wup, g_wdown = made
     norms = flat[:count].reshape(layers, 2, 8, model)
     units = flat[count : count + 2 * layers].reshape(layers, 2, model)
     g_bqv = jnp.stack([units[:, 1, :width], units[:, 1, 2 * width : 3 * width]], 1)
-    g_wqkv, g_wout, g_wup, g_wdown = (
-        jnp.stack([value.astype(f32) for value in values]) for values in lists
-    )
     g_wqkv = g_wqkv.reshape(layers, 3, width, model).transpose(0, 3, 1, 2)
     return (
         query_loss,

time: 582 us -> 551 us (0.947); the launches traced: 572 us -> 547 us
  other arithmetic: 11.9 us -> 4.34 us
  waiting for transfers between devices: 172 us -> 165 us
  Pallas kernels: 283 us -> 277 us
    ppermute x32, waiting for transfers between devices: 134 us -> 115 us  [to_dp(): return lax.ppermute(value, 'dp', [(at, at ^ bit) for at in range(n_dp)])]
    pallas_call x56 -> x57, Pallas kernels: 271 us -> 261 us  [run(): pl.pallas_call(outer, out_shape=tuple((spaces[kind != NEAR](shape, dtype)...]
    psum x1, waiting for transfers between devices: 0.02 us -> 9.03 us  [total_early(): lax.psum(value, 'dp', axis_index_groups=[list(range(side, n_dp, 2)) for s...]
    ppermute x16 -> x15, waiting for transfers between devices: 27.7 us -> 34 us  [to_x(): return lax.ppermute(value, 'mp', [(at, at ^ 2) for at in range(n_mp)])]
    pallas_call x0 -> x2, Pallas kernels: none -> 6.22 us  [store(): pl.pallas_call(body, out_shape=tuple((pltpu.HBM((layers, rows, model), f3...]
    unnamed x86 -> x73, local copies, waits for them, and re-layouts: 16.3 us -> 13.6 us
    ppermute x16 -> x15, starting transfers between devices: 18.9 us -> 17.1 us  [to_x(): return lax.ppermute(value, 'mp', [(at, at ^ 2) for at in range(n_mp)])]
  transfers between devices with their start and end apart: 82 -> 81, of which waited for: 39 -> 32; matrix products, arithmetic and copies ran while one was open for 2% -> 2% of each run, Pallas kernels for 45% -> 46%
where the time goes in v2:
time: 551 us; the launch traced here: 547 us
  Pallas kernels  277 us (50%)
  waiting for transfers between devices  165 us (30%)
  starting transfers between devices  66.7 us (12%)
  local copies, waits for them, and re-layouts  18 us (3%)
  between operations  15.2 us (3%)
    pallas_call x57, Pallas kernels, run(): pl.pallas_call(outer, out_shape=tuple((spaces[kind != NEAR](shape, dtype)...  261 us
    ppermute x32, waiting for transfers between devices, to_dp(): return lax.ppermute(value, 'dp', [(at, at ^ bit) for at in range(n_dp)])  115 us
    ppermute x32, starting transfers between devices, to_dp(): return lax.ppermute(value, 'dp', [(at, at ^ bit) for at in range(n_dp)])  41.5 us
    ppermute x15, waiting for transfers between devices, to_x(): return lax.ppermute(value, 'mp', [(at, at ^ 2) for at in range(n_mp)])  34 us
    ppermute x15, starting transfers between devices, to_x(): return lax.ppermute(value, 'mp', [(at, at ^ 2) for at in range(n_mp)])  17.1 us
    unnamed x73, local copies, waits for them, and re-layouts  13.6 us
  transfers between devices with their start and end apart: 81, of which 32 were waited for; matrix products, arithmetic and copies ran while one was open for 2% of the time, Pallas kernels for 46%

profile of v2, /device:TPU:0, one launch (start us, length us, event | category | flops | bytes accessed | tf_op | source)
XLA Modules:
  0.0 546.5 jit_solution(13739144232267595396)
XLA Ops:
  16.3 4.7 turn.1
  32.3 9.6 %attend.4 = (bf16[1152,192]{1,0:T(8,128)(2,1)}, bf16[1152,192]{1,0:T(8,128)(2,1)}, bf16[1152,192]{1,0:T(8,128)(2,1)}, bf16[1152,192]{1,0:T(8,128)(2,1)}, f32[8,1152]{1,0:T(8,128)}) custom-call(s32[34]{0:T(128)S(1)} %copy-done.13, bf16[1152,768]{1,0:T(8,128)(2,1)S(1)} %get-tuple-element.240.refs_1_, bf16[2,576,768]{2,1,0:T(8,128)(2,1)} %bitcast.41, ...), custom_call_target="tpu_custom_call" | custom-call | flops 5000000 | tf_op jit(solution)/shard_map/attend/pallas_call | solution.py:172
  42.0 13.7 %collective-permute-done.4.refs_6_.refs_13_ = bf16[192,768]{1,0:T(8,128)(2,1)S(1)} collective-permute-done((bf16[192,768]{1,0:T(8,128)(2,1)S(1)}, bf16[192,768]{1,0:T(8,128)(2,1)S(1)}, u32[]{:S(2)}, u32[]{:S(2)}) %collective-permute-start.4) | collective-permute-done | bytes 294944 | tf_op jit(solution)/shard_map/ppermute | solution.py:1111
  56.4 10.7 %attend.5 = (bf16[1152,192]{1,0:T(8,128)(2,1)}, bf16[1152,192]{1,0:T(8,128)(2,1)}, bf16[1152,192]{1,0:T(8,128)(2,1)}, bf16[1152,192]{1,0:T(8,128)(2,1)}, f32[8,1...) custom-call(s32[34]{0:T(128)S(1)} %copy-done.13, ...), custom_call_target="tpu_custom_call" | custom-call | flops 5000000 | tf_op jit(solution)/shard_map/attend/pallas_call | solution.py:172
  73.6 9.9 %ffn.4 = (bf16[1152,768]{1,0:T(8,128)(2,1)}, bf16[1152,768]{1,0:T(8,128)(2,1)}, f32[1152,1]{1,0:T(8,128)}, f32[1152,768]{1,0:T(8,128)}, bf16[1152,768]{1,0:T(8,128)(2,1)}, /*index=5*/bf16[1152,768]{1,0:T(8,128)(2,1)}) custom-call(s32[34]{0:T(128)S(1)} %copy-done.14, bf16[288,768]{1,0:T(8,128)(2,1)S(1)} %get-tuple-element.257.refs_1_, ...), custom_call_target="tpu_custom_call" | custom-call | flops 5000000 | tf_op jit(solution)/shard_map/ffn/pallas_call | solution.py:172
  88.0 9.6 %ffn.5 = (bf16[1152,768]{1,0:T(8,128)(2,1)}, bf16[1152,768]{1,0:T(8,128)(2,1)}, bf16[288,768]{1,0:T(8,128)(2,1)S(1)}, bf16[288,768]{1,0:T(8,128)(2,1)S(1)}, bf16...) custom-call(s32[34]{0:T(128)S(1)} %copy-done.15, bf16[1152,768]{1,0:T(8,128)(2,1)} %get-tuple-element.264.refs_1_.refs_16_.refs_5_, ...), custom_call_target="tpu_custom_call" | custom-call | flops 5000000 | tf_op jit(solution)/shard_map/ffn/pallas_call | solution.py:172
  100.5 4.8 collective-permute-done.11.refs_2_
  108.9 12.5 %attend.6 = (bf16[1152,768]{1,0:T(8,128)(2,1)}, bf16[1152,768]{1,0:T(8,128)(2,1)}, f32[1152,1]{1,0:T(8,128)}, f32[1152,768]{1,0:T(8,128)}, bf16[1152,192]{1,0:T(...) custom-call(s32[34]{0:T(128)S(1)} %copy-done.15, ...), custom_call_target="tpu_custom_call" | custom-call | flops 5000000 | tf_op jit(solution)/shard_map/attend/pallas_call | solution.py:172
  121.4 10.5 %attend.7 = (bf16[1152,192]{1,0:T(8,128)(2,1)}, bf16[1152,192]{1,0:T(8,128)(2,1)}, bf16[1152,192]{1,0:T(8,128)(2,1)}, bf16[1152,192]{1,0:T(8,128)(2,1)}, f32[8,1...) custom-call(s32[34]{0:T(128)S(1)} %copy-done.15, ...), custom_call_target="tpu_custom_call" | custom-call | flops 5000000 | tf_op jit(solution)/shard_map/attend/pallas_call | solution.py:172
  138.5 10.4 %ffn.6 = (bf16[1152,768]{1,0:T(8,128)(2,1)}, bf16[1152,768]{1,0:T(8,128)(2,1)}, f32[1152,1]{1,0:T(8,128)}, f32[1152,768]{1,0:T(8,128)}, bf16[1152,768]{1,0:T(8,128)(2,1)}, /*index=5*/bf16[1152,768]{1,0:T(8,128)(2,1)}) custom-call(s32[34]{0:T(128)S(1)} %copy-done.15, bf16[288,768]{1,0:T(8,128)(2,1)S(1)} %get-tuple-element.283.refs_1_, ...), custom_call_target="tpu_custom_call" | custom-call | flops 5000000 | tf_op jit(solution)/shard_map/ffn/pallas_call | solution.py:172
  150.6 9.6 %ffn.7 = (bf16[1152,768]{1,0:T(8,128)(2,1)}, bf16[1152,768]{1,0:T(8,128)(2,1)}, bf16[288,768]{1,0:T(8,128)(2,1)S(1)}, bf16[288,768]{1,0:T(8,128)(2,1)S(1)}, bf16...) custom-call(s32[34]{0:T(128)S(1)} %copy-done.15, bf16[1152,768]{1,0:T(8,128)(2,1)} %get-tuple-element.291.refs_1_.refs_8_.refs_5_, ...), custom_call_target="tpu_custom_call" | custom-call | flops 5000000 | tf_op jit(solution)/shard_map/ffn/pallas_call | solution.py:172
  164.0 7.2 %score.1 = (bf16[1152,768]{1,0:T(8,128)(2,1)}, bf16[1152,768]{1,0:T(8,128)(2,1)}, f32[1152,1]{1,0:T(8,128)}, bf16[512,128]{1,0:T(8,128)(2,1)S(1)}, f32[8,512]{1,0:T(8,128)S(1)}, /*index=5*/f32[8,128]{1,0:T(8,128)S(1)}) custom-call(s32[34]{0:T(128)S(1)} %copy-done.15, bf16[288,768]{1,0:T(8,128)(2,1)S(1)} %get-tuple-element.295.refs_1_, ...), custom_call_target="tpu_custom_call" | custom-call | flops 5000000 | tf_op jit(solution)/shard_map/score/pallas_call | solution.py:172
  186.6 6.7 %loss_back.1 = (f32[2,8,1]{2,1,0:T(8,128)S(1)}, f32[256,128]{1,0:T(8,128)S(1)}, bf16[128,768]{1,0:T(8,128)(2,1)S(1)}, f32[1152,768]{1,0:T(8,128)S(1)}) custom-call(s32[34]{0:T(128)S(1)} %copy-done.15, f32[8,128]{1,0:T(8,128)S(1)} %add.60.refs_1_, s32[1,128]{1,0:T(1,128)S(1)} %reshape.80.refs_2_, s32[2,8,1]{2,1,0:T(8,128)S(1)} %copy.45.refs_3_, ...), custom_call_target="tpu_custom_call" | custom-call | flops 5000000 | tf_op jit(solution)/shard_map/loss_back/pallas_call | solution.py:172
  194.9 12.1 %ffn_back.4 = (bf16[1664,768]{1,0:T(8,128)(2,1)}, f32[8,768]{1,0:T(8,128)}, f32[1152,768]{1,0:T(8,128)}, bf16[1152,768]{1,0:T(8,128)(2,1)}, f32[8,768]{1,0:T(8,128)}, /*index=5*/bf16[1152,768]{1,0:T(8,128)(2,1)}) custom-call(s32[34]{0:T(128)S(1)} %copy-done.15, f32[1152,768]{1,0:T(8,128)S(1)} %get-tuple-element.306.refs_1_, ...), custom_call_target="tpu_custom_call" | custom-call | flops 5000000 | tf_op jit(solution)/shard_map/ffn_back/pallas_call | solution.py:172
  209.0 12.4 %ffn_back.5 = (bf16[1664,768]{1,0:T(8,128)(2,1)}, f32[8,768]{1,0:T(8,128)}, bf16[288,768]{1,0:T(8,128)(2,1)S(1)}, bf16[288,768]{1,0:T(8,128)(2,1)S(1)}, bf16[288...) custom-call(s32[34]{0:T(128)S(1)} %copy-done.15, bf16[1152,768]{1,0:T(8,128)(2,1)} %get-tuple-element.318.refs_1_, ...), custom_call_target="tpu_custom_call" | custom-call | flops 5000000 | tf_op jit(solution)/shard_map/ffn_back/pallas_call | solution.py:172
  225.3 22.2 %attend_back.4 = (bf16[768,768]{1,0:T(8,128)(2,1)}, f32[8,576]{1,0:T(8,128)}, f32[1152,768]{1,0:T(8,128)}, bf16[1152,768]{1,0:T(8,128)(2,1)}, f32[8,768]{1,0:T(8,128)}, /*index=5*/bf16[1152,576]{1,0:T(8,128)(2,1)}) custom-call(s32[34]{0:T(128)S(1)} %copy-done.15, bf16[288,768]{1,0:T(8,128)(2,1)S(1)} %get-tuple-element.326.refs_1_, ...), custom_call_target="tpu_custom_call" | custom-call | flops 5000000 | tf_op jit(solution)/shard_map/attend_back/pallas_call | solution.py:172
  249.1 21.3 %attend_back.5 = (bf16[768,768]{1,0:T(8,128)(2,1)}, f32[8,576]{1,0:T(8,128)}, bf16[288,768]{1,0:T(8,128)(2,1)S(1)}, bf16[288,768]{1,0:T(8,128)(2,1)S(1)}, bf16[2...) custom-call(s32[34]{0:T(128)S(1)} %copy-done.15, bf16[1152,768]{1,0:T(8,128)(2,1)} %get-tuple-element.341.refs_1_, ...), custom_call_target="tpu_custom_call" | custom-call | flops 5000000 | tf_op jit(solution)/shard_map/attend_back/pallas_call | solution.py:172
  276.9 13.6 %ffn_back.6 = (bf16[1536,768]{1,0:T(8,128)(2,1)}, f32[8,768]{1,0:T(8,128)}, f32[1152,768]{1,0:T(8,128)}, bf16[1152,768]{1,0:T(8,128)(2,1)}, f32[8,768]{1,0:T(8,128)}, /*index=5*/bf16[1152,768]{1,0:T(8,128)(2,1)}) custom-call(s32[34]{0:T(128)S(1)} %copy-done.15, bf16[288,768]{1,0:T(8,128)(2,1)S(1)} %get-tuple-element.355.refs_1_, ...), custom_call_target="tpu_custom_call" | custom-call | flops 5000000 | tf_op jit(solution)/shard_map/ffn_back/pallas_call | solution.py:172
  290.5 10.4 %collective-permute-done.46.refs_1_ = bf16[832,768]{1,0:T(8,128)(2,1)S(1)} collective-permute-done((bf16[832,768]{1,0:T(8,128)(2,1)S(1)}, bf16[832,768]{1,0:T(8,128)(2,1)S(1)}, u32[]{:S(2)}, u32[]{:S(2)}) %collective-permute-start.46) | collective-permute-done | bytes 1277984 | tf_op jit(solution)/shard_map/ppermute | solution.py:1114
  304.7 12.7 %ffn_back.7 = (bf16[1536,768]{1,0:T(8,128)(2,1)}, f32[8,768]{1,0:T(8,128)}, bf16[288,768]{1,0:T(8,128)(2,1)S(1)}, bf16[288,768]{1,0:T(8,128)(2,1)S(1)}, bf16[288...) custom-call(s32[34]{0:T(128)S(1)} %copy-done.15, bf16[1152,768]{1,0:T(8,128)(2,1)} %get-tuple-element.373.refs_1_, ...), custom_call_target="tpu_custom_call" | custom-call | flops 5000000 | tf_op jit(solution)/shard_map/ffn_back/pallas_call | solution.py:172
  321.4 22.2 %attend_back.6 = (bf16[768,768]{1,0:T(8,128)(2,1)}, f32[8,576]{1,0:T(8,128)}, f32[1152,768]{1,0:T(8,128)}, bf16[1152,768]{1,0:T(8,128)(2,1)}, f32[8,768]{1,0:T(8,128)}, /*index=5*/bf16[1152,576]{1,0:T(8,128)(2,1)}) custom-call(s32[34]{0:T(128)S(1)} %copy-done.15, bf16[288,768]{1,0:T(8,128)(2,1)S(1)} %get-tuple-element.381.refs_1_, ...), custom_call_target="tpu_custom_call" | custom-call | flops 5000000 | tf_op jit(solution)/shard_map/attend_back/pallas_call | solution.py:172
  343.6 11.3 %collective-permute-done.53.refs_2_ = bf16[1536,768]{1,0:T(8,128)(2,1)S(1)} collective-permute-done((bf16[1536,768]{1,0:T(8,128)(2,1)}, bf16[1536,768]{1,0:T(8,128)(2,1)S(1)}, u32[]{:S(2)}, u32[]{:S(2)}) %collective-permute-start.53) | collective-permute-done | bytes 2359328 | tf_op jit(solution)/shard_map/ppermute | solution.py:1111
  358.3 9.0 %all-reduce.2.cloned.1.call-done.refs_1_ = bf16[832,768]{1,0:T(8,128)(2,1)} async-done(((bf16[832,768]{1,0:T(8,128)(2,1)}), bf16[832,768]{1,0:T(8,128)(2,1)}) %all-reduce.2.cloned.1.call-update) | async-done | bytes 1277968 | tf_op jit(solution)/shard_map/psum | solution.py:1284
  368.8 26.6 %attend_back.7 = (bf16[768,768]{1,0:T(8,128)(2,1)}, f32[8,576]{1,0:T(8,128)}, f32[576,768]{1,0:T(8,128)S(1)}, bf16[576,768]{1,0:T(8,128)(2,1)}) custom-call(s32[34]{0:T(128)S(1)} %copy-done.15, bf16[1152,768]{1,0:T(8,128)(2,1)} %get-tuple-element.402.refs_1_, bf16[2,192,768]{2,1,0:T(8,128)(2,1)} %refs_2_.7, ...), custom_call_target="tpu_custom_call" | custom-call | flops 5000000 | tf_op jit(solution)/shard_map/attend_back/pallas_call | solution.py:172
  406.1 7.9 %collective-permute-done.58.refs_1_ = bf16[96,768]{1,0:T(8,128)(2,1)S(1)} collective-permute-done((bf16[96,768]{1,0:T(8,128)(2,1)S(1)}, bf16[96,768]{1,0:T(8,128)(2,1)S(1)}, u32[]{:S(2)}, u32[]{:S(2)}) %collective-permute-start.58) | collective-permute-done | bytes 147488 | tf_op jit(solution)/shard_map/ppermute | solution.py:1114
  422.2 18.0 %collective-permute-done.62.refs_2_ = bf16[96,768]{1,0:T(8,128)(2,1)S(1)} collective-permute-done((bf16[96,768]{1,0:T(8,128)(2,1)S(1)}, bf16[96,768]{1,0:T(8,128)(2,1)S(1)}, u32[]{:S(2)}, u32[]{:S(2)}) %collective-permute-start.62) | collective-permute-done | bytes 147488 | tf_op jit(solution)/shard_map/ppermute | solution.py:1114
  441.1 6.2 %collective-permute-done.64.refs_1_ = f32[40,768]{1,0:T(8,128)S(1)} collective-permute-done((f32[40,768]{1,0:T(8,128)S(1)}, f32[40,768]{1,0:T(8,128)S(1)}, u32[]{:S(2)}, u32[]{:S(2)}) %collective-permute-start.64) | collective-permute-done | bytes 122912 | tf_op jit(solution)/shard_map/ppermute | solution.py:1114
  451.2 10.5 %collective-permute-done.68.refs_2_ = bf16[192,768]{1,0:T(8,128)(2,1)S(1)} collective-permute-done((bf16[192,768]{1,0:T(8,128)(2,1)S(1)}, bf16[192,768]{1,0:T(8,128)(2,1)S(1)}, u32[]{:S(2)}, u32[]{:S(2)}) %collective-permute-start.68) | collective-permute-done | bytes 294944 | tf_op jit(solution)/shard_map/ppermute | solution.py:1114
  470.3 12.5 %collective-permute-done.69.refs_1_ = f32[40,768]{1,0:T(8,128)S(1)} collective-permute-done((f32[40,768]{1,0:T(8,128)S(1)}, f32[40,768]{1,0:T(8,128)S(1)}, u32[]{:S(2)}, u32[]{:S(2)}) %collective-permute-start.69) | collective-permute-done | bytes 122912 | tf_op jit(solution)/shard_map/ppermute | solution.py:1114
  499.4 4.8 collective-permute-done.75.refs_2_
  508.6 17.0 %collective-permute-done.76.refs_2_ = bf16[768,768]{1,0:T(8,128)(2,1)S(1)} collective-permute-done((bf16[768,768]{1,0:T(8,128)(2,1)S(1)}, bf16[768,768]{1,0:T(8,128)(2,1)S(1)}, u32[]{:S(2)}, u32[]{:S(2)}) %collective-permute-start.76) | collective-permute-done | bytes 1179680 | tf_op jit(solution)/shard_map/ppermute | solution.py:1114
  525.7 10.8 %collective-permute-done.77.refs_2_ = bf16[384,768]{1,0:T(8,128)(2,1)S(1)} collective-permute-done((bf16[384,768]{1,0:T(8,128)(2,1)S(1)}, bf16[384,768]{1,0:T(8,128)(2,1)S(1)}, u32[]{:S(2)}, u32[]{:S(2)}) %collective-permute-start.77) | collective-permute-done | bytes 589856 | tf_op jit(solution)/shard_map/ppermute | solution.py:1114
  (296 shorter events, 149.9 us)
Async XLA Ops:
  7.2 80.8 %all-gather.5.cloned.1.call-start = ((), (), s32[]{:S(2)}) async-start(), calls=%async_computation.1 | async-start | bytes 2654208 | tf_op jit(solution)/shard_map/all_gather | solution.py:1145
  24.7 125.9 %all-gather.7.cloned.1.call-start = ((), (), s32[]{:S(2)}) async-start(), calls=%async_computation.2 | async-start | bytes 2654208 | tf_op jit(solution)/shard_map/all_gather | solution.py:1145
  28.8 26.9 %collective-permute-start.3 = (bf16[576,768]{1,0:T(8,128)(2,1)S(1)}, bf16[576,768]{1,0:T(8,128)(2,1)}, u32[]{:S(2)}, u32[]{:S(2)}) collective-permute-start(bf16[576,768]{1,0:T(8,128)(2,1)S(1)} %get-tuple-element.250), channel_id=1, source_target_pairs={{0,2},{1,3},{2,0},{3,1},{4,6},{5,7},{6,4},{7,5},{8,10},{9,11},{10,... | collective-permute-start | bytes 2654216 | tf_op jit(solution)/shard_map/ppermute | solution.py:1111
  28.8 26.9 %collective-permute-start.4 = (bf16[192,768]{1,0:T(8,128)(2,1)S(1)}, bf16[192,768]{1,0:T(8,128)(2,1)S(1)}, u32[]{:S(2)}, u32[]{:S(2)}) collective-permute-start(bf16[192,768]{1,0:T(8,128)(2,1)S(1)} %get-tuple-element.253), channel_id=1, source_target_pairs={{0,2},{1,3},{2,0},{3,1},{4,6},{5,7},{6,4},{7,5},{8,10},{9,11},{10,... | collective-permute-start | bytes 884744 | tf_op jit(solution)/shard_map/ppermute | solution.py:1111
  83.5 283.8 %all-reduce.2.cloned.1.call-start = ((), (), s32[]{:S(2)}) async-start(), calls=%async_computation | async-start | bytes 2555904 | tf_op jit(solution)/shard_map/psum | solution.py:1284
  86.9 34.5 %collective-permute-start.16 = (bf16[576,768]{1,0:T(8,128)(2,1)}, bf16[576,768]{1,0:T(8,128)(2,1)}, u32[]{:S(2)}, u32[]{:S(2)}) collective-permute-start(bf16[576,768]{1,0:T(8,128)(2,1)} %get-tuple-element.277), channel_id=1, source_target_pairs={{0,2},{1,3},{2,0},{3,1},{4,6},{5,7},{6,4},{7,5},{8,10},{9,11},{10,... | collective-permute-start | bytes 2654216 | tf_op jit(solution)/shard_map/ppermute | solution.py:1111
  106.1 15.3 %collective-permute-start.17 = (bf16[192,768]{1,0:T(8,128)(2,1)}, bf16[192,768]{1,0:T(8,128)(2,1)}, u32[]{:S(2)}, u32[]{:S(2)}) collective-permute-start(bf16[192,768]{1,0:T(8,128)(2,1)} %get-tuple-element.279), channel_id=1, source_target_pairs={{0,2},{1,3},{2,0},{3,1},{4,6},{5,7},{6,4},{7,5},{8,10},{9,11},{10,... | collective-permute-start | bytes 884744 | tf_op jit(solution)/shard_map/ppermute | solution.py:1111
  207.0 63.5 %collective-permute-start.41 = (bf16[1664,768]{1,0:T(8,128)(2,1)}, bf16[1664,768]{1,0:T(8,128)(2,1)S(1)}, u32[]{:S(2)}, u32[]{:S(2)}) collective-permute-start(bf16[1664,768]{1,0:T(8,128)(2,1)} %get-tuple-element.352), channel_id=1, source_target_pairs={{0,2},{1,3},{2,0},{3,1},{4,6},{5,7},{6,4},{7,5},{8,10},{9,11},{10,... | collective-permute-start | bytes 7667720 | tf_op jit(solution)/shard_map/ppermute | solution.py:1111
  207.7 14.4 %collective-permute-start.34 = (f32[64,128]{1,0:T(8,128)S(1)}, f32[64,128]{1,0:T(8,128)S(1)}, u32[]{:S(2)}, u32[]{:S(2)}) collective-permute-start(f32[64,128]{1,0:T(8,128)S(1)} %get-tuple-element.323), channel_id=1, source_target_pairs={{0,16},{4,20},{8,24},{12,28},{16,0},{20,4},{24,8},{28,12},{1,17},{... | collective-permute-start | bytes 98312 | tf_op jit(solution)/shard_map/ppermute | solution.py:1114
  223.2 24.3 %collective-permute-start.39 = (f32[32,128]{1,0:T(8,128)S(1)}, f32[32,128]{1,0:T(8,128)S(1)}, u32[]{:S(2)}, u32[]{:S(2)}) collective-permute-start(f32[32,128]{1,0:T(8,128)S(1)} %get-tuple-element.338), channel_id=1, source_target_pairs={{0,8},{4,12},{8,0},{12,4},{16,24},{20,28},{24,16},{28,20},{1,9},{5... | collective-permute-start | bytes 49160 | tf_op jit(solution)/shard_map/ppermute | solution.py:1114
  247.6 22.9 %collective-permute-start.40 = (f32[16,128]{1,0:T(8,128)S(1)}, f32[16,128]{1,0:T(8,128)S(1)}, u32[]{:S(2)}, u32[]{:S(2)}) collective-permute-start(f32[16,128]{1,0:T(8,128)S(1)} %get-tuple-element.348), channel_id=1, source_target_pairs={{0,4},{4,0},{8,12},{12,8},{16,20},{20,16},{24,28},{28,24},{1,5},{5... | collective-permute-start | bytes 24584 | tf_op jit(solution)/shard_map/ppermute | solution.py:1114
  271.2 29.8 %collective-permute-start.46 = (bf16[832,768]{1,0:T(8,128)(2,1)S(1)}, bf16[832,768]{1,0:T(8,128)(2,1)S(1)}, u32[]{:S(2)}, u32[]{:S(2)}) collective-permute-start(bf16[832,768]{1,0:T(8,128)(2,1)S(1)} %get-tuple-element.366), channel_id=1, source_target_pairs={{0,4},{4,0},{8,12},{12,8},{16,20},{20,16},{24,28},{28,24},{1,5},{5... | collective-permute-start | bytes 3833864 | tf_op jit(solution)/shard_map/ppermute | solution.py:1114
  271.8 30.5 %collective-permute-start.47 = (bf16[768,768]{1,0:T(8,128)(2,1)S(1)}, bf16[768,768]{1,0:T(8,128)(2,1)S(1)}, u32[]{:S(2)}, u32[]{:S(2)}) collective-permute-start(bf16[768,768]{1,0:T(8,128)(2,1)S(1)} %copy-done.34), channel_id=1, source_target_pairs={{0,2},{1,3},{2,0},{3,1},{4,6},{5,7},{6,4},{7,5},{8,10},{9,11},{10,... | collective-permute-start | bytes 3538952 | tf_op jit(solution)/shard_map/ppermute | solution.py:1111
  302.6 52.3 %collective-permute-start.53 = (bf16[1536,768]{1,0:T(8,128)(2,1)}, bf16[1536,768]{1,0:T(8,128)(2,1)S(1)}, u32[]{:S(2)}, u32[]{:S(2)}) collective-permute-start(bf16[1536,768]{1,0:T(8,128)(2,1)} %get-tuple-element.395), channel_id=1, source_target_pairs={{0,2},{1,3},{2,0},{3,1},{4,6},{5,7},{6,4},{7,5},{8,10},{9,11},{10,... | collective-permute-start | bytes 7077896 | tf_op jit(solution)/shard_map/ppermute | solution.py:1111
  319.2 37.7 %collective-permute-start.54 = (bf16[192,768]{1,0:T(8,128)(2,1)S(1)}, bf16[192,768]{1,0:T(8,128)(2,1)S(1)}, u32[]{:S(2)}, u32[]{:S(2)}) collective-permute-start(bf16[192,768]{1,0:T(8,128)(2,1)S(1)} %get-tuple-element.398), channel_id=1, source_target_pairs={{0,8},{4,12},{8,0},{12,4},{16,24},{20,28},{24,16},{28,20},{1,9},{5... | collective-permute-start | bytes 884744 | tf_op jit(solution)/shard_map/ppermute | solution.py:1114
  356.4 40.3 %collective-permute-start.56 = (bf16[768,768]{1,0:T(8,128)(2,1)}, bf16[768,768]{1,0:T(8,128)(2,1)S(1)}, u32[]{:S(2)}, u32[]{:S(2)}) collective-permute-start(bf16[768,768]{1,0:T(8,128)(2,1)} %get-tuple-element.418), channel_id=1, source_target_pairs={{0,4},{4,0},{8,12},{12,8},{16,20},{20,16},{24,28},{28,24},{1,5},{5... | collective-permute-start | bytes 3538952 | tf_op jit(solution)/shard_map/ppermute | solution.py:1114
  367.4 31.4 %collective-permute-start.57 = (bf16[768,768]{1,0:T(8,128)(2,1)}, bf16[768,768]{1,0:T(8,128)(2,1)S(1)}, u32[]{:S(2)}, u32[]{:S(2)}) collective-permute-start(bf16[768,768]{1,0:T(8,128)(2,1)} %get-tuple-element.423), channel_id=1, source_target_pairs={{0,2},{1,3},{2,0},{3,1},{4,6},{5,7},{6,4},{7,5},{8,10},{9,11},{10,... | collective-permute-start | bytes 3538952 | tf_op jit(solution)/shard_map/ppermute | solution.py:1111
  397.2 18.2 %collective-permute-start.60 = (bf16[384,768]{1,0:T(8,128)(2,1)S(1)}, bf16[384,768]{1,0:T(8,128)(2,1)S(1)}, u32[]{:S(2)}, u32[]{:S(2)}) collective-permute-start(bf16[384,768]{1,0:T(8,128)(2,1)S(1)} %get-tuple-element.430), channel_id=1, source_target_pairs={{0,8},{4,12},{8,0},{12,4},{16,24},{20,28},{24,16},{28,20},{1,9},{5... | collective-permute-start | bytes 1769480 | tf_op jit(solution)/shard_map/ppermute | solution.py:1114
  399.0 16.6 %collective-permute-start.61 = (bf16[384,768]{1,0:T(8,128)(2,1)S(1)}, bf16[384,768]{1,0:T(8,128)(2,1)S(1)}, u32[]{:S(2)}, u32[]{:S(2)}) collective-permute-start(bf16[384,768]{1,0:T(8,128)(2,1)S(1)} %get-tuple-element.433), channel_id=1, source_target_pairs={{0,4},{4,0},{8,12},{12,8},{16,20},{20,16},{24,28},{28,24},{1,5},{5... | collective-permute-start | bytes 1769480 | tf_op jit(solution)/shard_map/ppermute | solution.py:1114
  415.8 35.2 %collective-permute-start.67 = (bf16[832,768]{1,0:T(8,128)(2,1)S(1)}, bf16[832,768]{1,0:T(8,128)(2,1)S(1)}, u32[]{:S(2)}, u32[]{:S(2)}) collective-permute-start(bf16[832,768]{1,0:T(8,128)(2,1)S(1)} %copy-done.5), channel_id=1, source_target_pairs={{0,4},{4,0},{8,12},{12,8},{16,20},{20,16},{24,28},{28,24},{1,5},{5... | collective-permute-start | bytes 3833864 | tf_op jit(solution)/shard_map/ppermute | solution.py:1114
  417.3 49.9 %collective-permute-start.55 = (bf16[576,768]{1,0:T(8,128)(2,1)}, bf16[576,768]{1,0:T(8,128)(2,1)}, u32[]{:S(2)}, u32[]{:S(2)}) collective-permute-start(bf16[576,768]{1,0:T(8,128)(2,1)} %get-tuple-element.409), channel_id=1, source_target_pairs={{0,1},{1,0},{2,3},{3,2},{4,5},{5,4},{6,7},{7,6},{8,9},{9,8},{10,11... | collective-permute-start | bytes 2654216 | tf_op jit(solution)/shard_map/ppermute | solution.py:1108
  417.3 23.1 %collective-permute-start.63 = (bf16[192,768]{1,0:T(8,128)(2,1)S(1)}, bf16[192,768]{1,0:T(8,128)(2,1)S(1)}, u32[]{:S(2)}, u32[]{:S(2)}) collective-permute-start(bf16[192,768]{1,0:T(8,128)(2,1)S(1)} %get-tuple-element.437), channel_id=1, source_target_pairs={{0,16},{4,20},{8,24},{12,28},{16,0},{20,4},{24,8},{28,12},{1,17},{... | collective-permute-start | bytes 884744 | tf_op jit(solution)/shard_map/ppermute | solution.py:1114
  419.3 20.9 %collective-permute-start.62 = (bf16[96,768]{1,0:T(8,128)(2,1)S(1)}, bf16[96,768]{1,0:T(8,128)(2,1)S(1)}, u32[]{:S(2)}, u32[]{:S(2)}) collective-permute-start(bf16[96,768]{1,0:T(8,128)(2,1)S(1)} %add.76.refs_1_), channel_id=1, source_target_pairs={{0,16},{4,20},{8,24},{12,28},{16,0},{20,4},{24,8},{28,12},{1,17},{... | collective-permute-start | bytes 442376 | tf_op jit(solution)/shard_map/ppermute | solution.py:1114
  420.2 28.4 %collective-permute-start.65 = (bf16[192,768]{1,0:T(8,128)(2,1)S(1)}, bf16[192,768]{1,0:T(8,128)(2,1)S(1)}, u32[]{:S(2)}, u32[]{:S(2)}) collective-permute-start(bf16[192,768]{1,0:T(8,128)(2,1)S(1)} %get-tuple-element.440), channel_id=1, source_target_pairs={{0,8},{4,12},{8,0},{12,4},{16,24},{20,28},{24,16},{28,20},{1,9},{5... | collective-permute-start | bytes 884744 | tf_op jit(solution)/shard_map/ppermute | solution.py:1114
  447.3 14.4 %collective-permute-start.68 = (bf16[192,768]{1,0:T(8,128)(2,1)S(1)}, bf16[192,768]{1,0:T(8,128)(2,1)S(1)}, u32[]{:S(2)}, u32[]{:S(2)}) collective-permute-start(bf16[192,768]{1,0:T(8,128)(2,1)S(1)} %add.78.refs_1_), channel_id=1, source_target_pairs={{0,16},{4,20},{8,24},{12,28},{16,0},{20,4},{24,8},{28,12},{1,17},{... | collective-permute-start | bytes 884744 | tf_op jit(solution)/shard_map/ppermute | solution.py:1114
  449.5 36.5 %collective-permute-start.71 = (bf16[384,768]{1,0:T(8,128)(2,1)S(1)}, bf16[384,768]{1,0:T(8,128)(2,1)}, u32[]{:S(2)}, u32[]{:S(2)}) collective-permute-start(bf16[384,768]{1,0:T(8,128)(2,1)S(1)} %join.21.refs_1_), channel_id=1, source_target_pairs={{0,4},{4,0},{8,12},{12,8},{16,20},{20,16},{24,28},{28,24},{1,5},{5... | collective-permute-start | bytes 1769480 | tf_op jit(solution)/shard_map/ppermute | solution.py:1114
  462.6 30.8 %collective-permute-start.72 = (bf16[384,768]{1,0:T(8,128)(2,1)}, bf16[384,768]{1,0:T(8,128)(2,1)}, u32[]{:S(2)}, u32[]{:S(2)}) collective-permute-start(bf16[384,768]{1,0:T(8,128)(2,1)} %join.23.refs_1_), channel_id=1, source_target_pairs={{0,8},{4,12},{8,0},{12,4},{16,24},{20,28},{24,16},{28,20},{1,9},{5... | collective-permute-start | bytes 1769480 | tf_op jit(solution)/shard_map/ppermute | solution.py:1114
  464.6 18.2 %collective-permute-start.69 = (f32[40,768]{1,0:T(8,128)S(1)}, f32[40,768]{1,0:T(8,128)S(1)}, u32[]{:S(2)}, u32[]{:S(2)}) collective-permute-start(f32[40,768]{1,0:T(8,128)S(1)} %add.79.refs_0_), channel_id=1, source_target_pairs={{0,8},{4,12},{8,0},{12,4},{16,24},{20,28},{24,16},{28,20},{1,9},{5... | collective-permute-start | bytes 368648 | tf_op jit(solution)/shard_map/ppermute | solution.py:1114
  466.6 16.4 %collective-permute-start.70 = (bf16[96,768]{1,0:T(8,128)(2,1)}, bf16[96,768]{1,0:T(8,128)(2,1)S(1)}, u32[]{:S(2)}, u32[]{:S(2)}) collective-permute-start(bf16[96,768]{1,0:T(8,128)(2,1)} %get-tuple-element.448), channel_id=1, source_target_pairs={{0,16},{4,20},{8,24},{12,28},{16,0},{20,4},{24,8},{28,12},{1,17},{... | collective-permute-start | bytes 442376 | tf_op jit(solution)/shard_map/ppermute | solution.py:1114
  482.8 15.9 %collective-permute-start.74 = (f32[40,768]{1,0:T(8,128)S(1)}, f32[40,768]{1,0:T(8,128)S(1)}, u32[]{:S(2)}, u32[]{:S(2)}) collective-permute-start(f32[40,768]{1,0:T(8,128)S(1)} %add.80.refs_0_), channel_id=1, source_target_pairs={{0,16},{4,20},{8,24},{12,28},{16,0},{20,4},{24,8},{28,12},{1,17},{... | collective-permute-start | bytes 368648 | tf_op jit(solution)/shard_map/ppermute | solution.py:1114
  496.5 29.0 %collective-permute-start.76 = (bf16[768,768]{1,0:T(8,128)(2,1)S(1)}, bf16[768,768]{1,0:T(8,128)(2,1)S(1)}, u32[]{:S(2)}, u32[]{:S(2)}) collective-permute-start(bf16[768,768]{1,0:T(8,128)(2,1)S(1)} %join.25.refs_1_), channel_id=1, source_target_pairs={{0,4},{4,0},{8,12},{12,8},{16,20},{20,16},{24,28},{28,24},{1,5},{5... | collective-permute-start | bytes 3538952 | tf_op jit(solution)/shard_map/ppermute | solution.py:1114
  504.2 32.3 %collective-permute-start.77 = (bf16[384,768]{1,0:T(8,128)(2,1)S(1)}, bf16[384,768]{1,0:T(8,128)(2,1)S(1)}, u32[]{:S(2)}, u32[]{:S(2)}) collective-permute-start(bf16[384,768]{1,0:T(8,128)(2,1)S(1)} %join.27.refs_1_), channel_id=1, source_target_pairs={{0,4},{4,0},{8,12},{12,8},{16,20},{20,16},{24,28},{28,24},{1,5},{5... | collective-permute-start | bytes 1769480 | tf_op jit(solution)/shard_map/ppermute | solution.py:1114
  (84 other events, 538.6 us)
Sparse Core Ops, SparseCore 0:
  24.8 52.2 all-gather.4
  83.6 54.7 all-gather.6
  303.9 63.4 all-reduce.1

commit v3 on v2

--- a/solution.py
+++ b/solution.py
@@ -18,7 +18,7 @@
 Q_ROWS = 512
 AHEAD = 3
 COST = 5000000
-TURNS = (2, 3, 1, 4, 2, 3, 0, 1, 2, 4, 3, 1, 0, 2, 4, 3, 1, 2, 3, 4, 3, 2, 3)
+TURNS = (2, 3, 1, 4, 2, 3, 0, 1, 2, 3, 1, 2, 3, 2, 0, 1, 4, 3, 4, 3, 4, 2, 3)
 VMEM_LIMIT = 40 * 2**20
 
 bf16 = jnp.bfloat16
@@ -1155,12 +1155,12 @@
 
     strip = strips_of(meta, [(w_up, 0), (w_down, 0)])
     strip_par = to_x(strip)
-    turned = turn(after(meta, strip), per, small, passages_in, x_other)
     vecs, lines, first_carried = gather_small(
-        after(meta, turned.low), per, b_out, b_down, ln_gain, ln_shift, b_up, b_qv, queries
+        after(meta, strip), per, b_out, b_down, ln_gain, ln_shift, b_up, b_qv, queries
     )
     lines_par = to_x(lines)
-    sent = slices(after(meta, lines), [(w_qkv, 0), (w_out, 0)], [], strip_rows)
+    turned = turn(after(meta, lines), per, small, passages_in, x_other)
+    sent = slices(after(meta, turned.low), [(w_qkv, 0), (w_out, 0)], [], strip_rows)
     w_par = [SimpleNamespace() for _ in range(layers)]
     w_par[0].up, w_par[0].down = gathered(after(strip_par, sent[0]))
     w_par[0].qkv, w_par[0].out = (to_x(after(value, lines_par)) for value in sent)

time: 551 us -> 538 us (0.976)
  waiting for transfers between devices: 165 us -> 146 us
    ppermute x32, waiting for transfers between devices: 115 us -> 95.8 us  [to_dp(): return lax.ppermute(value, 'dp', [(at, at ^ bit) for at in range(n_dp)])]
  transfers between devices with their start and end apart: 81 -> 81, of which waited for: 32 -> 30; matrix products, arithmetic and copies ran while one was open for 2% -> 2% of each run, Pallas kernels for 46% -> 47%
where the time goes in v3:
time: 538 us; the launch traced here: 534 us
  Pallas kernels  278 us (52%)
  waiting for transfers between devices  146 us (27%)
  starting transfers between devices  70.4 us (13%)
  local copies, waits for them, and re-layouts  19.2 us (4%)
  between operations  15.2 us (3%)
    pallas_call x57, Pallas kernels, run(): pl.pallas_call(outer, out_shape=tuple((spaces[kind != NEAR](shape, dtype)...  262 us
    ppermute x32, waiting for transfers between devices, to_dp(): return lax.ppermute(value, 'dp', [(at, at ^ bit) for at in range(n_dp)])  95.8 us
    ppermute x32, starting transfers between devices, to_dp(): return lax.ppermute(value, 'dp', [(at, at ^ bit) for at in range(n_dp)])  45 us
    ppermute x15, waiting for transfers between devices, to_x(): return lax.ppermute(value, 'mp', [(at, at ^ 2) for at in range(n_mp)])  33.9 us
    ppermute x15, starting transfers between devices, to_x(): return lax.ppermute(value, 'mp', [(at, at ^ 2) for at in range(n_mp)])  17.2 us
    unnamed x73, local copies, waits for them, and re-layouts  14.8 us
  transfers between devices with their start and end apart: 81, of which 30 were waited for; matrix products, arithmetic and copies ran while one was open for 2% of the time, Pallas kernels for 47%

profile of v3, /device:TPU:0, one launch (start us, length us, event | category | flops | bytes accessed | tf_op | source)
XLA Modules:
  0.0 533.7 jit_solution(11478844933677052241)
XLA Ops:
  17.8 4.7 turn.1
  25.0 3.8 collective-permute-done.2.refs_3_
  32.3 9.6 %attend.4 = (bf16[1152,192]{1,0:T(8,128)(2,1)}, bf16[1152,192]{1,0:T(8,128)(2,1)}, bf16[1152,192]{1,0:T(8,128)(2,1)}, bf16[1152,192]{1,0:T(8,128)(2,1)}, f32[8,1152]{1,0:T(8,128)}) custom-call(s32[34]{0:T(128)S(1)} %copy-done.15, bf16[1152,768]{1,0:T(8,128)(2,1)S(1)} %get-tuple-element.242.refs_1_, bf16[2,576,768]{2,1,0:T(8,128)(2,1)} %bitcast.41, ...), custom_call_target="tpu_custom_call" | custom-call | flops 5000000 | tf_op jit(solution)/shard_map/attend/pallas_call | solution.py:172
  42.0 13.7 %collective-permute-done.4.refs_6_.refs_13_ = bf16[192,768]{1,0:T(8,128)(2,1)S(1)} collective-permute-done((bf16[192,768]{1,0:T(8,128)(2,1)S(1)}, bf16[192,768]{1,0:T(8,128)(2,1)S(1)}, u32[]{:S(2)}, u32[]{:S(2)}) %collective-permute-start.4) | collective-permute-done | bytes 294944 | tf_op jit(solution)/shard_map/ppermute | solution.py:1111
  56.4 10.7 %attend.5 = (bf16[1152,192]{1,0:T(8,128)(2,1)}, bf16[1152,192]{1,0:T(8,128)(2,1)}, bf16[1152,192]{1,0:T(8,128)(2,1)}, bf16[1152,192]{1,0:T(8,128)(2,1)}, f32[8,1...) custom-call(s32[34]{0:T(128)S(1)} %copy-done.15, ...), custom_call_target="tpu_custom_call" | custom-call | flops 5000000 | tf_op jit(solution)/shard_map/attend/pallas_call | solution.py:172
  73.5 9.8 %ffn.4 = (bf16[1152,768]{1,0:T(8,128)(2,1)}, bf16[1152,768]{1,0:T(8,128)(2,1)}, f32[1152,1]{1,0:T(8,128)}, f32[1152,768]{1,0:T(8,128)}, bf16[1152,768]{1,0:T(8,128)(2,1)}, /*index=5*/bf16[1152,768]{1,0:T(8,128)(2,1)}) custom-call(s32[34]{0:T(128)S(1)} %copy-done.16, bf16[288,768]{1,0:T(8,128)(2,1)S(1)} %get-tuple-element.257.refs_1_, ...), custom_call_target="tpu_custom_call" | custom-call | flops 5000000 | tf_op jit(solution)/shard_map/ffn/pallas_call | solution.py:172
  87.9 9.6 %ffn.5 = (bf16[1152,768]{1,0:T(8,128)(2,1)}, bf16[1152,768]{1,0:T(8,128)(2,1)}, bf16[288,768]{1,0:T(8,128)(2,1)S(1)}, bf16[288,768]{1,0:T(8,128)(2,1)S(1)}, bf16...) custom-call(s32[34]{0:T(128)S(1)} %copy-done.17, bf16[1152,768]{1,0:T(8,128)(2,1)} %get-tuple-element.264.refs_1_.refs_16_.refs_5_, ...), custom_call_target="tpu_custom_call" | custom-call | flops 5000000 | tf_op jit(solution)/shard_map/ffn/pallas_call | solution.py:172
  100.5 4.7 collective-permute-done.11.refs_2_
  108.8 12.5 %attend.6 = (bf16[1152,768]{1,0:T(8,128)(2,1)}, bf16[1152,768]{1,0:T(8,128)(2,1)}, f32[1152,1]{1,0:T(8,128)}, f32[1152,768]{1,0:T(8,128)}, bf16[1152,192]{1,0:T(...) custom-call(s32[34]{0:T(128)S(1)} %copy-done.17, ...), custom_call_target="tpu_custom_call" | custom-call | flops 5000000 | tf_op jit(solution)/shard_map/attend/pallas_call | solution.py:172
  121.3 10.5 %attend.7 = (bf16[1152,192]{1,0:T(8,128)(2,1)}, bf16[1152,192]{1,0:T(8,128)(2,1)}, bf16[1152,192]{1,0:T(8,128)(2,1)}, bf16[1152,192]{1,0:T(8,128)(2,1)}, f32[8,1...) custom-call(s32[34]{0:T(128)S(1)} %copy-done.17, ...), custom_call_target="tpu_custom_call" | custom-call | flops 5000000 | tf_op jit(solution)/shard_map/attend/pallas_call | solution.py:172
  138.4 10.4 %ffn.6 = (bf16[1152,768]{1,0:T(8,128)(2,1)}, bf16[1152,768]{1,0:T(8,128)(2,1)}, f32[1152,1]{1,0:T(8,128)}, f32[1152,768]{1,0:T(8,128)}, bf16[1152,768]{1,0:T(8,128)(2,1)}, /*index=5*/bf16[1152,768]{1,0:T(8,128)(2,1)}) custom-call(s32[34]{0:T(128)S(1)} %copy-done.17, bf16[288,768]{1,0:T(8,128)(2,1)S(1)} %get-tuple-element.283.refs_1_, ...), custom_call_target="tpu_custom_call" | custom-call | flops 5000000 | tf_op jit(solution)/shard_map/ffn/pallas_call | solution.py:172
  150.4 9.6 %ffn.7 = (bf16[1152,768]{1,0:T(8,128)(2,1)}, bf16[1152,768]{1,0:T(8,128)(2,1)}, bf16[288,768]{1,0:T(8,128)(2,1)S(1)}, bf16[288,768]{1,0:T(8,128)(2,1)S(1)}, bf16...) custom-call(s32[34]{0:T(128)S(1)} %copy-done.17, bf16[1152,768]{1,0:T(8,128)(2,1)} %get-tuple-element.291.refs_1_.refs_8_.refs_5_, ...), custom_call_target="tpu_custom_call" | custom-call | flops 5000000 | tf_op jit(solution)/shard_map/ffn/pallas_call | solution.py:172
  163.9 7.2 %score.1 = (bf16[1152,768]{1,0:T(8,128)(2,1)}, bf16[1152,768]{1,0:T(8,128)(2,1)}, f32[1152,1]{1,0:T(8,128)}, bf16[512,128]{1,0:T(8,128)(2,1)S(1)}, f32[8,512]{1,0:T(8,128)S(1)}, /*index=5*/f32[8,128]{1,0:T(8,128)S(1)}) custom-call(s32[34]{0:T(128)S(1)} %copy-done.17, bf16[288,768]{1,0:T(8,128)(2,1)S(1)} %get-tuple-element.295.refs_1_, ...), custom_call_target="tpu_custom_call" | custom-call | flops 5000000 | tf_op jit(solution)/shard_map/score/pallas_call | solution.py:172
  186.5 6.7 %loss_back.1 = (f32[2,8,1]{2,1,0:T(8,128)S(1)}, f32[256,128]{1,0:T(8,128)S(1)}, bf16[128,768]{1,0:T(8,128)(2,1)S(1)}, f32[1152,768]{1,0:T(8,128)S(1)}) custom-call(s32[34]{0:T(128)S(1)} %copy-done.17, f32[8,128]{1,0:T(8,128)S(1)} %add.60.refs_1_, s32[1,128]{1,0:T(1,128)S(1)} %reshape.80.refs_2_, s32[2,8,1]{2,1,0:T(8,128)S(1)} %copy.45.refs_3_, ...), custom_call_target="tpu_custom_call" | custom-call | flops 5000000 | tf_op jit(solution)/shard_map/loss_back/pallas_call | solution.py:172
  194.8 12.1 %ffn_back.4 = (bf16[1664,768]{1,0:T(8,128)(2,1)}, f32[8,768]{1,0:T(8,128)}, f32[1152,768]{1,0:T(8,128)}, bf16[1152,768]{1,0:T(8,128)(2,1)}, f32[8,768]{1,0:T(8,128)}, /*index=5*/bf16[1152,768]{1,0:T(8,128)(2,1)}) custom-call(s32[34]{0:T(128)S(1)} %copy-done.17, f32[1152,768]{1,0:T(8,128)S(1)} %get-tuple-element.306.refs_1_, ...), custom_call_target="tpu_custom_call" | custom-call | flops 5000000 | tf_op jit(solution)/shard_map/ffn_back/pallas_call | solution.py:172
  208.9 12.4 %ffn_back.5 = (bf16[1664,768]{1,0:T(8,128)(2,1)}, f32[8,768]{1,0:T(8,128)}, bf16[288,768]{1,0:T(8,128)(2,1)S(1)}, bf16[288,768]{1,0:T(8,128)(2,1)S(1)}, bf16[288...) custom-call(s32[34]{0:T(128)S(1)} %copy-done.17, bf16[1152,768]{1,0:T(8,128)(2,1)} %get-tuple-element.318.refs_1_, ...), custom_call_target="tpu_custom_call" | custom-call | flops 5000000 | tf_op jit(solution)/shard_map/ffn_back/pallas_call | solution.py:172
  225.2 22.2 %attend_back.4 = (bf16[768,768]{1,0:T(8,128)(2,1)}, f32[8,576]{1,0:T(8,128)}, f32[1152,768]{1,0:T(8,128)}, bf16[1152,768]{1,0:T(8,128)(2,1)}, f32[8,768]{1,0:T(8,128)}, /*index=5*/bf16[1152,576]{1,0:T(8,128)(2,1)}) custom-call(s32[34]{0:T(128)S(1)} %copy-done.17, bf16[288,768]{1,0:T(8,128)(2,1)S(1)} %get-tuple-element.326.refs_1_, ...), custom_call_target="tpu_custom_call" | custom-call | flops 5000000 | tf_op jit(solution)/shard_map/attend_back/pallas_call | solution.py:172
  249.0 21.3 %attend_back.5 = (bf16[768,768]{1,0:T(8,128)(2,1)}, f32[8,576]{1,0:T(8,128)}, bf16[288,768]{1,0:T(8,128)(2,1)S(1)}, bf16[288,768]{1,0:T(8,128)(2,1)S(1)}, bf16[2...) custom-call(s32[34]{0:T(128)S(1)} %copy-done.17, bf16[1152,768]{1,0:T(8,128)(2,1)} %get-tuple-element.341.refs_1_, ...), custom_call_target="tpu_custom_call" | custom-call | flops 5000000 | tf_op jit(solution)/shard_map/attend_back/pallas_call | solution.py:172
  276.8 13.5 %ffn_back.6 = (bf16[1536,768]{1,0:T(8,128)(2,1)}, f32[8,768]{1,0:T(8,128)}, f32[1152,768]{1,0:T(8,128)}, bf16[1152,768]{1,0:T(8,128)(2,1)}, f32[8,768]{1,0:T(8,128)}, /*index=5*/bf16[1152,768]{1,0:T(8,128)(2,1)}) custom-call(s32[34]{0:T(128)S(1)} %copy-done.17, bf16[288,768]{1,0:T(8,128)(2,1)S(1)} %get-tuple-element.355.refs_1_, ...), custom_call_target="tpu_custom_call" | custom-call | flops 5000000 | tf_op jit(solution)/shard_map/ffn_back/pallas_call | solution.py:172
  290.4 10.4 %collective-permute-done.46.refs_1_ = bf16[832,768]{1,0:T(8,128)(2,1)S(1)} collective-permute-done((bf16[832,768]{1,0:T(8,128)(2,1)S(1)}, bf16[832,768]{1,0:T(8,128)(2,1)S(1)}, u32[]{:S(2)}, u32[]{:S(2)}) %collective-permute-start.46) | collective-permute-done | bytes 1277984 | tf_op jit(solution)/shard_map/ppermute | solution.py:1114
  304.7 12.7 %ffn_back.7 = (bf16[1536,768]{1,0:T(8,128)(2,1)}, f32[8,768]{1,0:T(8,128)}, bf16[288,768]{1,0:T(8,128)(2,1)S(1)}, bf16[288,768]{1,0:T(8,128)(2,1)S(1)}, bf16[288...) custom-call(s32[34]{0:T(128)S(1)} %copy-done.17, bf16[1152,768]{1,0:T(8,128)(2,1)} %get-tuple-element.373.refs_1_, ...), custom_call_target="tpu_custom_call" | custom-call | flops 5000000 | tf_op jit(solution)/shard_map/ffn_back/pallas_call | solution.py:172
  321.3 22.2 %attend_back.6 = (bf16[768,768]{1,0:T(8,128)(2,1)}, f32[8,576]{1,0:T(8,128)}, f32[1152,768]{1,0:T(8,128)}, bf16[1152,768]{1,0:T(8,128)(2,1)}, f32[8,768]{1,0:T(8,128)}, /*index=5*/bf16[1152,576]{1,0:T(8,128)(2,1)}) custom-call(s32[34]{0:T(128)S(1)} %copy-done.17, bf16[288,768]{1,0:T(8,128)(2,1)S(1)} %get-tuple-element.381.refs_1_, ...), custom_call_target="tpu_custom_call" | custom-call | flops 5000000 | tf_op jit(solution)/shard_map/attend_back/pallas_call | solution.py:172
  343.5 11.2 %collective-permute-done.53.refs_2_ = bf16[1536,768]{1,0:T(8,128)(2,1)S(1)} collective-permute-done((bf16[1536,768]{1,0:T(8,128)(2,1)}, bf16[1536,768]{1,0:T(8,128)(2,1)S(1)}, u32[]{:S(2)}, u32[]{:S(2)}) %collective-permute-start.53) | collective-permute-done | bytes 2359328 | tf_op jit(solution)/shard_map/ppermute | solution.py:1111
  358.3 8.9 %all-reduce.2.cloned.1.call-done.refs_1_ = bf16[832,768]{1,0:T(8,128)(2,1)} async-done(((bf16[832,768]{1,0:T(8,128)(2,1)}), bf16[832,768]{1,0:T(8,128)(2,1)}) %all-reduce.2.cloned.1.call-update) | async-done | bytes 1277968 | tf_op jit(solution)/shard_map/psum | solution.py:1284
  368.7 26.6 %attend_back.7 = (bf16[768,768]{1,0:T(8,128)(2,1)}, f32[8,576]{1,0:T(8,128)}, f32[576,768]{1,0:T(8,128)S(1)}, bf16[576,768]{1,0:T(8,128)(2,1)}) custom-call(s32[34]{0:T(128)S(1)} %copy-done.17, bf16[1152,768]{1,0:T(8,128)(2,1)} %get-tuple-element.402.refs_1_, bf16[2,192,768]{2,1,0:T(8,128)(2,1)} %refs_2_.7, ...), custom_call_target="tpu_custom_call" | custom-call | flops 5000000 | tf_op jit(solution)/shard_map/attend_back/pallas_call | solution.py:172
  401.8 3.6 pack.1
  406.1 7.9 %collective-permute-done.58.refs_1_ = bf16[96,768]{1,0:T(8,128)(2,1)S(1)} collective-permute-done((bf16[96,768]{1,0:T(8,128)(2,1)S(1)}, bf16[96,768]{1,0:T(8,128)(2,1)S(1)}, u32[]{:S(2)}, u32[]{:S(2)}) %collective-permute-start.58) | collective-permute-done | bytes 147488 | tf_op jit(solution)/shard_map/ppermute | solution.py:1114
  422.3 14.7 %collective-permute-done.62.refs_2_ = bf16[96,768]{1,0:T(8,128)(2,1)S(1)} collective-permute-done((bf16[96,768]{1,0:T(8,128)(2,1)S(1)}, bf16[96,768]{1,0:T(8,128)(2,1)S(1)}, u32[]{:S(2)}, u32[]{:S(2)}) %collective-permute-start.62) | collective-permute-done | bytes 147488 | tf_op jit(solution)/shard_map/ppermute | solution.py:1114
  439.9 10.9 %collective-permute-done.65.refs_2_ = bf16[192,768]{1,0:T(8,128)(2,1)S(1)} collective-permute-done((bf16[192,768]{1,0:T(8,128)(2,1)S(1)}, bf16[192,768]{1,0:T(8,128)(2,1)S(1)}, u32[]{:S(2)}, u32[]{:S(2)}) %collective-permute-start.65) | collective-permute-done | bytes 294944 | tf_op jit(solution)/shard_map/ppermute | solution.py:1114
  457.4 10.9 %collective-permute-done.67.refs_1_ = bf16[96,768]{1,0:T(8,128)(2,1)S(1)} collective-permute-done((bf16[96,768]{1,0:T(8,128)(2,1)S(1)}, bf16[96,768]{1,0:T(8,128)(2,1)S(1)}, u32[]{:S(2)}, u32[]{:S(2)}) %collective-permute-start.67) | collective-permute-done | bytes 147488 | tf_op jit(solution)/shard_map/ppermute | solution.py:1114
  499.1 16.3 %collective-permute-done.76.refs_2_ = bf16[768,768]{1,0:T(8,128)(2,1)} collective-permute-done((bf16[768,768]{1,0:T(8,128)(2,1)}, bf16[768,768]{1,0:T(8,128)(2,1)}, u32[]{:S(2)}, u32[]{:S(2)}) %collective-permute-start.76) | collective-permute-done | bytes 1179680 | tf_op jit(solution)/shard_map/ppermute | solution.py:1114
  517.1 6.6 %collective-permute-done.77.refs_2_ = bf16[384,768]{1,0:T(8,128)(2,1)S(1)} collective-permute-done((bf16[384,768]{1,0:T(8,128)(2,1)S(1)}, bf16[384,768]{1,0:T(8,128)(2,1)S(1)}, u32[]{:S(2)}, u32[]{:S(2)}) %collective-permute-start.77) | collective-permute-done | bytes 589856 | tf_op jit(solution)/shard_map/ppermute | solution.py:1114
  (296 shorter events, 150.6 us)
Async XLA Ops:
  7.2 80.8 %all-gather.5.cloned.1.call-start = ((), (), s32[]{:S(2)}) async-start(), calls=%async_computation.1 | async-start | bytes 2654208 | tf_op jit(solution)/shard_map/all_gather | solution.py:1145
  24.6 125.8 %all-gather.7.cloned.1.call-start = ((), (), s32[]{:S(2)}) async-start(), calls=%async_computation.2 | async-start | bytes 2654208 | tf_op jit(solution)/shard_map/all_gather | solution.py:1145
  28.8 26.9 %collective-permute-start.3 = (bf16[576,768]{1,0:T(8,128)(2,1)S(1)}, bf16[576,768]{1,0:T(8,128)(2,1)}, u32[]{:S(2)}, u32[]{:S(2)}) collective-permute-start(bf16[576,768]{1,0:T(8,128)(2,1)S(1)} %get-tuple-element.250), channel_id=1, source_target_pairs={{0,2},{1,3},{2,0},{3,1},{4,6},{5,7},{6,4},{7,5},{8,10},{9,11},{10,... | collective-permute-start | bytes 2654216 | tf_op jit(solution)/shard_map/ppermute | solution.py:1111
  28.8 26.9 %collective-permute-start.4 = (bf16[192,768]{1,0:T(8,128)(2,1)S(1)}, bf16[192,768]{1,0:T(8,128)(2,1)S(1)}, u32[]{:S(2)}, u32[]{:S(2)}) collective-permute-start(bf16[192,768]{1,0:T(8,128)(2,1)S(1)} %get-tuple-element.253), channel_id=1, source_target_pairs={{0,2},{1,3},{2,0},{3,1},{4,6},{5,7},{6,4},{7,5},{8,10},{9,11},{10,... | collective-permute-start | bytes 884744 | tf_op jit(solution)/shard_map/ppermute | solution.py:1111
  83.4 283.8 %all-reduce.2.cloned.1.call-start = ((), (), s32[]{:S(2)}) async-start(), calls=%async_computation | async-start | bytes 2555904 | tf_op jit(solution)/shard_map/psum | solution.py:1284
  86.8 34.5 %collective-permute-start.16 = (bf16[576,768]{1,0:T(8,128)(2,1)}, bf16[576,768]{1,0:T(8,128)(2,1)}, u32[]{:S(2)}, u32[]{:S(2)}) collective-permute-start(bf16[576,768]{1,0:T(8,128)(2,1)} %get-tuple-element.277), channel_id=1, source_target_pairs={{0,2},{1,3},{2,0},{3,1},{4,6},{5,7},{6,4},{7,5},{8,10},{9,11},{10,... | collective-permute-start | bytes 2654216 | tf_op jit(solution)/shard_map/ppermute | solution.py:1111
  106.0 15.3 %collective-permute-start.17 = (bf16[192,768]{1,0:T(8,128)(2,1)}, bf16[192,768]{1,0:T(8,128)(2,1)}, u32[]{:S(2)}, u32[]{:S(2)}) collective-permute-start(bf16[192,768]{1,0:T(8,128)(2,1)} %get-tuple-element.279), channel_id=1, source_target_pairs={{0,2},{1,3},{2,0},{3,1},{4,6},{5,7},{6,4},{7,5},{8,10},{9,11},{10,... | collective-permute-start | bytes 884744 | tf_op jit(solution)/shard_map/ppermute | solution.py:1111
  206.9 63.5 %collective-permute-start.41 = (bf16[1664,768]{1,0:T(8,128)(2,1)}, bf16[1664,768]{1,0:T(8,128)(2,1)S(1)}, u32[]{:S(2)}, u32[]{:S(2)}) collective-permute-start(bf16[1664,768]{1,0:T(8,128)(2,1)} %get-tuple-element.352), channel_id=1, source_target_pairs={{0,2},{1,3},{2,0},{3,1},{4,6},{5,7},{6,4},{7,5},{8,10},{9,11},{10,... | collective-permute-start | bytes 7667720 | tf_op jit(solution)/shard_map/ppermute | solution.py:1111
  207.6 14.4 %collective-permute-start.34 = (f32[64,128]{1,0:T(8,128)S(1)}, f32[64,128]{1,0:T(8,128)S(1)}, u32[]{:S(2)}, u32[]{:S(2)}) collective-permute-start(f32[64,128]{1,0:T(8,128)S(1)} %get-tuple-element.323), channel_id=1, source_target_pairs={{0,16},{4,20},{8,24},{12,28},{16,0},{20,4},{24,8},{28,12},{1,17},{... | collective-permute-start | bytes 98312 | tf_op jit(solution)/shard_map/ppermute | solution.py:1114
  223.2 24.3 %collective-permute-start.39 = (f32[32,128]{1,0:T(8,128)S(1)}, f32[32,128]{1,0:T(8,128)S(1)}, u32[]{:S(2)}, u32[]{:S(2)}) collective-permute-start(f32[32,128]{1,0:T(8,128)S(1)} %get-tuple-element.338), channel_id=1, source_target_pairs={{0,8},{4,12},{8,0},{12,4},{16,24},{20,28},{24,16},{28,20},{1,9},{5... | collective-permute-start | bytes 49160 | tf_op jit(solution)/shard_map/ppermute | solution.py:1114
  247.5 22.8 %collective-permute-start.40 = (f32[16,128]{1,0:T(8,128)S(1)}, f32[16,128]{1,0:T(8,128)S(1)}, u32[]{:S(2)}, u32[]{:S(2)}) collective-permute-start(f32[16,128]{1,0:T(8,128)S(1)} %get-tuple-element.348), channel_id=1, source_target_pairs={{0,4},{4,0},{8,12},{12,8},{16,20},{20,16},{24,28},{28,24},{1,5},{5... | collective-permute-start | bytes 24584 | tf_op jit(solution)/shard_map/ppermute | solution.py:1114
  271.0 29.7 %collective-permute-start.46 = (bf16[832,768]{1,0:T(8,128)(2,1)S(1)}, bf16[832,768]{1,0:T(8,128)(2,1)S(1)}, u32[]{:S(2)}, u32[]{:S(2)}) collective-permute-start(bf16[832,768]{1,0:T(8,128)(2,1)S(1)} %get-tuple-element.366), channel_id=1, source_target_pairs={{0,4},{4,0},{8,12},{12,8},{16,20},{20,16},{24,28},{28,24},{1,5},{5... | collective-permute-start | bytes 3833864 | tf_op jit(solution)/shard_map/ppermute | solution.py:1114
  271.7 30.5 %collective-permute-start.47 = (bf16[768,768]{1,0:T(8,128)(2,1)S(1)}, bf16[768,768]{1,0:T(8,128)(2,1)S(1)}, u32[]{:S(2)}, u32[]{:S(2)}) collective-permute-start(bf16[768,768]{1,0:T(8,128)(2,1)S(1)} %copy-done.34), channel_id=1, source_target_pairs={{0,2},{1,3},{2,0},{3,1},{4,6},{5,7},{6,4},{7,5},{8,10},{9,11},{10,... | collective-permute-start | bytes 3538952 | tf_op jit(solution)/shard_map/ppermute | solution.py:1111
  302.5 52.2 %collective-permute-start.53 = (bf16[1536,768]{1,0:T(8,128)(2,1)}, bf16[1536,768]{1,0:T(8,128)(2,1)S(1)}, u32[]{:S(2)}, u32[]{:S(2)}) collective-permute-start(bf16[1536,768]{1,0:T(8,128)(2,1)} %get-tuple-element.395), channel_id=1, source_target_pairs={{0,2},{1,3},{2,0},{3,1},{4,6},{5,7},{6,4},{7,5},{8,10},{9,11},{10,... | collective-permute-start | bytes 7077896 | tf_op jit(solution)/shard_map/ppermute | solution.py:1111
  303.7 14.4 %collective-permute-start.48 = (bf16[384,768]{1,0:T(8,128)(2,1)S(1)}, bf16[384,768]{1,0:T(8,128)(2,1)S(1)}, u32[]{:S(2)}, u32[]{:S(2)}) collective-permute-start(bf16[384,768]{1,0:T(8,128)(2,1)S(1)} %get-tuple-element.378), channel_id=1, source_target_pairs={{0,4},{4,0},{8,12},{12,8},{16,20},{20,16},{24,28},{28,24},{1,5},{5... | collective-permute-start | bytes 1769480 | tf_op jit(solution)/shard_map/ppermute | solution.py:1114
  319.2 37.7 %collective-permute-start.54 = (bf16[192,768]{1,0:T(8,128)(2,1)S(1)}, bf16[192,768]{1,0:T(8,128)(2,1)S(1)}, u32[]{:S(2)}, u32[]{:S(2)}) collective-permute-start(bf16[192,768]{1,0:T(8,128)(2,1)S(1)} %get-tuple-element.398), channel_id=1, source_target_pairs={{0,8},{4,12},{8,0},{12,4},{16,24},{20,28},{24,16},{28,20},{1,9},{5... | collective-permute-start | bytes 884744 | tf_op jit(solution)/shard_map/ppermute | solution.py:1114
  356.3 40.4 %collective-permute-start.56 = (bf16[768,768]{1,0:T(8,128)(2,1)}, bf16[768,768]{1,0:T(8,128)(2,1)S(1)}, u32[]{:S(2)}, u32[]{:S(2)}) collective-permute-start(bf16[768,768]{1,0:T(8,128)(2,1)} %get-tuple-element.418), channel_id=1, source_target_pairs={{0,4},{4,0},{8,12},{12,8},{16,20},{20,16},{24,28},{28,24},{1,5},{5... | collective-permute-start | bytes 3538952 | tf_op jit(solution)/shard_map/ppermute | solution.py:1114
  367.3 31.4 %collective-permute-start.57 = (bf16[768,768]{1,0:T(8,128)(2,1)}, bf16[768,768]{1,0:T(8,128)(2,1)S(1)}, u32[]{:S(2)}, u32[]{:S(2)}) collective-permute-start(bf16[768,768]{1,0:T(8,128)(2,1)} %get-tuple-element.423), channel_id=1, source_target_pairs={{0,2},{1,3},{2,0},{3,1},{4,6},{5,7},{6,4},{7,5},{8,10},{9,11},{10,... | collective-permute-start | bytes 3538952 | tf_op jit(solution)/shard_map/ppermute | solution.py:1111
  397.2 18.2 %collective-permute-start.60 = (bf16[384,768]{1,0:T(8,128)(2,1)S(1)}, bf16[384,768]{1,0:T(8,128)(2,1)S(1)}, u32[]{:S(2)}, u32[]{:S(2)}) collective-permute-start(bf16[384,768]{1,0:T(8,128)(2,1)S(1)} %get-tuple-element.430), channel_id=1, source_target_pairs={{0,8},{4,12},{8,0},{12,4},{16,24},{20,28},{24,16},{28,20},{1,9},{5... | collective-permute-start | bytes 1769480 | tf_op jit(solution)/shard_map/ppermute | solution.py:1114
  399.0 18.7 %collective-permute-start.61 = (bf16[384,768]{1,0:T(8,128)(2,1)S(1)}, bf16[384,768]{1,0:T(8,128)(2,1)S(1)}, u32[]{:S(2)}, u32[]{:S(2)}) collective-permute-start(bf16[384,768]{1,0:T(8,128)(2,1)S(1)} %get-tuple-element.433), channel_id=1, source_target_pairs={{0,4},{4,0},{8,12},{12,8},{16,20},{20,16},{24,28},{28,24},{1,5},{5... | collective-permute-start | bytes 1769480 | tf_op jit(solution)/shard_map/ppermute | solution.py:1114
  415.6 21.5 %collective-permute-start.63 = (bf16[192,768]{1,0:T(8,128)(2,1)S(1)}, bf16[192,768]{1,0:T(8,128)(2,1)S(1)}, u32[]{:S(2)}, u32[]{:S(2)}) collective-permute-start(bf16[192,768]{1,0:T(8,128)(2,1)S(1)} %get-tuple-element.437), channel_id=1, source_target_pairs={{0,16},{4,20},{8,24},{12,28},{16,0},{20,4},{24,8},{28,12},{1,17},{... | collective-permute-start | bytes 884744 | tf_op jit(solution)/shard_map/ppermute | solution.py:1114
  417.9 58.4 %collective-permute-start.69 = (bf16[832,768]{1,0:T(8,128)(2,1)S(1)}, bf16[832,768]{1,0:T(8,128)(2,1)}, u32[]{:S(2)}, u32[]{:S(2)}) collective-permute-start(bf16[832,768]{1,0:T(8,128)(2,1)S(1)} %copy-done.6), channel_id=1, source_target_pairs={{0,4},{4,0},{8,12},{12,8},{16,20},{20,16},{24,28},{28,24},{1,5},{5... | collective-permute-start | bytes 3833864 | tf_op jit(solution)/shard_map/ppermute | solution.py:1114
  419.4 17.6 %collective-permute-start.62 = (bf16[96,768]{1,0:T(8,128)(2,1)S(1)}, bf16[96,768]{1,0:T(8,128)(2,1)S(1)}, u32[]{:S(2)}, u32[]{:S(2)}) collective-permute-start(bf16[96,768]{1,0:T(8,128)(2,1)S(1)} %add.76.refs_1_), channel_id=1, source_target_pairs={{0,16},{4,20},{8,24},{12,28},{16,0},{20,4},{24,8},{28,12},{1,17},{... | collective-permute-start | bytes 442376 | tf_op jit(solution)/shard_map/ppermute | solution.py:1114
  420.3 19.5 %collective-permute-start.64 = (bf16[192,768]{1,0:T(8,128)(2,1)S(1)}, bf16[192,768]{1,0:T(8,128)(2,1)S(1)}, u32[]{:S(2)}, u32[]{:S(2)}) collective-permute-start(bf16[192,768]{1,0:T(8,128)(2,1)S(1)} %get-tuple-element.439), channel_id=1, source_target_pairs={{0,8},{4,12},{8,0},{12,4},{16,24},{20,28},{24,16},{28,20},{1,9},{5... | collective-permute-start | bytes 884744 | tf_op jit(solution)/shard_map/ppermute | solution.py:1114
  437.0 13.7 %collective-permute-start.65 = (bf16[192,768]{1,0:T(8,128)(2,1)S(1)}, bf16[192,768]{1,0:T(8,128)(2,1)S(1)}, u32[]{:S(2)}, u32[]{:S(2)}) collective-permute-start(bf16[192,768]{1,0:T(8,128)(2,1)S(1)} %join.20.refs_1_), channel_id=1, source_target_pairs={{0,8},{4,12},{8,0},{12,4},{16,24},{20,28},{24,16},{28,20},{1,9},{5... | collective-permute-start | bytes 884744 | tf_op jit(solution)/shard_map/ppermute | solution.py:1114
  437.2 15.6 %collective-permute-start.66 = (bf16[192,768]{1,0:T(8,128)(2,1)S(1)}, bf16[192,768]{1,0:T(8,128)(2,1)S(1)}, u32[]{:S(2)}, u32[]{:S(2)}) collective-permute-start(bf16[192,768]{1,0:T(8,128)(2,1)S(1)} %add.78.refs_1_), channel_id=1, source_target_pairs={{0,16},{4,20},{8,24},{12,28},{16,0},{20,4},{24,8},{28,12},{1,17},{... | collective-permute-start | bytes 884744 | tf_op jit(solution)/shard_map/ppermute | solution.py:1114
  439.8 43.8 %collective-permute-start.55 = (bf16[576,768]{1,0:T(8,128)(2,1)}, bf16[576,768]{1,0:T(8,128)(2,1)}, u32[]{:S(2)}, u32[]{:S(2)}) collective-permute-start(bf16[576,768]{1,0:T(8,128)(2,1)} %get-tuple-element.409), channel_id=1, source_target_pairs={{0,1},{1,0},{2,3},{3,2},{4,5},{5,4},{6,7},{7,6},{8,9},{9,8},{10,11... | collective-permute-start | bytes 2654216 | tf_op jit(solution)/shard_map/ppermute | solution.py:1108
  452.9 18.9 %collective-permute-start.68 = (bf16[384,768]{1,0:T(8,128)(2,1)S(1)}, bf16[384,768]{1,0:T(8,128)(2,1)S(1)}, u32[]{:S(2)}, u32[]{:S(2)}) collective-permute-start(bf16[384,768]{1,0:T(8,128)(2,1)S(1)} %join.22.refs_1_), channel_id=1, source_target_pairs={{0,8},{4,12},{8,0},{12,4},{16,24},{20,28},{24,16},{28,20},{1,9},{5... | collective-permute-start | bytes 1769480 | tf_op jit(solution)/shard_map/ppermute | solution.py:1114
  453.1 25.9 %collective-permute-start.70 = (bf16[384,768]{1,0:T(8,128)(2,1)S(1)}, bf16[384,768]{1,0:T(8,128)(2,1)}, u32[]{:S(2)}, u32[]{:S(2)}) collective-permute-start(bf16[384,768]{1,0:T(8,128)(2,1)S(1)} %join.21.refs_1_), channel_id=1, source_target_pairs={{0,4},{4,0},{8,12},{12,8},{16,20},{20,16},{24,28},{28,24},{1,5},{5... | collective-permute-start | bytes 1769480 | tf_op jit(solution)/shard_map/ppermute | solution.py:1114
  454.6 13.6 %collective-permute-start.67 = (bf16[96,768]{1,0:T(8,128)(2,1)S(1)}, bf16[96,768]{1,0:T(8,128)(2,1)S(1)}, u32[]{:S(2)}, u32[]{:S(2)}) collective-permute-start(bf16[96,768]{1,0:T(8,128)(2,1)S(1)} %get-tuple-element.444), channel_id=1, source_target_pairs={{0,16},{4,20},{8,24},{12,28},{16,0},{20,4},{24,8},{28,12},{1,17},{... | collective-permute-start | bytes 442376 | tf_op jit(solution)/shard_map/ppermute | solution.py:1114
  486.1 29.2 %collective-permute-start.76 = (bf16[768,768]{1,0:T(8,128)(2,1)}, bf16[768,768]{1,0:T(8,128)(2,1)}, u32[]{:S(2)}, u32[]{:S(2)}) collective-permute-start(bf16[768,768]{1,0:T(8,128)(2,1)} %join.23.refs_1_), channel_id=1, source_target_pairs={{0,4},{4,0},{8,12},{12,8},{16,20},{20,16},{24,28},{28,24},{1,5},{5... | collective-permute-start | bytes 3538952 | tf_op jit(solution)/shard_map/ppermute | solution.py:1114
  495.0 28.7 %collective-permute-start.77 = (bf16[384,768]{1,0:T(8,128)(2,1)S(1)}, bf16[384,768]{1,0:T(8,128)(2,1)S(1)}, u32[]{:S(2)}, u32[]{:S(2)}) collective-permute-start(bf16[384,768]{1,0:T(8,128)(2,1)S(1)} %join.27.refs_1_), channel_id=1, source_target_pairs={{0,4},{4,0},{8,12},{12,8},{16,20},{20,16},{24,28},{28,24},{1,5},{5... | collective-permute-start | bytes 1769480 | tf_op jit(solution)/shard_map/ppermute | solution.py:1114
  (84 other events, 534.3 us)
Sparse Core Ops, SparseCore 0:
  24.8 52.2 all-gather.4
  83.6 54.7 all-gather.6
  303.8 63.4 all-reduce.1
